TPU v7x, 32 devices: a whole 2x2x4 slice. The times are simulated.
32 devices in a mesh: tm: 16 (over z, y, x), panel: 2 (over core).
Axes of the slice: x: 2, y: 2, z: 4, core: 2. Of those that a mesh axis runs over, the one named last changes fastest.
Arguments:
- factor_inverse: float32 [16, 768, 768], P('tm', None, 'panel'), may hold values from -1 to 1, as said below
- coupling: float32 [16, 768, 768], P('tm', None, 'panel'), may hold values from -1 to 1
- sigma_after: float32 [768, 768], replicated, may hold values from -1 to 3, as said below
Outputs:
- marginal_cov: float32 [16, 768, 768], P('tm', None, 'panel')
- propagator: bfloat16 [16, 768, 768], P('tm', None, 'panel')
Inputs may be any that keep to these rules, and one draw needn't show every extreme that they name: `factor_inverse`: factor_inverse_t is lower triangular with a positive diagonal. sigma_after is symmetric.
All inputs are finite; a program needn't handle non-finite values.
Results may differ from a plain program's by a relative error of at most 0.007.
The roundings to bfloat16 on the way count: a program that leaves them out, or rounds other values in their place, can miss the bound.
Values may be sent and summed in bfloat16 or wider, within the bound.
No kernel may reach another device: no remote copies, remote signals or barrier semaphores. Data moves between devices by JAX's collectives and lax.ppermute only.
A program may use at most 64 MiB of HBM per device.

v0:
```python
import functools

import jax
import jax.numpy as jnp
from jax import lax
from jax.experimental import pallas as pl
from jax.experimental.pallas import tpu as pltpu
from jax.sharding import PartitionSpec as P

BF = jnp.bfloat16
F32 = jnp.float32
GROUP = 4
ANY = pl.BlockSpec(memory_space=pl.ANY)
VMEM = pl.BlockSpec(memory_space=pltpu.VMEM)
MIB = 1 << 20


def mm(a, b):
    return jnp.dot(a, b, preferred_element_type=F32)


def mm_t(a, b):
    return lax.dot_general(a, b, (((0,), (0,)), ((), ())), preferred_element_type=F32)


def whole(ref):
    return jnp.concatenate([ref[p] for p in range(ref.shape[0])], axis=1)


def put(ref, value):
    width = ref.shape[2]
    for p in range(ref.shape[0]):
        ref[p] = value[:, p * width : (p + 1) * width].astype(ref.dtype)


def where_am_i():
    t = lax.axis_index("tm")
    return t // GROUP, lax.rem(t, GROUP), lax.axis_index("panel")


def run(copies):
    for c in copies:
        c.start()
    for c in copies:
        c.wait()


def copy_all(pairs, sems):
    return [pltpu.make_async_copy(s, d, sems.at[i]) for i, (s, d) in enumerate(pairs)]


def panel_pairs(pieces, dst, q):
    n = len(pieces)
    return [(piece, dst.at[lax.rem(q + r, n)]) for r, piece in enumerate(pieces)]


def group_start(blocks, dst, sems, lo, q, order):
    own, first, second, diag = blocks
    n = len(own)

    def start(slot, r, p, mask, piece):
        @pl.when(jnp.bitwise_xor(lo, mask) == slot)
        def _():
            pltpu.make_async_copy(piece, dst.at[slot, p], sems.at[slot, p]).start()

    for slot in order:
        for r in range(n):
            p = lax.rem(q + r, n)
            even = 1 - lax.rem(p, 2)
            near, far = 1 + even, 2 - even
            for mask, piece in ((0, own[r]), (near, first[r]), (far, second[r]), (3, diag[r])):
                start(slot, r, p, mask, piece)


def group_wait(own, dst, sems, *slots):
    for slot in slots:
        for p in range(len(own)):
            pltpu.make_async_copy(own[p], dst.at[slot, p], sems.at[slot, p]).wait()


def split(refs, *counts):
    out, at = [], 0
    for c in counts:
        out.append(refs[at : at + c])
        at += c
    return out


def call(kernel, ins, in_specs, outs, scratch, flops):
    size = sum(a.size * a.dtype.itemsize for a in ins) + sum(
        o.size * o.dtype.itemsize for o in outs
    )
    return pl.pallas_call(
        kernel,
        in_specs=in_specs,
        out_specs=[VMEM] * len(outs),
        out_shape=outs,
        scratch_shapes=scratch,
        compiler_params=pltpu.CompilerParams(vmem_limit_bytes=28 * MIB),
        cost_estimate=pl.CostEstimate(flops=flops, bytes_accessed=size, transcendentals=0),
    )(*ins)


def base_kernel(n, *refs):
    factor, sigma, f_parts, c_parts, (base, base_bf), (f_all, c_all, sig, sems) = split(
        refs, 1, 1, n, n, 2, 4
    )
    factor, sigma = factor[0], sigma[0]
    hi, lo, q = where_am_i()
    width = factor.shape[1]
    run(copy_all(panel_pairs(f_parts, f_all, q), sems))
    own = factor[...]
    high = own.astype(BF)
    low = (own - high.astype(F32)).astype(BF)
    for p in range(n):
        part = f_all[p]
        base[p * width : (p + 1) * width, :] = mm_t(part, high) + mm_t(part, low)

    @pl.when(lax.axis_index("tm") == lax.axis_size("tm") - 1)
    def _():
        run(copy_all(panel_pairs(c_parts, c_all, q) + [(sigma, sig)], sems))
        s = sig[...]
        s_high = s.astype(BF)
        s_low = (s - s_high.astype(F32)).astype(BF)
        c_own = c_all[q]
        mid = mm(s_high, c_own) + mm(s_low, c_own)
        mid_high = mid.astype(BF)
        mid_low = (mid - mid_high.astype(F32)).astype(BF)
        c_full = whole(c_all)
        base[...] += mm_t(c_full, mid_high) + mm_t(c_full, mid_low)

    base_bf[...] = base[...].astype(BF)


def group_comp_kernel(n, *refs):
    *blocks, outs, (sems,) = split(refs, n, n, n, n, 4, 1)
    c, c01_ref, c23_ref, agg = outs
    hi, lo, q = where_am_i()
    group_start(blocks, c, sems, lo, q, (1, 0, 3, 2))
    group_wait(blocks[0], c, sems, 1, 0)
    c01 = mm(whole(c.at[1]), whole(c.at[0])).astype(BF)
    put(c01_ref, c01)
    group_wait(blocks[0], c, sems, 3, 2)
    c23 = mm(whole(c.at[3]), whole(c.at[2])).astype(BF)
    c23_ref[...] = c23
    put(agg, mm(c23, c01))


def tail_comp_kernel(n, c, c01, c23, agg, *outs):
    c_t, c01_t, mine, mine_t, agg_t = outs
    hi, lo, q = where_am_i()
    agg_t[...] = whole(agg).T
    c01_t[...] = whole(c01).T
    for k in range(GROUP - 1):
        c_t[k] = whole(c.at[k]).T

    @pl.when(lo == 0)
    def _():
        mine[...] = agg[...]
        mine_t[...] = agg_t[...]

    @pl.when(lo == 1)
    def _():
        value = mm(c23[...], whole(c.at[1])).astype(BF)
        put(mine, value)
        mine_t[...] = value.T

    @pl.when(lo == 2)
    def _():
        put(mine, c23[...])
        mine_t[...] = c23[...].T

    @pl.when(lo == 3)
    def _():
        mine[...] = c[3]
        mine_t[...] = whole(c.at[3]).T


def sandwich(cov, comp, comp_t):
    return mm(comp_t, mm(cov, comp).astype(BF))


def group_cov_kernel(n, *refs):
    ins, *blocks, outs, scratch = split(refs, 5, n, n, n, n, 3, 3)
    base, c, c_t, c01, c01_t = ins
    mine, agg, agg_bf = outs
    s, s23, sems = scratch
    hi, lo, q = where_am_i()
    group_start(blocks, s, sems, lo, q, (3, 2, 1, 0))
    group_wait(blocks[0], s, sems, 3)
    mid = mm(whole(s.at[3]), whole(c.at[2])).astype(BF)
    group_wait(blocks[0], s, sems, 2)
    s23[...] = (whole(s.at[2]).astype(F32) + mm(c_t[2], mid)).astype(BF)
    group_wait(blocks[0], s, sems, 1, 0)
    agg[...] = s[0, q].astype(F32)

    @pl.when(lo == 0)
    def _():
        agg[...] = base[...]

    agg[...] += sandwich(whole(s.at[1]), c[0, q], c_t[0])
    agg[...] += sandwich(s23[...], c01[q], c01_t[...])
    agg_bf[...] = agg[...].astype(BF)

    @pl.when(lo == 0)
    def _():
        mine[...] = agg[...]

    @pl.when(lo == 1)
    def _():
        mine[...] = base[...] + sandwich(s23[...], c[1, q], c_t[1])

    @pl.when(lo == 2)
    def _():
        mine[...] = base[...] + sandwich(whole(s.at[3]), c[2, q], c_t[2])

    @pl.when(lo == 3)
    def _():
        mine[...] = base[...]


def is_lower(bit):
    hi, lo, q = where_am_i()
    return lax.rem(hi // (1 << bit), 2) == 0


def panel_rows(q, r, n, w):
    return pl.ds(pl.multiple_of(lax.rem(q + r, n) * w, w), w)


def quarter_rows(place, nb):
    rows = nb // GROUP
    return pl.ds(pl.multiple_of(place * rows, rows), rows)


def times(pieces, right, lo, q, n):
    nb = right.shape[0]
    w = nb // n

    def product(some):
        return sum(mm(x[...], right[panel_rows(q, r, n, w), :]) for r, x in enumerate(some))

    if len(pieces) == n:
        return [(slice(None), product(pieces))]
    return [
        (quarter_rows(jnp.bitwise_xor(lo, k), nb), product(pieces[k * n : k * n + n]))
        for k in range(GROUP)
    ]


def own_columns(pieces, lo, q, n, nb):
    if len(pieces) == n:
        return [(slice(None), pieces[0])]
    return [(quarter_rows(jnp.bitwise_xor(lo, k), nb), pieces[k * n]) for k in range(GROUP)]


def place_whole(pieces, dst, lo, q, n):
    for r in range(n):
        p = lax.rem(q + r, n)
        if len(pieces) == n:
            dst[p] = pieces[r][...]
        else:
            for k in range(GROUP):
                rows = quarter_rows(jnp.bitwise_xor(lo, k), dst.shape[1])
                dst[p, rows, :] = pieces[k * n + r][...]


def share_comp_kernel(n, m, bit, *refs):
    (agg,), parts, (share,), (got, pair) = split(refs, 1, m, 1, 2)
    hi, lo, q = where_am_i()
    lower = is_lower(bit)

    @pl.when(lower)
    def _():
        for rows, value in times(parts, agg.at[q], lo, q, n):
            pair[rows, :] = value.astype(BF)

    @pl.when(jnp.logical_not(lower))
    def _():
        place_whole(parts, got, lo, q, n)
        pair[...] = mm(whole(agg), got[q]).astype(BF)

    share[...] = pair[quarter_rows(lo, pair.shape[0]), :]


def pair_comp_kernel(n, m, bit, *refs):
    (agg,), parts, (new_agg, new_agg_t, share), (got,) = split(refs, 1, m, 3, 1)
    hi, lo, q = where_am_i()
    lower = is_lower(bit)
    place_whole(parts, got, lo, q, n)

    @pl.when(lower)
    def _():
        put(new_agg, mm(whole(got), whole(agg)))

    @pl.when(jnp.logical_not(lower))
    def _():
        put(new_agg, mm(whole(agg), whole(got)))

    new_agg_t[...] = whole(new_agg).T
    share[...] = new_agg[q, quarter_rows(lo, new_agg.shape[1]), :]


def mine_comp_kernel(n, m, bit, *refs):
    (mine, mine_t), parts, (new_mine, new_mine_t) = split(refs, 2, m, 2)
    hi, lo, q = where_am_i()
    lower = is_lower(bit)

    @pl.when(lower)
    def _():
        for p in range(n):
            for rows, value in times(parts, mine.at[p], lo, q, n):
                new_mine[p, rows, :] = value.astype(BF)
        new_mine_t[...] = whole(new_mine).T

    @pl.when(jnp.logical_not(lower))
    def _():
        new_mine[...] = mine[...]
        new_mine_t[...] = mine_t[...]


def last_comp_kernel(n, m, bit, *refs):
    (mine,), parts, (out,) = split(refs, 1, m, 1)
    hi, lo, q = where_am_i()
    lower = is_lower(bit)

    @pl.when(lower)
    def _():
        for rows, value in times(parts, mine.at[q], lo, q, n):
            out[0, rows, :] = value.astype(BF)

    @pl.when(jnp.logical_not(lower))
    def _():
        out[0] = mine[q]


def level_cov_kernel(n, m, bit, to_last, *refs):
    ins, here, c_parts, parts, outs, scratch = split(refs, 6, n, m, m, 2 if to_last else 4, 3)
    cov, agg, mine, mine_t, agg_c, agg_t = ins
    new_cov, share = outs[:2]
    mid, total, got = scratch
    hi, lo, q = where_am_i()
    lower = is_lower(bit)
    nb, w = cov.shape
    mine_rows = quarter_rows(lo, nb)

    def middle(pieces, right):
        for rows, value in times(pieces, right, lo, q, n):
            mid[rows, :] = value.astype(BF)

    @pl.when(lower)
    def _():
        middle(parts, agg_c.at[q])
        if to_last:
            share[...] = (agg[mine_rows, :] + mm(agg_t[mine_rows, :], mid[...])).astype(BF)
        else:
            total[...] = agg[...] + mm(agg_t[...], mid[...])
        middle(parts, mine.at[q])
        new_cov[...] = cov[...] + mm(mine_t[...], mid[...])

    @pl.when(jnp.logical_not(lower))
    def _():
        place_whole(c_parts, got, lo, q, n)
        middle(here, got.at[q])
        for rows, value in own_columns(parts, lo, q, n, nb):
            total[rows, :] = value[...].astype(F32)
        for p in range(n):
            total[p * w : (p + 1) * w, :] += mm_t(got[p], mid[...])
        new_cov[...] = cov[...]
        if to_last:
            share[...] = total[mine_rows, :].astype(BF)

    if not to_last:
        new_agg, new_agg_bf = outs[2:]
        new_agg[...] = total[...]
        new_agg_bf[...] = total[...].astype(BF)
        share[...] = new_agg_bf[mine_rows, :]


def last_cov_kernel(n, m, bit, *refs):
    (cov, mine, mine_t), parts, (out,), (mid,) = split(refs, 3, m, 1, 1)
    hi, lo, q = where_am_i()
    lower = is_lower(bit)

    @pl.when(lower)
    def _():
        for rows, value in times(parts, mine.at[q], lo, q, n):
            mid[rows, :] = value.astype(BF)
        out[0] = cov[...] + mm(mine_t[...], mid[...])

    @pl.when(jnp.logical_not(lower))
    def _():
        out[0] = cov[...]


def over_panels(x):
    n = lax.axis_size("panel")
    return [x] + [
        lax.ppermute(x, "panel", [((i + r) % n, i) for i in range(n)]) for r in range(1, n)
    ]


def swap(value, odd_mask, even_mask):
    steps, n = lax.axis_size("tm"), lax.axis_size("panel")
    pairs = []
    for t in range(steps):
        for q in range(n):
            mask = odd_mask if q % 2 else even_mask
            pairs.append((t * n + q, (t ^ mask) * n + q))
    return lax.ppermute(value, ("tm", "panel"), pairs)


def across(x, bit, last):
    steps = lax.axis_size("tm")
    d = GROUP << bit
    return lax.ppermute(
        x, "tm", [(t, t ^ d) for t in range(steps) if (t ^ d) < steps and (t & d or not last)]
    )


def in_group(x):
    return [x] + [swap(x, mask, mask) for mask in range(1, GROUP)]


def quarters(x):
    return [p for block in in_group(x) for p in over_panels(block)]


def after(x, *others):
    return lax.optimization_barrier((x, *others))[0]


def shards(factor_inverse, coupling, sigma_after):
    steps = lax.axis_size("tm")
    n = lax.axis_size("panel")
    nb, w = factor_inverse.shape[1:]
    levels = (steps // GROUP - 1).bit_length()
    panel_bf = jax.ShapeDtypeStruct((nb, w), BF)
    panel_f32 = jax.ShapeDtypeStruct((nb, w), F32)
    full_bf = jax.ShapeDtypeStruct((n, nb, w), BF)
    square_bf = jax.ShapeDtypeStruct((nb, nb), BF)
    group_bf = jax.ShapeDtypeStruct((GROUP, n, nb, w), BF)
    turned_bf = jax.ShapeDtypeStruct((GROUP - 1, nb, nb), BF)
    share_bf = jax.ShapeDtypeStruct((nb // GROUP, w), BF)
    full_scratch = pltpu.VMEM((n, nb, w), BF)
    one = 2 * nb * nb * w
    sems = pltpu.SemaphoreType.DMA

    comp = coupling[0].astype(BF)
    c_first = swap(comp, 1, 2)
    c_second = swap(comp, 2, 1)
    factor = after(factor_inverse[0], comp)
    f_parts = over_panels(factor.astype(BF))
    c_own = over_panels(comp)
    base, base_bf = call(
        functools.partial(base_kernel, n),
        [factor, sigma_after, *f_parts, *c_own],
        [VMEM] + [ANY] * (1 + 2 * n),
        [panel_f32, panel_bf],
        [full_scratch, full_scratch, pltpu.VMEM((nb, n * w), F32), sems((n + 1,))],
        2 * one,
    )
    c_diag = swap(after(c_first, base_bf), 2, 1)
    s_first = swap(base_bf, 1, 2)
    c_diag = after(c_diag, s_first)
    c_pieces = [p for v in (c_first, c_second, c_diag) for p in over_panels(v)]
    s_second = swap(after(base_bf, c_second), 2, 1)
    c_all, c01, c23, agg_c = call(
        functools.partial(group_comp_kernel, n),
        c_own + c_pieces,
        [ANY] * (GROUP * n),
        [group_bf, full_bf, square_bf, full_bf],
        [sems((GROUP, n))],
        3 * n * one,
    )
    agg_panel = lax.dynamic_index_in_dim(agg_c, lax.axis_index("panel"), 0, keepdims=False)
    c_got = across(agg_panel, 0, levels == 1)
    c_t, c01_t, mine, mine_t, agg_t = call(
        functools.partial(tail_comp_kernel, n),
        [c_all, c01, c23, agg_c],
        [VMEM] * 4,
        [turned_bf, square_bf, full_bf, square_bf, square_bf],
        [],
        n * one,
    )
    s_diag = swap(s_first, 2, 1)
    s_own = over_panels(after(base_bf, c_got))
    s_pieces = s_own + [p for v in (s_first, s_second, s_diag) for p in over_panels(v)]
    cov, agg, agg_bf = call(
        functools.partial(group_cov_kernel, n),
        [base, c_all, c_t, c01, c01_t, *s_pieces],
        [VMEM] * 5 + [ANY] * (GROUP * n),
        [panel_f32, panel_f32, panel_bf],
        [pltpu.VMEM((GROUP, n, nb, w), BF), pltpu.VMEM((nb, nb), BF), sems((GROUP, n))],
        (2 * n + 6) * one,
    )
    out_cov = jax.ShapeDtypeStruct((1, nb, w), F32)
    out_comp = jax.ShapeDtypeStruct((1, nb, w), BF)
    panel_scratch = pltpu.VMEM((nb, w), BF)
    sum_scratch = pltpu.VMEM((nb, w), F32)
    c_parts = over_panels(c_got)
    s_send = agg_bf
    for bit in range(levels):
        last = bit + 1 == levels
        to_last = bit + 2 == levels
        m = len(c_parts)
        s_got = across(s_send, bit, last)
        if last:
            (prop,) = call(
                functools.partial(last_comp_kernel, n, m, bit),
                [mine, *c_parts],
                [VMEM] * (1 + m),
                [out_comp],
                [],
                one,
            )
            s_got = after(s_got, prop)
            s_parts = quarters(s_got) if bit else over_panels(s_got)
            (cov,) = call(
                functools.partial(last_cov_kernel, n, m, bit),
                [cov, mine, mine_t, *s_parts],
                [VMEM] * (3 + m),
                [out_cov],
                [panel_scratch],
                2 * one,
            )
            break
        agg_in = after(agg_c, agg_bf)
        if to_last:
            (c_send,) = call(
                functools.partial(share_comp_kernel, n, m, bit),
                [agg_in, *c_parts],
                [VMEM] * (1 + m),
                [share_bf],
                [full_scratch, panel_scratch],
                one,
            )
        else:
            new_agg_c, new_agg_t, c_send = call(
                functools.partial(pair_comp_kernel, n, m, bit),
                [agg_in, *c_parts],
                [VMEM] * (1 + m),
                [full_bf, square_bf, share_bf],
                [full_scratch],
                n * one,
            )
        c_far = across(c_send, bit + 1, to_last)
        new_mine, new_mine_t = call(
            functools.partial(mine_comp_kernel, n, m, bit),
            [after(mine, c_send), mine_t, *c_parts],
            [VMEM] * (2 + m),
            [full_bf, square_bf],
            [],
            n * one,
        )
        s_got = after(s_got, c_far, new_mine)
        s_parts = quarters(s_got) if bit else over_panels(s_got)
        c_blocks = in_group(c_far)
        outs = call(
            functools.partial(level_cov_kernel, n, m, bit, to_last),
            [cov, agg, mine, mine_t, agg_c, agg_t, *over_panels(agg_bf), *c_parts, *s_parts],
            [VMEM] * (6 + n + 2 * m),
            [panel_f32, share_bf] + ([] if to_last else [panel_f32, panel_bf]),
            [panel_scratch, sum_scratch, full_scratch],
            4 * one,
        )
        cov, s_send = outs[:2]
        if not to_last:
            agg, agg_bf = outs[2:]
            agg_c, agg_t = new_agg_c, new_agg_t
        c_parts = [p for b in c_blocks for p in over_panels(after(b, s_send))]
        mine, mine_t = new_mine, new_mine_t
    return cov, prop


def solution(mesh):
    placed = (P("tm", None, "panel"), P("tm", None, "panel"), P())
    return jax.shard_map(
        shards,
        mesh=mesh,
        in_specs=placed,
        out_specs=(P("tm", None, "panel"), P("tm", None, "panel")),
        check_vma=False,
    )
```

profile of v0, /device:TPU:0, one launch (start us, length us, event | category | flops | bytes accessed | tf_op | source)
XLA Modules:
  0.0 124.0 jit_solution(15968661655179150117)
XLA Ops:
  0.6 1.5 %convert_bitcast_fusion.refs_4_.refs_0_ = bf16[768,384]{1,0:T(8,128)(2,1)S(1)} fusion(f32[1,768,384]{2,1,0:T(8,128)} %param.4), kind=kLoop, calls=%fused_computation.1 | loop fusion | flops 294912 | bytes 1769472 | tf_op jit(solution)/shard_map/convert_element_type | solution.py:449
  2.9 2.9 %collective-permute-start.2 = (bf16[768,384]{1,0:T(8,128)(2,1)S(1)}, bf16[768,384]{1,0:T(8,128)(2,1)}, u32[]{:S(2)}, u32[]{:S(2)}) collective-permute-start(bf16[768,384]{1,0:T(8,128)(2,1)S(1)} %convert_bitcast_fusion.refs_4_.refs_0_), channel_id=1, source_target_pairs={{0,4},{1,3},{2,6},{3,1},{4,0},{5,7},{6,2},{7,5},{8,12},{9,11},{10,... | collective-permute-start | bytes 1769480 | tf_op jit(solution)/shard_map/ppermute | solution.py:410
  5.9 1.5 %collective-permute-start.4 = (bf16[768,384]{1,0:T(8,128)(2,1)S(1)}, bf16[768,384]{1,0:T(8,128)(2,1)}, u32[]{:S(2)}, u32[]{:S(2)}) collective-permute-start(bf16[768,384]{1,0:T(8,128)(2,1)S(1)} %convert_bitcast_fusion.refs_4_.refs_0_), channel_id=1, source_target_pairs={{0,2},{1,5},{2,0},{3,7},{4,6},{5,1},{6,4},{7,3},{8,10},{9,13},{10,... | collective-permute-start | bytes 1769480 | tf_op jit(solution)/shard_map/ppermute | solution.py:410
  7.4 1.8 %shard_map.50 = (f32[768,384]{1,0:T(8,128)S(1)}, bf16[768,384]{1,0:T(8,128)(2,1)S(1)}) custom-call(f32[768,384]{1,0:T(8,128)S(1)} %bitcast.6, f32[768,768]{1,0:T(8,128)S(1)} %copy-done.1, bf16[768,384]{1,0:T(8,128)(2,1)S(1)} %convert_element_type.10.refs_2_, bf16[768,384]{1,0:T(8,128)(2,1)S(1)} %collective-permute-done.refs_3_, ...), custom_call_target="tpu_custom_call" | custom-call | flops 905969664 | bytes 7667712 | tf_op jit(solution)/shard_map/pallas_call | solution.py:93
  9.2 10.2 %collective-permute-done.2.refs_2_ = bf16[768,384]{1,0:T(8,128)(2,1)} collective-permute-done((bf16[768,384]{1,0:T(8,128)(2,1)S(1)}, bf16[768,384]{1,0:T(8,128)(2,1)}, u32[]{:S(2)}, u32[]{:S(2)}) %collective-permute-start.2) | collective-permute-done | bytes 589856 | tf_op jit(solution)/shard_map/ppermute | solution.py:410
  19.4 1.9 %collective-permute-start.6 = (bf16[768,384]{1,0:T(8,128)(2,1)}, bf16[768,384]{1,0:T(8,128)(2,1)}, u32[]{:S(2)}, u32[]{:S(2)}) collective-permute-start(bf16[768,384]{1,0:T(8,128)(2,1)} %collective-permute-done.2.refs_2_), channel_id=1, source_target_pairs={{0,2},{1,5},{2,0},{3,7},{4,6},{5,1},{6,4},{7,3},{8,10},{9,13},{10,... | collective-permute-start | bytes 1769480 | tf_op jit(solution)/shard_map/ppermute | solution.py:410
  21.3 1.7 %collective-permute-start.7 = (bf16[768,384]{1,0:T(8,128)(2,1)S(1)}, bf16[768,384]{1,0:T(8,128)(2,1)S(1)}, u32[]{:S(2)}, u32[]{:S(2)}) collective-permute-start(bf16[768,384]{1,0:T(8,128)(2,1)S(1)} %get-tuple-element.45.refs_5_), channel_id=1, source_target_pairs={{0,4},{1,3},{2,6},{3,1},{4,0},{5,7},{6,2},{7,5},{8,12},{9,11},{10,... | collective-permute-start | bytes 1769480 | tf_op jit(solution)/shard_map/ppermute | solution.py:410
  23.5 12.0 %collective-permute-done.6.refs_6_ = bf16[768,384]{1,0:T(8,128)(2,1)} collective-permute-done((bf16[768,384]{1,0:T(8,128)(2,1)}, bf16[768,384]{1,0:T(8,128)(2,1)}, u32[]{:S(2)}, u32[]{:S(2)}) %collective-permute-start.6) | collective-permute-done | bytes 589856 | tf_op jit(solution)/shard_map/ppermute | solution.py:410
  36.5 1.1 collective-permute-start.14
  37.9 4.5 %shard_map.51 = (bf16[4,2,768,384]{3,2,1,0:T(8,128)(2,1)S(1)}, bf16[2,768,384]{2,1,0:T(8,128)(2,1)S(1)}, bf16[768,768]{1,0:T(8,128)(2,1)S(1)}, bf16[2,768,384]{2,1,0:T(8,128)(2,1)S(1)}) custom-call(bf16[768,384]{1,0:T(8,128)(2,1)S(1)} %convert_bitcast_fusion.refs_4_.refs_0_, bf16[768,384]{1,0:T(8,128)(2,1)S(1)} %collective-permute-done.1.refs_5_.refs_1_, ...), custom_call_target="tpu_custom_call" | custom-call | flops 2717908992 | bytes 12976128 | tf_op jit(solution)/shard_map/pallas_call | solution.py:93
  42.5 1.1 collective-permute-start.9
  43.6 1.9 %collective-permute-done.12.refs_9_ = bf16[768,384]{1,0:T(8,128)(2,1)S(1)} collective-permute-done((bf16[768,384]{1,0:T(8,128)(2,1)S(1)}, bf16[768,384]{1,0:T(8,128)(2,1)S(1)}, u32[]{:S(2)}, u32[]{:S(2)}) %collective-permute-start.12) | collective-permute-done | bytes 589856 | tf_op jit(solution)/shard_map/ppermute | solution.py:410
  45.5 6.3 %collective-permute-done.14.refs_11_ = bf16[768,384]{1,0:T(8,128)(2,1)S(1)} collective-permute-done((bf16[768,384]{1,0:T(8,128)(2,1)S(1)}, bf16[768,384]{1,0:T(8,128)(2,1)S(1)}, u32[]{:S(2)}, u32[]{:S(2)}) %collective-permute-start.14) | collective-permute-done | bytes 589856 | tf_op jit(solution)/shard_map/ppermute | solution.py:410
  51.8 6.2 %collective-permute-done.9.refs_1_.refs_2_.refs_8_ = bf16[768,384]{1,0:T(8,128)(2,1)S(1)} collective-permute-done((bf16[768,384]{1,0:T(8,128)(2,1)S(1)}, bf16[768,384]{1,0:T(8,128)(2,1)S(1)}, u32[]{:S(2)}, u32[]{:S(2)}) %collective-permute-start.9) | collective-permute-done | bytes 589856 | tf_op jit(solution)/shard_map/ppermute | solution.py:416
  58.0 1.8 %shard_map.52 = (bf16[3,768,768]{2,1,0:T(8,128)(2,1)S(1)}, bf16[768,768]{1,0:T(8,128)(2,1)S(1)}, bf16[2,768,384]{2,1,0:T(8,128)(2,1)S(1)}, bf16[768,768]{1,0:T(8,128)(2,1)S(1)}, bf16[768,768]{1,0:T(8,128)(2,1)S(1)}) custom-call(bf16[4,2,768,384]{3,2,1,0:T(8,128)(2,1)S(1)} %get-tuple-element.38.c.refs_1_, ...), custom_call_target="tpu_custom_call" | custom-call | flops 905969664 | bytes 16515072 | tf_op jit(solution)/shard_map/pallas_call | solution.py:93
  60.3 7.0 %shard_map.53 = (f32[768,384]{1,0:T(8,128)S(1)}, f32[768,384]{1,0:T(8,128)S(1)}, bf16[768,384]{1,0:T(8,128)(2,1)S(1)}) custom-call(f32[768,384]{1,0:T(8,128)S(1)} %get-tuple-element.34.refs_0_, bf16[4,2,768,384]{3,2,1,0:T(8,128)(2,1)S(1)} %get-tuple-element.38.c.refs_1_, bf16[3,768,768]{2,1,0:T(8,128)(2,1)S(1)} %get-tuple-element.42.refs_2_, ...), custom_call_target="tpu_custom_call" | custom-call | flops 4529848320 | bytes 19464192 | tf_op jit(solution)/shard_map/pallas_call | solution.py:93
  67.4 1.1 collective-permute-start.18
  69.3 1.3 %collective-permute-start.19 = (bf16[192,384]{1,0:T(8,128)(2,1)S(1)}, bf16[192,384]{1,0:T(8,128)(2,1)S(1)}, u32[]{:S(2)}, u32[]{:S(2)}) collective-permute-start(bf16[192,384]{1,0:T(8,128)(2,1)S(1)} %shard_map.54), channel_id=1, source_target_pairs={{16,0},{18,2},{20,4},{22,6},{24,8},{26,10},{28,12},{30,14},{17,1},... | collective-permute-start | bytes 442376 | tf_op jit(solution)/shard_map/ppermute | solution.py:416
  70.7 1.8 %shard_map.55 = (bf16[2,768,384]{2,1,0:T(8,128)(2,1)S(1)}, bf16[768,768]{1,0:T(8,128)(2,1)S(1)}) custom-call(bf16[2,768,384]{2,1,0:T(8,128)(2,1)S(1)} %get-tuple-element.53.refs_0_.refs_2_, bf16[768,768]{1,0:T(8,128)(2,1)S(1)} %get-tuple-element.49.refs_1_.refs_3_, bf16[768,384]{1,0:T(8,128)(2,1)S(1)} %collective-permute-done.9.refs_1_.refs_2_.refs_8_, ...), custom_call_target="tpu_custom_call" | custom-call | flops 905969664 | bytes 5898240 | tf_op jit(solution)/shard_map/pallas_call | solution.py:93
  72.5 5.2 %collective-permute-done.19.refs_1_ = bf16[192,384]{1,0:T(8,128)(2,1)S(1)} collective-permute-done((bf16[192,384]{1,0:T(8,128)(2,1)S(1)}, bf16[192,384]{1,0:T(8,128)(2,1)S(1)}, u32[]{:S(2)}, u32[]{:S(2)}) %collective-permute-start.19) | collective-permute-done | bytes 147488 | tf_op jit(solution)/shard_map/ppermute | solution.py:416
  77.7 8.1 %collective-permute-done.18.refs_10_ = bf16[768,384]{1,0:T(8,128)(2,1)S(1)} collective-permute-done((bf16[768,384]{1,0:T(8,128)(2,1)S(1)}, bf16[768,384]{1,0:T(8,128)(2,1)S(1)}, u32[]{:S(2)}, u32[]{:S(2)}) %collective-permute-start.18) | collective-permute-done | bytes 589856 | tf_op jit(solution)/shard_map/ppermute | solution.py:416
  85.8 1.3 %collective-permute-start.27 = (bf16[192,384]{1,0:T(8,128)(2,1)S(1)}, bf16[192,384]{1,0:T(8,128)(2,1)S(1)}, u32[]{:S(2)}, u32[]{:S(2)}) collective-permute-start(bf16[192,384]{1,0:T(8,128)(2,1)S(1)} %collective-permute-done.19.refs_1_), channel_id=1, source_target_pairs={{0,6},{1,7},{2,4},{3,5},{4,2},{5,3},{6,0},{7,1},{8,14},{9,15},{10,... | collective-permute-start | bytes 442376 | tf_op jit(solution)/shard_map/ppermute | solution.py:410
  87.1 3.6 %collective-permute-start.25 = (bf16[192,384]{1,0:T(8,128)(2,1)S(1)}, bf16[192,384]{1,0:T(8,128)(2,1)S(1)}, u32[]{:S(2)}, u32[]{:S(2)}) collective-permute-start(bf16[192,384]{1,0:T(8,128)(2,1)S(1)} %collective-permute-done.19.refs_1_), channel_id=1, source_target_pairs={{0,4},{1,5},{2,6},{3,7},{4,0},{5,1},{6,2},{7,3},{8,12},{9,13},{10,... | collective-permute-start | bytes 442376 | tf_op jit(solution)/shard_map/ppermute | solution.py:410
  90.7 2.7 %shard_map.56 = (f32[768,384]{1,0:T(8,128)S(1)}, bf16[192,384]{1,0:T(8,128)(2,1)S(1)}) custom-call(f32[768,384]{1,0:T(8,128)S(1)} %get-tuple-element.46.refs_0_, f32[768,384]{1,0:T(8,128)S(1)} %get-tuple-element.47.refs_1_, bf16[2,768,384]{2,1,0:T(8,128)(2,1)S(1)} %get-tuple-element.53.refs_0_.refs_2_, ...), custom_call_target="tpu_custom_call" | custom-call | flops 1811939328 | bytes 11943936 | tf_op jit(solution)/shard_map/pallas_call | solution.py:93
  93.5 2.6 %collective-permute-done.25.refs_5_ = bf16[192,384]{1,0:T(8,128)(2,1)S(1)} collective-permute-done((bf16[192,384]{1,0:T(8,128)(2,1)S(1)}, bf16[192,384]{1,0:T(8,128)(2,1)S(1)}, u32[]{:S(2)}, u32[]{:S(2)}) %collective-permute-start.25) | collective-permute-done | bytes 147488 | tf_op jit(solution)/shard_map/ppermute | solution.py:410
  97.4 1.3 %collective-permute-start.21 = (bf16[192,384]{1,0:T(8,128)(2,1)S(1)}, bf16[192,384]{1,0:T(8,128)(2,1)S(1)}, u32[]{:S(2)}, u32[]{:S(2)}) collective-permute-start(bf16[192,384]{1,0:T(8,128)(2,1)S(1)} %get-tuple-element.58), channel_id=1, source_target_pairs={{16,0},{18,2},{20,4},{22,6},{24,8},{26,10},{28,12},{30,14},{17,1},... | collective-permute-start | bytes 442376 | tf_op jit(solution)/shard_map/ppermute | solution.py:416
  98.8 1.7 %shard_map.57 = bf16[1,768,384]{2,1,0:T(8,128)(2,1)} custom-call(bf16[2,768,384]{2,1,0:T(8,128)(2,1)S(1)} %get-tuple-element.54.refs_0_.refs_1_, bf16[192,384]{1,0:T(8,128)(2,1)S(1)} %collective-permute-done.19.refs_1_, bf16[192,384]{1,0:T(8,128)(2,1)S(1)} %collective-permute-done.22.refs_2_, bf16[192,384]{1,0:T(8,128)(2,1)S(1)} %collective-permute-done.23.refs_3_, ...), custom_call_target="tpu_custom_call" | custom-call | flops 452984832 | bytes 2949120 | tf_op jit(solution)/shard_map/pallas_call | solution.py:93
  100.5 8.6 %collective-permute-done.21.refs_3_ = bf16[192,384]{1,0:T(8,128)(2,1)S(1)} collective-permute-done((bf16[192,384]{1,0:T(8,128)(2,1)S(1)}, bf16[192,384]{1,0:T(8,128)(2,1)S(1)}, u32[]{:S(2)}, u32[]{:S(2)}) %collective-permute-start.21) | collective-permute-done | bytes 147488 | tf_op jit(solution)/shard_map/ppermute | solution.py:416
  109.1 2.3 %collective-permute-start.30 = (bf16[192,384]{1,0:T(8,128)(2,1)S(1)}, bf16[192,384]{1,0:T(8,128)(2,1)S(1)}, u32[]{:S(2)}, u32[]{:S(2)}) collective-permute-start(bf16[192,384]{1,0:T(8,128)(2,1)S(1)} %collective-permute-done.21.refs_3_), channel_id=1, source_target_pairs={{0,2},{1,3},{2,0},{3,1},{4,6},{5,7},{6,4},{7,5},{8,10},{9,11},{10,... | collective-permute-start | bytes 442376 | tf_op jit(solution)/shard_map/ppermute | solution.py:410
  112.9 2.8 %collective-permute-done.30.refs_5_ = bf16[192,384]{1,0:T(8,128)(2,1)S(1)} collective-permute-done((bf16[192,384]{1,0:T(8,128)(2,1)S(1)}, bf16[192,384]{1,0:T(8,128)(2,1)S(1)}, u32[]{:S(2)}, u32[]{:S(2)}) %collective-permute-start.30) | collective-permute-done | bytes 147488 | tf_op jit(solution)/shard_map/ppermute | solution.py:410
  115.7 4.1 %collective-permute-done.32.refs_7_ = bf16[192,384]{1,0:T(8,128)(2,1)S(1)} collective-permute-done((bf16[192,384]{1,0:T(8,128)(2,1)S(1)}, bf16[192,384]{1,0:T(8,128)(2,1)S(1)}, u32[]{:S(2)}, u32[]{:S(2)}) %collective-permute-start.32) | collective-permute-done | bytes 147488 | tf_op jit(solution)/shard_map/ppermute | solution.py:410
  121.3 2.7 %shard_map.58 = f32[1,768,384]{2,1,0:T(8,128)} custom-call(f32[768,384]{1,0:T(8,128)S(1)} %get-tuple-element.56.refs_0_, bf16[2,768,384]{2,1,0:T(8,128)(2,1)S(1)} %get-tuple-element.54.refs_0_.refs_1_, bf16[768,768]{1,0:T(8,128)(2,1)S(1)} %get-tuple-element.57.refs_2_, bf16[192,384]{1,0:T(8,128)(2,1)S(1)} %collective-permute-done.21.refs_3_, ...), custom_call_target="tpu_custom_call" | custom-call | flops 905969664 | bytes 5898240 | tf_op jit(solution)/shard_map/pallas_call | solution.py:93
  (56 shorter events, 8.6 us)
Async XLA Ops:
  2.3 5.0 %collective-permute-start = (bf16[768,384]{1,0:T(8,128)(2,1)S(1)}, bf16[768,384]{1,0:T(8,128)(2,1)S(1)}, u32[]{:S(2)}, u32[]{:S(2)}) collective-permute-start(bf16[768,384]{1,0:T(8,128)(2,1)S(1)} %convert_element_type.10.refs_2_), channel_id=1, source_target_pairs={{1,0},{0,1},{3,2},{2,3},{5,4},{4,5},{7,6},{6,7},{9,8},{8,9},{11,10... | collective-permute-start | bytes 1769480 | tf_op jit(solution)/shard_map/ppermute | solution.py:399
  2.8 4.5 %collective-permute-start.1 = (bf16[768,384]{1,0:T(8,128)(2,1)S(1)}, bf16[768,384]{1,0:T(8,128)(2,1)S(1)}, u32[]{:S(2)}, u32[]{:S(2)}) collective-permute-start(bf16[768,384]{1,0:T(8,128)(2,1)S(1)} %convert_bitcast_fusion.refs_4_.refs_0_), channel_id=1, source_target_pairs={{1,0},{0,1},{3,2},{2,3},{5,4},{4,5},{7,6},{6,7},{9,8},{8,9},{11,10... | collective-permute-start | bytes 1769480 | tf_op jit(solution)/shard_map/ppermute | solution.py:399
  2.9 16.4 %collective-permute-start.2 = (bf16[768,384]{1,0:T(8,128)(2,1)S(1)}, bf16[768,384]{1,0:T(8,128)(2,1)}, u32[]{:S(2)}, u32[]{:S(2)}) collective-permute-start(bf16[768,384]{1,0:T(8,128)(2,1)S(1)} %convert_bitcast_fusion.refs_4_.refs_0_), channel_id=1, source_target_pairs={{0,4},{1,3},{2,6},{3,1},{4,0},{5,7},{6,2},{7,5},{8,12},{9,11},{10,... | collective-permute-start | bytes 1769480 | tf_op jit(solution)/shard_map/ppermute | solution.py:410
  5.9 17.2 %collective-permute-start.4 = (bf16[768,384]{1,0:T(8,128)(2,1)S(1)}, bf16[768,384]{1,0:T(8,128)(2,1)}, u32[]{:S(2)}, u32[]{:S(2)}) collective-permute-start(bf16[768,384]{1,0:T(8,128)(2,1)S(1)} %convert_bitcast_fusion.refs_4_.refs_0_), channel_id=1, source_target_pairs={{0,2},{1,5},{2,0},{3,7},{4,6},{5,1},{6,4},{7,3},{8,10},{9,13},{10,... | collective-permute-start | bytes 1769480 | tf_op jit(solution)/shard_map/ppermute | solution.py:410
  19.4 16.2 %collective-permute-start.6 = (bf16[768,384]{1,0:T(8,128)(2,1)}, bf16[768,384]{1,0:T(8,128)(2,1)}, u32[]{:S(2)}, u32[]{:S(2)}) collective-permute-start(bf16[768,384]{1,0:T(8,128)(2,1)} %collective-permute-done.2.refs_2_), channel_id=1, source_target_pairs={{0,2},{1,5},{2,0},{3,7},{4,6},{5,1},{6,4},{7,3},{8,10},{9,13},{10,... | collective-permute-start | bytes 1769480 | tf_op jit(solution)/shard_map/ppermute | solution.py:410
  21.3 14.3 %collective-permute-start.7 = (bf16[768,384]{1,0:T(8,128)(2,1)S(1)}, bf16[768,384]{1,0:T(8,128)(2,1)S(1)}, u32[]{:S(2)}, u32[]{:S(2)}) collective-permute-start(bf16[768,384]{1,0:T(8,128)(2,1)S(1)} %get-tuple-element.45.refs_5_), channel_id=1, source_target_pairs={{0,4},{1,3},{2,6},{3,1},{4,0},{5,7},{6,2},{7,5},{8,12},{9,11},{10,... | collective-permute-start | bytes 1769480 | tf_op jit(solution)/shard_map/ppermute | solution.py:410
  23.0 14.6 %collective-permute-start.3 = (bf16[768,384]{1,0:T(8,128)(2,1)}, bf16[768,384]{1,0:T(8,128)(2,1)}, u32[]{:S(2)}, u32[]{:S(2)}) collective-permute-start(bf16[768,384]{1,0:T(8,128)(2,1)} %collective-permute-done.2.refs_2_), channel_id=1, source_target_pairs={{1,0},{0,1},{3,2},{2,3},{5,4},{4,5},{7,6},{6,7},{9,8},{8,9},{11,10... | collective-permute-start | bytes 1769480 | tf_op jit(solution)/shard_map/ppermute | solution.py:399
  23.0 14.6 %collective-permute-start.5 = (bf16[768,384]{1,0:T(8,128)(2,1)}, bf16[768,384]{1,0:T(8,128)(2,1)}, u32[]{:S(2)}, u32[]{:S(2)}) collective-permute-start(bf16[768,384]{1,0:T(8,128)(2,1)} %collective-permute-done.4.refs_4_), channel_id=1, source_target_pairs={{1,0},{0,1},{3,2},{2,3},{5,4},{4,5},{7,6},{6,7},{9,8},{8,9},{11,10... | collective-permute-start | bytes 1769480 | tf_op jit(solution)/shard_map/ppermute | solution.py:399
  35.6 2.3 %collective-permute-start.8 = (bf16[768,384]{1,0:T(8,128)(2,1)}, bf16[768,384]{1,0:T(8,128)(2,1)}, u32[]{:S(2)}, u32[]{:S(2)}) collective-permute-start(bf16[768,384]{1,0:T(8,128)(2,1)} %collective-permute-done.6.refs_6_), channel_id=1, source_target_pairs={{1,0},{0,1},{3,2},{2,3},{5,4},{4,5},{7,6},{6,7},{9,8},{8,9},{11,10... | collective-permute-start | bytes 1769480 | tf_op jit(solution)/shard_map/ppermute | solution.py:399
  35.6 9.9 %collective-permute-start.12 = (bf16[768,384]{1,0:T(8,128)(2,1)S(1)}, bf16[768,384]{1,0:T(8,128)(2,1)S(1)}, u32[]{:S(2)}, u32[]{:S(2)}) collective-permute-start(bf16[768,384]{1,0:T(8,128)(2,1)S(1)} %get-tuple-element.45.refs_5_), channel_id=1, source_target_pairs={{0,2},{1,5},{2,0},{3,7},{4,6},{5,1},{6,4},{7,3},{8,10},{9,13},{10,... | collective-permute-start | bytes 1769480 | tf_op jit(solution)/shard_map/ppermute | solution.py:410
  36.5 15.3 %collective-permute-start.14 = (bf16[768,384]{1,0:T(8,128)(2,1)S(1)}, bf16[768,384]{1,0:T(8,128)(2,1)S(1)}, u32[]{:S(2)}, u32[]{:S(2)}) collective-permute-start(bf16[768,384]{1,0:T(8,128)(2,1)S(1)} %collective-permute-done.7.refs_7_), channel_id=1, source_target_pairs={{0,2},{1,5},{2,0},{3,7},{4,6},{5,1},{6,4},{7,3},{8,10},{9,13},{10,... | collective-permute-start | bytes 1769480 | tf_op jit(solution)/shard_map/ppermute | solution.py:410
  42.5 15.4 %collective-permute-start.9 = (bf16[768,384]{1,0:T(8,128)(2,1)S(1)}, bf16[768,384]{1,0:T(8,128)(2,1)S(1)}, u32[]{:S(2)}, u32[]{:S(2)}) collective-permute-start(bf16[768,384]{1,0:T(8,128)(2,1)S(1)} %dynamic-slice_bitcast_fusion), channel_id=1, source_target_pairs={{0,8},{2,10},{4,12},{6,14},{8,0},{10,2},{12,4},{14,6},{16,24},{18,... | collective-permute-start | bytes 1769480 | tf_op jit(solution)/shard_map/ppermute | solution.py:416
  43.6 16.7 %collective-permute-start.11 = (bf16[768,384]{1,0:T(8,128)(2,1)S(1)}, bf16[768,384]{1,0:T(8,128)(2,1)S(1)}, u32[]{:S(2)}, u32[]{:S(2)}) collective-permute-start(bf16[768,384]{1,0:T(8,128)(2,1)S(1)} %collective-permute-done.7.refs_7_), channel_id=1, source_target_pairs={{1,0},{0,1},{3,2},{2,3},{5,4},{4,5},{7,6},{6,7},{9,8},{8,9},{11,10... | collective-permute-start | bytes 1769480 | tf_op jit(solution)/shard_map/ppermute | solution.py:399
  45.5 14.8 %collective-permute-start.13 = (bf16[768,384]{1,0:T(8,128)(2,1)S(1)}, bf16[768,384]{1,0:T(8,128)(2,1)S(1)}, u32[]{:S(2)}, u32[]{:S(2)}) collective-permute-start(bf16[768,384]{1,0:T(8,128)(2,1)S(1)} %collective-permute-done.12.refs_9_), channel_id=1, source_target_pairs={{1,0},{0,1},{3,2},{2,3},{5,4},{4,5},{7,6},{6,7},{9,8},{8,9},{11,10... | collective-permute-start | bytes 1769480 | tf_op jit(solution)/shard_map/ppermute | solution.py:399
  51.8 8.5 %collective-permute-start.15 = (bf16[768,384]{1,0:T(8,128)(2,1)S(1)}, bf16[768,384]{1,0:T(8,128)(2,1)S(1)}, u32[]{:S(2)}, u32[]{:S(2)}) collective-permute-start(bf16[768,384]{1,0:T(8,128)(2,1)S(1)} %collective-permute-done.14.refs_11_), channel_id=1, source_target_pairs={{1,0},{0,1},{3,2},{2,3},{5,4},{4,5},{7,6},{6,7},{9,8},{8,9},{11,10... | collective-permute-start | bytes 1769480 | tf_op jit(solution)/shard_map/ppermute | solution.py:399
  58.0 2.3 %collective-permute-start.10 = (bf16[768,384]{1,0:T(8,128)(2,1)S(1)}, bf16[768,384]{1,0:T(8,128)(2,1)S(1)}, u32[]{:S(2)}, u32[]{:S(2)}) collective-permute-start(bf16[768,384]{1,0:T(8,128)(2,1)S(1)} %get-tuple-element.45.refs_5_), channel_id=1, source_target_pairs={{1,0},{0,1},{3,2},{2,3},{5,4},{4,5},{7,6},{6,7},{9,8},{8,9},{11,10... | collective-permute-start | bytes 1769480 | tf_op jit(solution)/shard_map/ppermute | solution.py:399
  59.7 8.7 %collective-permute-start.17 = (bf16[768,384]{1,0:T(8,128)(2,1)S(1)}, bf16[768,384]{1,0:T(8,128)(2,1)S(1)}, u32[]{:S(2)}, u32[]{:S(2)}) collective-permute-start(bf16[768,384]{1,0:T(8,128)(2,1)S(1)} %collective-permute-done.9.refs_1_.refs_2_.refs_8_), channel_id=1, source_target_pairs={{1,0},{0,1},{3,2},{2,3},{5,4},{4,5},{7,6},{6,7},{9,8},{8,9},{11,10... | collective-permute-start | bytes 1769480 | tf_op jit(solution)/shard_map/ppermute | solution.py:399
  67.4 18.5 %collective-permute-start.18 = (bf16[768,384]{1,0:T(8,128)(2,1)S(1)}, bf16[768,384]{1,0:T(8,128)(2,1)S(1)}, u32[]{:S(2)}, u32[]{:S(2)}) collective-permute-start(bf16[768,384]{1,0:T(8,128)(2,1)S(1)} %get-tuple-element.51.refs_6_), channel_id=1, source_target_pairs={{0,8},{2,10},{4,12},{6,14},{8,0},{10,2},{12,4},{14,6},{16,24},{18,... | collective-permute-start | bytes 1769480 | tf_op jit(solution)/shard_map/ppermute | solution.py:416
  69.3 8.4 %collective-permute-start.19 = (bf16[192,384]{1,0:T(8,128)(2,1)S(1)}, bf16[192,384]{1,0:T(8,128)(2,1)S(1)}, u32[]{:S(2)}, u32[]{:S(2)}) collective-permute-start(bf16[192,384]{1,0:T(8,128)(2,1)S(1)} %shard_map.54), channel_id=1, source_target_pairs={{16,0},{18,2},{20,4},{22,6},{24,8},{26,10},{28,12},{30,14},{17,1},... | collective-permute-start | bytes 442376 | tf_op jit(solution)/shard_map/ppermute | solution.py:416
  70.6 20.1 %collective-permute-start.16 = (bf16[768,384]{1,0:T(8,128)(2,1)S(1)}, bf16[768,384]{1,0:T(8,128)(2,1)S(1)}, u32[]{:S(2)}, u32[]{:S(2)}) collective-permute-start(bf16[768,384]{1,0:T(8,128)(2,1)S(1)} %get-tuple-element.51.refs_6_), channel_id=1, source_target_pairs={{1,0},{0,1},{3,2},{2,3},{5,4},{4,5},{7,6},{6,7},{9,8},{8,9},{11,10... | collective-permute-start | bytes 1769480 | tf_op jit(solution)/shard_map/ppermute | solution.py:399
  85.8 4.9 %collective-permute-start.20 = (bf16[768,384]{1,0:T(8,128)(2,1)S(1)}, bf16[768,384]{1,0:T(8,128)(2,1)S(1)}, u32[]{:S(2)}, u32[]{:S(2)}) collective-permute-start(bf16[768,384]{1,0:T(8,128)(2,1)S(1)} %collective-permute-done.18.refs_10_), channel_id=1, source_target_pairs={{1,0},{0,1},{3,2},{2,3},{5,4},{4,5},{7,6},{6,7},{9,8},{8,9},{11,10... | collective-permute-start | bytes 1769480 | tf_op jit(solution)/shard_map/ppermute | solution.py:399
  85.8 7.6 %collective-permute-start.27 = (bf16[192,384]{1,0:T(8,128)(2,1)S(1)}, bf16[192,384]{1,0:T(8,128)(2,1)S(1)}, u32[]{:S(2)}, u32[]{:S(2)}) collective-permute-start(bf16[192,384]{1,0:T(8,128)(2,1)S(1)} %collective-permute-done.19.refs_1_), channel_id=1, source_target_pairs={{0,6},{1,7},{2,4},{3,5},{4,2},{5,3},{6,0},{7,1},{8,14},{9,15},{10,... | collective-permute-start | bytes 442376 | tf_op jit(solution)/shard_map/ppermute | solution.py:410
  87.1 9.0 %collective-permute-start.25 = (bf16[192,384]{1,0:T(8,128)(2,1)S(1)}, bf16[192,384]{1,0:T(8,128)(2,1)S(1)}, u32[]{:S(2)}, u32[]{:S(2)}) collective-permute-start(bf16[192,384]{1,0:T(8,128)(2,1)S(1)} %collective-permute-done.19.refs_1_), channel_id=1, source_target_pairs={{0,4},{1,5},{2,6},{3,7},{4,0},{5,1},{6,2},{7,3},{8,12},{9,13},{10,... | collective-permute-start | bytes 442376 | tf_op jit(solution)/shard_map/ppermute | solution.py:410
  90.7 6.2 %collective-permute-start.23 = (bf16[192,384]{1,0:T(8,128)(2,1)S(1)}, bf16[192,384]{1,0:T(8,128)(2,1)S(1)}, u32[]{:S(2)}, u32[]{:S(2)}) collective-permute-start(bf16[192,384]{1,0:T(8,128)(2,1)S(1)} %collective-permute-done.19.refs_1_), channel_id=1, source_target_pairs={{0,2},{1,3},{2,0},{3,1},{4,6},{5,7},{6,4},{7,5},{8,10},{9,11},{10,... | collective-permute-start | bytes 442376 | tf_op jit(solution)/shard_map/ppermute | solution.py:410
  93.5 5.3 %collective-permute-start.28 = (bf16[192,384]{1,0:T(8,128)(2,1)S(1)}, bf16[192,384]{1,0:T(8,128)(2,1)S(1)}, u32[]{:S(2)}, u32[]{:S(2)}) collective-permute-start(bf16[192,384]{1,0:T(8,128)(2,1)S(1)} %collective-permute-done.27.refs_7_), channel_id=1, source_target_pairs={{1,0},{0,1},{3,2},{2,3},{5,4},{4,5},{7,6},{6,7},{9,8},{8,9},{11,10... | collective-permute-start | bytes 442376 | tf_op jit(solution)/shard_map/ppermute | solution.py:399
  96.2 2.6 %collective-permute-start.26 = (bf16[192,384]{1,0:T(8,128)(2,1)S(1)}, bf16[192,384]{1,0:T(8,128)(2,1)S(1)}, u32[]{:S(2)}, u32[]{:S(2)}) collective-permute-start(bf16[192,384]{1,0:T(8,128)(2,1)S(1)} %collective-permute-done.25.refs_5_), channel_id=1, source_target_pairs={{1,0},{0,1},{3,2},{2,3},{5,4},{4,5},{7,6},{6,7},{9,8},{8,9},{11,10... | collective-permute-start | bytes 442376 | tf_op jit(solution)/shard_map/ppermute | solution.py:399
  97.4 11.7 %collective-permute-start.21 = (bf16[192,384]{1,0:T(8,128)(2,1)S(1)}, bf16[192,384]{1,0:T(8,128)(2,1)S(1)}, u32[]{:S(2)}, u32[]{:S(2)}) collective-permute-start(bf16[192,384]{1,0:T(8,128)(2,1)S(1)} %get-tuple-element.58), channel_id=1, source_target_pairs={{16,0},{18,2},{20,4},{22,6},{24,8},{26,10},{28,12},{30,14},{17,1},... | collective-permute-start | bytes 442376 | tf_op jit(solution)/shard_map/ppermute | solution.py:416
  109.1 6.5 %collective-permute-start.30 = (bf16[192,384]{1,0:T(8,128)(2,1)S(1)}, bf16[192,384]{1,0:T(8,128)(2,1)S(1)}, u32[]{:S(2)}, u32[]{:S(2)}) collective-permute-start(bf16[192,384]{1,0:T(8,128)(2,1)S(1)} %collective-permute-done.21.refs_3_), channel_id=1, source_target_pairs={{0,2},{1,3},{2,0},{3,1},{4,6},{5,7},{6,4},{7,5},{8,10},{9,11},{10,... | collective-permute-start | bytes 442376 | tf_op jit(solution)/shard_map/ppermute | solution.py:410
  111.4 8.4 %collective-permute-start.32 = (bf16[192,384]{1,0:T(8,128)(2,1)S(1)}, bf16[192,384]{1,0:T(8,128)(2,1)S(1)}, u32[]{:S(2)}, u32[]{:S(2)}) collective-permute-start(bf16[192,384]{1,0:T(8,128)(2,1)S(1)} %collective-permute-done.21.refs_3_), channel_id=1, source_target_pairs={{0,4},{1,5},{2,6},{3,7},{4,0},{5,1},{6,2},{7,3},{8,12},{9,13},{10,... | collective-permute-start | bytes 442376 | tf_op jit(solution)/shard_map/ppermute | solution.py:410
  112.4 7.4 %collective-permute-start.34 = (bf16[192,384]{1,0:T(8,128)(2,1)S(1)}, bf16[192,384]{1,0:T(8,128)(2,1)S(1)}, u32[]{:S(2)}, u32[]{:S(2)}) collective-permute-start(bf16[192,384]{1,0:T(8,128)(2,1)S(1)} %collective-permute-done.21.refs_3_), channel_id=1, source_target_pairs={{0,6},{1,7},{2,4},{3,5},{4,2},{5,3},{6,0},{7,1},{8,14},{9,15},{10,... | collective-permute-start | bytes 442376 | tf_op jit(solution)/shard_map/ppermute | solution.py:410
  112.9 7.4 %collective-permute-start.29 = (bf16[192,384]{1,0:T(8,128)(2,1)S(1)}, bf16[192,384]{1,0:T(8,128)(2,1)S(1)}, u32[]{:S(2)}, u32[]{:S(2)}) collective-permute-start(bf16[192,384]{1,0:T(8,128)(2,1)S(1)} %collective-permute-done.21.refs_3_), channel_id=1, source_target_pairs={{1,0},{0,1},{3,2},{2,3},{5,4},{4,5},{7,6},{6,7},{9,8},{8,9},{11,10... | collective-permute-start | bytes 442376 | tf_op jit(solution)/shard_map/ppermute | solution.py:399
  115.7 4.6 %collective-permute-start.31 = (bf16[192,384]{1,0:T(8,128)(2,1)S(1)}, bf16[192,384]{1,0:T(8,128)(2,1)S(1)}, u32[]{:S(2)}, u32[]{:S(2)}) collective-permute-start(bf16[192,384]{1,0:T(8,128)(2,1)S(1)} %collective-permute-done.30.refs_5_), channel_id=1, source_target_pairs={{1,0},{0,1},{3,2},{2,3},{5,4},{4,5},{7,6},{6,7},{9,8},{8,9},{11,10... | collective-permute-start | bytes 442376 | tf_op jit(solution)/shard_map/ppermute | solution.py:399
  (6 other events, 15.0 us)
where the time goes:
time: 124 us
  waiting for transfers between devices  70.2 us (57%)
  starting transfers between devices  26.4 us (21%)
  Pallas kernels  24.9 us (20%)
  other arithmetic  1.55 us (1%)
    ppermute x12, waiting for transfers between devices, swap(): return lax.ppermute(value, ('tm', 'panel'), pairs)  40.6 us
    ppermute x4, waiting for transfers between devices, across(): lax.ppermute(x, 'tm', [(t, t ^ d) for t in range(steps) if t ^ d < steps...  28.1 us
    pallas_call x9, Pallas kernels, call(): pl.pallas_call(kernel, in_specs=in_specs, out_specs=[VMEM] * len(outs), o...  24.9 us
    ppermute x12, starting transfers between devices, swap(): return lax.ppermute(value, ('tm', 'panel'), pairs)  18.7 us
    ppermute x4, starting transfers between devices, across(): lax.ppermute(x, 'tm', [(t, t ^ d) for t in range(steps) if t ^ d < steps...  4.72 us
    ppermute x20, starting transfers between devices, over_panels(): lax.ppermute(x, 'panel', [((i + r) % n, i) for i in range(n)])  2.93 us
  transfers between devices with their start and end apart: 36, of which 15 were waited for; matrix products, arithmetic and copies ran while one was open for 0% of the time, Pallas kernels for 18%

commit v1 on v0

--- a/solution.py
+++ b/solution.py
@@ -460,11 +460,10 @@
         [full_scratch, full_scratch, pltpu.VMEM((nb, n * w), F32), sems((n + 1,))],
         2 * one,
     )
-    c_diag = swap(after(c_first, base_bf), 2, 1)
+    c_diag = swap(c_first, 2, 1)
     s_first = swap(base_bf, 1, 2)
-    c_diag = after(c_diag, s_first)
     c_pieces = [p for v in (c_first, c_second, c_diag) for p in over_panels(v)]
-    s_second = swap(after(base_bf, c_second), 2, 1)
+    s_second = swap(base_bf, 2, 1)
     c_all, c01, c23, agg_c = call(
         functools.partial(group_comp_kernel, n),
         c_own + c_pieces,
@@ -484,7 +483,7 @@
         n * one,
     )
     s_diag = swap(s_first, 2, 1)
-    s_own = over_panels(after(base_bf, c_got))
+    s_own = over_panels(base_bf)
     s_pieces = s_own + [p for v in (s_first, s_second, s_diag) for p in over_panels(v)]
     cov, agg, agg_bf = call(
         functools.partial(group_cov_kernel, n),
@@ -504,7 +503,7 @@
         last = bit + 1 == levels
         to_last = bit + 2 == levels
         m = len(c_parts)
-        s_got = across(s_send, bit, last)
+        s_got = s_far if bit else across(after(s_send, c_got), bit, last)
         if last:
             (prop,) = call(
                 functools.partial(last_comp_kernel, n, m, bit),
@@ -514,7 +513,6 @@
                 [],
                 one,
             )
-            s_got = after(s_got, prop)
             s_parts = quarters(s_got) if bit else over_panels(s_got)
             (cov,) = call(
                 functools.partial(last_cov_kernel, n, m, bit),
@@ -555,7 +553,6 @@
         )
         s_got = after(s_got, c_far, new_mine)
         s_parts = quarters(s_got) if bit else over_panels(s_got)
-        c_blocks = in_group(c_far)
         outs = call(
             functools.partial(level_cov_kernel, n, m, bit, to_last),
             [cov, agg, mine, mine_t, agg_c, agg_t, *over_panels(agg_bf), *c_parts, *s_parts],
@@ -568,7 +565,9 @@
         if not to_last:
             agg, agg_bf = outs[2:]
             agg_c, agg_t = new_agg_c, new_agg_t
-        c_parts = [p for b in c_blocks for p in over_panels(after(b, s_send))]
+        s_far = across(s_send, bit + 1, to_last)
+        c_blocks = in_group(after(c_far, s_send))
+        c_parts = [p for b in c_blocks for p in over_panels(after(b, s_far))]
         mine, mine_t = new_mine, new_mine_t
     return cov, prop
 

time: 124 us -> 118 us (0.952)
  waiting for transfers between devices: 70.2 us -> 61.5 us
  starting transfers between devices: 26.4 us -> 29.3 us
    ppermute x12, waiting for transfers between devices: 40.6 us -> 35.2 us  [swap(): return lax.ppermute(value, ('tm', 'panel'), pairs)]
    ppermute x4, waiting for transfers between devices: 28.1 us -> 24 us  [across(): lax.ppermute(x, 'tm', [(t, t ^ d) for t in range(steps) if t ^ d < steps...]
    ppermute x4, starting transfers between devices: 4.72 us -> 6.39 us  [across(): lax.ppermute(x, 'tm', [(t, t ^ d) for t in range(steps) if t ^ d < steps...]
    ppermute x12, starting transfers between devices: 18.7 us -> 20.4 us  [swap(): return lax.ppermute(value, ('tm', 'panel'), pairs)]
  transfers between devices with their start and end apart: 36 -> 36, of which waited for: 15 -> 13; matrix products, arithmetic and copies ran while one was open for 0% -> 0% of each run, Pallas kernels for 18% -> 16%
where the time goes in v1:
time: 118 us
  waiting for transfers between devices  61.5 us (52%)
  starting transfers between devices  29.3 us (25%)
  Pallas kernels  24.6 us (21%)
  other arithmetic  1.55 us (1%)
    ppermute x12, waiting for transfers between devices, swap(): return lax.ppermute(value, ('tm', 'panel'), pairs)  35.2 us
    pallas_call x9, Pallas kernels, call(): pl.pallas_call(kernel, in_specs=in_specs, out_specs=[VMEM] * len(outs), o...  24.6 us
    ppermute x4, waiting for transfers between devices, across(): lax.ppermute(x, 'tm', [(t, t ^ d) for t in range(steps) if t ^ d < steps...  24 us
    ppermute x12, starting transfers between devices, swap(): return lax.ppermute(value, ('tm', 'panel'), pairs)  20.4 us
    ppermute x4, starting transfers between devices, across(): lax.ppermute(x, 'tm', [(t, t ^ d) for t in range(steps) if t ^ d < steps...  6.39 us
    ppermute x20, starting transfers between devices, over_panels(): lax.ppermute(x, 'panel', [((i + r) % n, i) for i in range(n)])  2.48 us
  transfers between devices with their start and end apart: 36, of which 13 were waited for; matrix products, arithmetic and copies ran while one was open for 0% of the time, Pallas kernels for 16%

profile of v1, /device:TPU:0, one launch (start us, length us, event | category | flops | bytes accessed | tf_op | source)
XLA Modules:
  0.0 117.8 jit_solution(7240300336480599736)
XLA Ops:
  0.6 1.5 %convert_bitcast_fusion.refs_4_.refs_0_ = bf16[768,384]{1,0:T(8,128)(2,1)S(1)} fusion(f32[1,768,384]{2,1,0:T(8,128)} %param.4), kind=kLoop, calls=%fused_computation.1 | loop fusion | flops 294912 | bytes 1769472 | tf_op jit(solution)/shard_map/convert_element_type | solution.py:449
  2.1 3.0 %collective-permute-start.2 = (bf16[768,384]{1,0:T(8,128)(2,1)S(1)}, bf16[768,384]{1,0:T(8,128)(2,1)}, u32[]{:S(2)}, u32[]{:S(2)}) collective-permute-start(bf16[768,384]{1,0:T(8,128)(2,1)S(1)} %convert_bitcast_fusion.refs_4_.refs_0_), channel_id=1, source_target_pairs={{0,4},{1,3},{2,6},{3,1},{4,0},{5,7},{6,2},{7,5},{8,12},{9,11},{10,... | collective-permute-start | bytes 1769480 | tf_op jit(solution)/shard_map/ppermute | solution.py:410
  5.8 1.5 %collective-permute-start.4 = (bf16[768,384]{1,0:T(8,128)(2,1)S(1)}, bf16[768,384]{1,0:T(8,128)(2,1)}, u32[]{:S(2)}, u32[]{:S(2)}) collective-permute-start(bf16[768,384]{1,0:T(8,128)(2,1)S(1)} %convert_bitcast_fusion.refs_4_.refs_0_), channel_id=1, source_target_pairs={{0,2},{1,5},{2,0},{3,7},{4,6},{5,1},{6,4},{7,3},{8,10},{9,13},{10,... | collective-permute-start | bytes 1769480 | tf_op jit(solution)/shard_map/ppermute | solution.py:410
  7.3 10.9 %collective-permute-done.2.refs_2_ = bf16[768,384]{1,0:T(8,128)(2,1)} collective-permute-done((bf16[768,384]{1,0:T(8,128)(2,1)S(1)}, bf16[768,384]{1,0:T(8,128)(2,1)}, u32[]{:S(2)}, u32[]{:S(2)}) %collective-permute-start.2) | collective-permute-done | bytes 589856 | tf_op jit(solution)/shard_map/ppermute | solution.py:410
  18.2 1.9 %collective-permute-start.6 = (bf16[768,384]{1,0:T(8,128)(2,1)}, bf16[768,384]{1,0:T(8,128)(2,1)}, u32[]{:S(2)}, u32[]{:S(2)}) collective-permute-start(bf16[768,384]{1,0:T(8,128)(2,1)} %collective-permute-done.2.refs_2_), channel_id=1, source_target_pairs={{0,2},{1,5},{2,0},{3,7},{4,6},{5,1},{6,4},{7,3},{8,10},{9,13},{10,... | collective-permute-start | bytes 1769480 | tf_op jit(solution)/shard_map/ppermute | solution.py:410
  20.1 1.8 %shard_map.50 = (f32[768,384]{1,0:T(8,128)S(1)}, bf16[768,384]{1,0:T(8,128)(2,1)S(1)}) custom-call(f32[768,384]{1,0:T(8,128)S(1)} %bitcast.6, f32[768,768]{1,0:T(8,128)S(1)} %copy-done.1, bf16[768,384]{1,0:T(8,128)(2,1)S(1)} %convert_element_type.10.refs_2_, bf16[768,384]{1,0:T(8,128)(2,1)S(1)} %collective-permute-done.refs_3_, ...), custom_call_target="tpu_custom_call" | custom-call | flops 905969664 | bytes 7667712 | tf_op jit(solution)/shard_map/pallas_call | solution.py:93
  21.9 2.6 %collective-permute-start.9 = (bf16[768,384]{1,0:T(8,128)(2,1)S(1)}, bf16[768,384]{1,0:T(8,128)(2,1)S(1)}, u32[]{:S(2)}, u32[]{:S(2)}) collective-permute-start(bf16[768,384]{1,0:T(8,128)(2,1)S(1)} %get-tuple-element.38.refs_5_), channel_id=1, source_target_pairs={{0,4},{1,3},{2,6},{3,1},{4,0},{5,7},{6,2},{7,5},{8,12},{9,11},{10,... | collective-permute-start | bytes 1769480 | tf_op jit(solution)/shard_map/ppermute | solution.py:410
  25.1 9.5 %collective-permute-done.6.refs_6_ = bf16[768,384]{1,0:T(8,128)(2,1)} collective-permute-done((bf16[768,384]{1,0:T(8,128)(2,1)}, bf16[768,384]{1,0:T(8,128)(2,1)}, u32[]{:S(2)}, u32[]{:S(2)}) %collective-permute-start.6) | collective-permute-done | bytes 589856 | tf_op jit(solution)/shard_map/ppermute | solution.py:410
  34.5 2.0 %collective-permute-start.11 = (bf16[768,384]{1,0:T(8,128)(2,1)S(1)}, bf16[768,384]{1,0:T(8,128)(2,1)}, u32[]{:S(2)}, u32[]{:S(2)}) collective-permute-start(bf16[768,384]{1,0:T(8,128)(2,1)S(1)} %get-tuple-element.38.refs_5_), channel_id=1, source_target_pairs={{0,2},{1,5},{2,0},{3,7},{4,6},{5,1},{6,4},{7,3},{8,10},{9,13},{10,... | collective-permute-start | bytes 1769480 | tf_op jit(solution)/shard_map/ppermute | solution.py:410
  36.9 4.5 %shard_map.51 = (bf16[4,2,768,384]{3,2,1,0:T(8,128)(2,1)S(1)}, bf16[2,768,384]{2,1,0:T(8,128)(2,1)S(1)}, bf16[768,768]{1,0:T(8,128)(2,1)S(1)}, bf16[2,768,384]{2,1,0:T(8,128)(2,1)S(1)}) custom-call(bf16[768,384]{1,0:T(8,128)(2,1)S(1)} %convert_bitcast_fusion.refs_4_.refs_0_, bf16[768,384]{1,0:T(8,128)(2,1)S(1)} %collective-permute-done.1.refs_5_.refs_1_, ...), custom_call_target="tpu_custom_call" | custom-call | flops 2717908992 | bytes 12976128 | tf_op jit(solution)/shard_map/pallas_call | solution.py:93
  41.5 2.0 %collective-permute-start.16 = (bf16[768,384]{1,0:T(8,128)(2,1)S(1)}, bf16[768,384]{1,0:T(8,128)(2,1)S(1)}, u32[]{:S(2)}, u32[]{:S(2)}) collective-permute-start(bf16[768,384]{1,0:T(8,128)(2,1)S(1)} %dynamic-slice_bitcast_fusion), channel_id=1, source_target_pairs={{0,8},{2,10},{4,12},{6,14},{8,0},{10,2},{12,4},{14,6},{16,24},{18,... | collective-permute-start | bytes 1769480 | tf_op jit(solution)/shard_map/ppermute | solution.py:416
  44.5 6.3 %collective-permute-done.13.refs_11_ = bf16[768,384]{1,0:T(8,128)(2,1)} collective-permute-done((bf16[768,384]{1,0:T(8,128)(2,1)S(1)}, bf16[768,384]{1,0:T(8,128)(2,1)}, u32[]{:S(2)}, u32[]{:S(2)}) %collective-permute-start.13) | collective-permute-done | bytes 589856 | tf_op jit(solution)/shard_map/ppermute | solution.py:410
  50.9 1.8 %shard_map.52 = (bf16[3,768,768]{2,1,0:T(8,128)(2,1)S(1)}, bf16[768,768]{1,0:T(8,128)(2,1)S(1)}, bf16[2,768,384]{2,1,0:T(8,128)(2,1)S(1)}, bf16[768,768]{1,0:T(8,128)(2,1)S(1)}, bf16[768,768]{1,0:T(8,128)(2,1)S(1)}) custom-call(bf16[4,2,768,384]{3,2,1,0:T(8,128)(2,1)S(1)} %get-tuple-element.32.c.refs_1_, ...), custom_call_target="tpu_custom_call" | custom-call | flops 905969664 | bytes 16515072 | tf_op jit(solution)/shard_map/pallas_call | solution.py:93
  52.6 4.6 %collective-permute-done.16.refs_1_.refs_2_.refs_8_ = bf16[768,384]{1,0:T(8,128)(2,1)S(1)} collective-permute-done((bf16[768,384]{1,0:T(8,128)(2,1)S(1)}, bf16[768,384]{1,0:T(8,128)(2,1)S(1)}, u32[]{:S(2)}, u32[]{:S(2)}) %collective-permute-start.16) | collective-permute-done | bytes 589856 | tf_op jit(solution)/shard_map/ppermute | solution.py:416
  57.2 6.8 %shard_map.53 = (f32[768,384]{1,0:T(8,128)S(1)}, f32[768,384]{1,0:T(8,128)S(1)}, bf16[768,384]{1,0:T(8,128)(2,1)S(1)}) custom-call(f32[768,384]{1,0:T(8,128)S(1)} %get-tuple-element.31.refs_0_, bf16[4,2,768,384]{3,2,1,0:T(8,128)(2,1)S(1)} %get-tuple-element.32.c.refs_1_, bf16[3,768,768]{2,1,0:T(8,128)(2,1)S(1)} %get-tuple-element.36.refs_2_, ...), custom_call_target="tpu_custom_call" | custom-call | flops 4529848320 | bytes 19464192 | tf_op jit(solution)/shard_map/pallas_call | solution.py:93
  64.0 1.8 %collective-permute-start.18 = (bf16[768,384]{1,0:T(8,128)(2,1)S(1)}, bf16[768,384]{1,0:T(8,128)(2,1)S(1)}, u32[]{:S(2)}, u32[]{:S(2)}) collective-permute-start(bf16[768,384]{1,0:T(8,128)(2,1)S(1)} %get-tuple-element.45.refs_6_), channel_id=1, source_target_pairs={{0,8},{2,10},{4,12},{6,14},{8,0},{10,2},{12,4},{14,6},{16,24},{18,... | collective-permute-start | bytes 1769480 | tf_op jit(solution)/shard_map/ppermute | solution.py:416
  66.7 1.3 %collective-permute-start.19 = (bf16[192,384]{1,0:T(8,128)(2,1)S(1)}, bf16[192,384]{1,0:T(8,128)(2,1)S(1)}, u32[]{:S(2)}, u32[]{:S(2)}) collective-permute-start(bf16[192,384]{1,0:T(8,128)(2,1)S(1)} %shard_map.54), channel_id=1, source_target_pairs={{16,0},{18,2},{20,4},{22,6},{24,8},{26,10},{28,12},{30,14},{17,1},... | collective-permute-start | bytes 442376 | tf_op jit(solution)/shard_map/ppermute | solution.py:416
  68.3 1.8 %shard_map.55 = (bf16[2,768,384]{2,1,0:T(8,128)(2,1)S(1)}, bf16[768,768]{1,0:T(8,128)(2,1)S(1)}) custom-call(bf16[2,768,384]{2,1,0:T(8,128)(2,1)S(1)} %get-tuple-element.47.refs_0_.refs_2_, bf16[768,768]{1,0:T(8,128)(2,1)S(1)} %get-tuple-element.42.refs_1_.refs_3_, bf16[768,384]{1,0:T(8,128)(2,1)S(1)} %collective-permute-done.16.refs_1_.refs_2_.refs_8_, ...), custom_call_target="tpu_custom_call" | custom-call | flops 905969664 | bytes 5898240 | tf_op jit(solution)/shard_map/pallas_call | solution.py:93
  70.1 12.9 %collective-permute-done.18.refs_10_ = bf16[768,384]{1,0:T(8,128)(2,1)S(1)} collective-permute-done((bf16[768,384]{1,0:T(8,128)(2,1)S(1)}, bf16[768,384]{1,0:T(8,128)(2,1)S(1)}, u32[]{:S(2)}, u32[]{:S(2)}) %collective-permute-start.18) | collective-permute-done | bytes 589856 | tf_op jit(solution)/shard_map/ppermute | solution.py:416
  83.0 2.0 %collective-permute-done.20.refs_11_ = bf16[768,384]{1,0:T(8,128)(2,1)S(1)} collective-permute-done((bf16[768,384]{1,0:T(8,128)(2,1)S(1)}, bf16[768,384]{1,0:T(8,128)(2,1)S(1)}, u32[]{:S(2)}, u32[]{:S(2)}) %collective-permute-start.20) | collective-permute-done | bytes 589856 | tf_op jit(solution)/shard_map/ppermute | solution.py:399
  85.0 2.7 %shard_map.56 = (f32[768,384]{1,0:T(8,128)S(1)}, bf16[192,384]{1,0:T(8,128)(2,1)S(1)}) custom-call(f32[768,384]{1,0:T(8,128)S(1)} %get-tuple-element.39.refs_0_, f32[768,384]{1,0:T(8,128)S(1)} %get-tuple-element.40.refs_1_, bf16[2,768,384]{2,1,0:T(8,128)(2,1)S(1)} %get-tuple-element.47.refs_0_.refs_2_, ...), custom_call_target="tpu_custom_call" | custom-call | flops 1811939328 | bytes 11943936 | tf_op jit(solution)/shard_map/pallas_call | solution.py:93
  87.7 1.8 %collective-permute-start.34 = (bf16[192,384]{1,0:T(8,128)(2,1)S(1)}, bf16[192,384]{1,0:T(8,128)(2,1)S(1)}, u32[]{:S(2)}, u32[]{:S(2)}) collective-permute-start(bf16[192,384]{1,0:T(8,128)(2,1)S(1)} %collective-permute-done.19.refs_1_), channel_id=1, source_target_pairs={{0,6},{1,7},{2,4},{3,5},{4,2},{5,3},{6,0},{7,1},{8,14},{9,15},{10,... | collective-permute-start | bytes 442376 | tf_op jit(solution)/shard_map/ppermute | solution.py:410
  89.5 1.3 %collective-permute-start.21 = (bf16[192,384]{1,0:T(8,128)(2,1)S(1)}, bf16[192,384]{1,0:T(8,128)(2,1)S(1)}, u32[]{:S(2)}, u32[]{:S(2)}) collective-permute-start(bf16[192,384]{1,0:T(8,128)(2,1)S(1)} %get-tuple-element.52), channel_id=1, source_target_pairs={{16,0},{18,2},{20,4},{22,6},{24,8},{26,10},{28,12},{30,14},{17,1},... | collective-permute-start | bytes 442376 | tf_op jit(solution)/shard_map/ppermute | solution.py:416
  90.8 3.0 %collective-permute-start.32 = (bf16[192,384]{1,0:T(8,128)(2,1)S(1)}, bf16[192,384]{1,0:T(8,128)(2,1)S(1)}, u32[]{:S(2)}, u32[]{:S(2)}) collective-permute-start(bf16[192,384]{1,0:T(8,128)(2,1)S(1)} %collective-permute-done.19.refs_1_), channel_id=1, source_target_pairs={{0,4},{1,5},{2,6},{3,7},{4,0},{5,1},{6,2},{7,3},{8,12},{9,13},{10,... | collective-permute-start | bytes 442376 | tf_op jit(solution)/shard_map/ppermute | solution.py:410
  94.6 6.5 %collective-permute-done.21.refs_3_ = bf16[192,384]{1,0:T(8,128)(2,1)S(1)} collective-permute-done((bf16[192,384]{1,0:T(8,128)(2,1)S(1)}, bf16[192,384]{1,0:T(8,128)(2,1)S(1)}, u32[]{:S(2)}, u32[]{:S(2)}) %collective-permute-start.21) | collective-permute-done | bytes 147488 | tf_op jit(solution)/shard_map/ppermute | solution.py:416
  101.6 1.8 %collective-permute-start.23 = (bf16[192,384]{1,0:T(8,128)(2,1)S(1)}, bf16[192,384]{1,0:T(8,128)(2,1)S(1)}, u32[]{:S(2)}, u32[]{:S(2)}) collective-permute-start(bf16[192,384]{1,0:T(8,128)(2,1)S(1)} %collective-permute-done.21.refs_3_), channel_id=1, source_target_pairs={{0,2},{1,3},{2,0},{3,1},{4,6},{5,7},{6,4},{7,5},{8,10},{9,11},{10,... | collective-permute-start | bytes 442376 | tf_op jit(solution)/shard_map/ppermute | solution.py:410
  104.6 1.5 %collective-permute-start.27 = (bf16[192,384]{1,0:T(8,128)(2,1)S(1)}, bf16[192,384]{1,0:T(8,128)(2,1)S(1)}, u32[]{:S(2)}, u32[]{:S(2)}) collective-permute-start(bf16[192,384]{1,0:T(8,128)(2,1)S(1)} %collective-permute-done.21.refs_3_), channel_id=1, source_target_pairs={{0,6},{1,7},{2,4},{3,5},{4,2},{5,3},{6,0},{7,1},{8,14},{9,15},{10,... | collective-permute-start | bytes 442376 | tf_op jit(solution)/shard_map/ppermute | solution.py:410
  106.6 1.6 %collective-permute-done.23.refs_5_ = bf16[192,384]{1,0:T(8,128)(2,1)S(1)} collective-permute-done((bf16[192,384]{1,0:T(8,128)(2,1)S(1)}, bf16[192,384]{1,0:T(8,128)(2,1)S(1)}, u32[]{:S(2)}, u32[]{:S(2)}) %collective-permute-start.23) | collective-permute-done | bytes 147488 | tf_op jit(solution)/shard_map/ppermute | solution.py:410
  108.2 3.3 %collective-permute-done.25.refs_7_ = bf16[192,384]{1,0:T(8,128)(2,1)S(1)} collective-permute-done((bf16[192,384]{1,0:T(8,128)(2,1)S(1)}, bf16[192,384]{1,0:T(8,128)(2,1)S(1)}, u32[]{:S(2)}, u32[]{:S(2)}) %collective-permute-start.25) | collective-permute-done | bytes 147488 | tf_op jit(solution)/shard_map/ppermute | solution.py:410
  111.5 1.9 %collective-permute-done.27.refs_9_ = bf16[192,384]{1,0:T(8,128)(2,1)S(1)} collective-permute-done((bf16[192,384]{1,0:T(8,128)(2,1)S(1)}, bf16[192,384]{1,0:T(8,128)(2,1)S(1)}, u32[]{:S(2)}, u32[]{:S(2)}) %collective-permute-start.27) | collective-permute-done | bytes 147488 | tf_op jit(solution)/shard_map/ppermute | solution.py:410
  113.4 1.7 %shard_map.58 = bf16[1,768,384]{2,1,0:T(8,128)(2,1)} custom-call(bf16[2,768,384]{2,1,0:T(8,128)(2,1)S(1)} %get-tuple-element.48.refs_1_.refs_0_, bf16[192,384]{1,0:T(8,128)(2,1)S(1)} %collective-permute-done.19.refs_1_, bf16[192,384]{1,0:T(8,128)(2,1)S(1)} %collective-permute-done.29.refs_2_, bf16[192,384]{1,0:T(8,128)(2,1)S(1)} %collective-permute-done.30.refs_3_, ...), custom_call_target="tpu_custom_call" | custom-call | flops 452984832 | bytes 2949120 | tf_op jit(solution)/shard_map/pallas_call | solution.py:93
  115.1 2.7 %shard_map.57 = f32[1,768,384]{2,1,0:T(8,128)} custom-call(f32[768,384]{1,0:T(8,128)S(1)} %get-tuple-element.50.refs_0_, bf16[2,768,384]{2,1,0:T(8,128)(2,1)S(1)} %get-tuple-element.48.refs_1_.refs_0_, bf16[768,768]{1,0:T(8,128)(2,1)S(1)} %get-tuple-element.51.refs_2_, bf16[192,384]{1,0:T(8,128)(2,1)S(1)} %collective-permute-done.21.refs_3_, ...), custom_call_target="tpu_custom_call" | custom-call | flops 905969664 | bytes 5898240 | tf_op jit(solution)/shard_map/pallas_call | solution.py:93
  (56 shorter events, 6.8 us)
Async XLA Ops:
  2.1 16.1 %collective-permute-start.2 = (bf16[768,384]{1,0:T(8,128)(2,1)S(1)}, bf16[768,384]{1,0:T(8,128)(2,1)}, u32[]{:S(2)}, u32[]{:S(2)}) collective-permute-start(bf16[768,384]{1,0:T(8,128)(2,1)S(1)} %convert_bitcast_fusion.refs_4_.refs_0_), channel_id=1, source_target_pairs={{0,4},{1,3},{2,6},{3,1},{4,0},{5,7},{6,2},{7,5},{8,12},{9,11},{10,... | collective-permute-start | bytes 1769480 | tf_op jit(solution)/shard_map/ppermute | solution.py:410
  5.2 15.0 %collective-permute-start.1 = (bf16[768,384]{1,0:T(8,128)(2,1)S(1)}, bf16[768,384]{1,0:T(8,128)(2,1)S(1)}, u32[]{:S(2)}, u32[]{:S(2)}) collective-permute-start(bf16[768,384]{1,0:T(8,128)(2,1)S(1)} %convert_bitcast_fusion.refs_4_.refs_0_), channel_id=1, source_target_pairs={{1,0},{0,1},{3,2},{2,3},{5,4},{4,5},{7,6},{6,7},{9,8},{8,9},{11,10... | collective-permute-start | bytes 1769480 | tf_op jit(solution)/shard_map/ppermute | solution.py:399
  5.2 14.9 %collective-permute-start = (bf16[768,384]{1,0:T(8,128)(2,1)S(1)}, bf16[768,384]{1,0:T(8,128)(2,1)S(1)}, u32[]{:S(2)}, u32[]{:S(2)}) collective-permute-start(bf16[768,384]{1,0:T(8,128)(2,1)S(1)} %convert_element_type.10.refs_2_), channel_id=1, source_target_pairs={{1,0},{0,1},{3,2},{2,3},{5,4},{4,5},{7,6},{6,7},{9,8},{8,9},{11,10... | collective-permute-start | bytes 1769480 | tf_op jit(solution)/shard_map/ppermute | solution.py:399
  5.8 18.7 %collective-permute-start.4 = (bf16[768,384]{1,0:T(8,128)(2,1)S(1)}, bf16[768,384]{1,0:T(8,128)(2,1)}, u32[]{:S(2)}, u32[]{:S(2)}) collective-permute-start(bf16[768,384]{1,0:T(8,128)(2,1)S(1)} %convert_bitcast_fusion.refs_4_.refs_0_), channel_id=1, source_target_pairs={{0,2},{1,5},{2,0},{3,7},{4,6},{5,1},{6,4},{7,3},{8,10},{9,13},{10,... | collective-permute-start | bytes 1769480 | tf_op jit(solution)/shard_map/ppermute | solution.py:410
  18.2 16.3 %collective-permute-start.6 = (bf16[768,384]{1,0:T(8,128)(2,1)}, bf16[768,384]{1,0:T(8,128)(2,1)}, u32[]{:S(2)}, u32[]{:S(2)}) collective-permute-start(bf16[768,384]{1,0:T(8,128)(2,1)} %collective-permute-done.2.refs_2_), channel_id=1, source_target_pairs={{0,2},{1,5},{2,0},{3,7},{4,6},{5,1},{6,4},{7,3},{8,10},{9,13},{10,... | collective-permute-start | bytes 1769480 | tf_op jit(solution)/shard_map/ppermute | solution.py:410
  21.9 14.6 %collective-permute-start.9 = (bf16[768,384]{1,0:T(8,128)(2,1)S(1)}, bf16[768,384]{1,0:T(8,128)(2,1)S(1)}, u32[]{:S(2)}, u32[]{:S(2)}) collective-permute-start(bf16[768,384]{1,0:T(8,128)(2,1)S(1)} %get-tuple-element.38.refs_5_), channel_id=1, source_target_pairs={{0,4},{1,3},{2,6},{3,1},{4,0},{5,7},{6,2},{7,5},{8,12},{9,11},{10,... | collective-permute-start | bytes 1769480 | tf_op jit(solution)/shard_map/ppermute | solution.py:410
  24.6 12.0 %collective-permute-start.3 = (bf16[768,384]{1,0:T(8,128)(2,1)}, bf16[768,384]{1,0:T(8,128)(2,1)}, u32[]{:S(2)}, u32[]{:S(2)}) collective-permute-start(bf16[768,384]{1,0:T(8,128)(2,1)} %collective-permute-done.2.refs_2_), channel_id=1, source_target_pairs={{1,0},{0,1},{3,2},{2,3},{5,4},{4,5},{7,6},{6,7},{9,8},{8,9},{11,10... | collective-permute-start | bytes 1769480 | tf_op jit(solution)/shard_map/ppermute | solution.py:399
  24.6 12.0 %collective-permute-start.5 = (bf16[768,384]{1,0:T(8,128)(2,1)}, bf16[768,384]{1,0:T(8,128)(2,1)}, u32[]{:S(2)}, u32[]{:S(2)}) collective-permute-start(bf16[768,384]{1,0:T(8,128)(2,1)} %collective-permute-done.4.refs_4_), channel_id=1, source_target_pairs={{1,0},{0,1},{3,2},{2,3},{5,4},{4,5},{7,6},{6,7},{9,8},{8,9},{11,10... | collective-permute-start | bytes 1769480 | tf_op jit(solution)/shard_map/ppermute | solution.py:399
  34.5 10.0 %collective-permute-start.11 = (bf16[768,384]{1,0:T(8,128)(2,1)S(1)}, bf16[768,384]{1,0:T(8,128)(2,1)}, u32[]{:S(2)}, u32[]{:S(2)}) collective-permute-start(bf16[768,384]{1,0:T(8,128)(2,1)S(1)} %get-tuple-element.38.refs_5_), channel_id=1, source_target_pairs={{0,2},{1,5},{2,0},{3,7},{4,6},{5,1},{6,4},{7,3},{8,10},{9,13},{10,... | collective-permute-start | bytes 1769480 | tf_op jit(solution)/shard_map/ppermute | solution.py:410
  36.5 14.3 %collective-permute-start.13 = (bf16[768,384]{1,0:T(8,128)(2,1)S(1)}, bf16[768,384]{1,0:T(8,128)(2,1)}, u32[]{:S(2)}, u32[]{:S(2)}) collective-permute-start(bf16[768,384]{1,0:T(8,128)(2,1)S(1)} %collective-permute-done.9.refs_7_), channel_id=1, source_target_pairs={{0,2},{1,5},{2,0},{3,7},{4,6},{5,1},{6,4},{7,3},{8,10},{9,13},{10,... | collective-permute-start | bytes 1769480 | tf_op jit(solution)/shard_map/ppermute | solution.py:410
  36.6 20.6 %collective-permute-start.8 = (bf16[768,384]{1,0:T(8,128)(2,1)S(1)}, bf16[768,384]{1,0:T(8,128)(2,1)S(1)}, u32[]{:S(2)}, u32[]{:S(2)}) collective-permute-start(bf16[768,384]{1,0:T(8,128)(2,1)S(1)} %get-tuple-element.38.refs_5_), channel_id=1, source_target_pairs={{1,0},{0,1},{3,2},{2,3},{5,4},{4,5},{7,6},{6,7},{9,8},{8,9},{11,10... | collective-permute-start | bytes 1769480 | tf_op jit(solution)/shard_map/ppermute | solution.py:399
  41.5 15.7 %collective-permute-start.16 = (bf16[768,384]{1,0:T(8,128)(2,1)S(1)}, bf16[768,384]{1,0:T(8,128)(2,1)S(1)}, u32[]{:S(2)}, u32[]{:S(2)}) collective-permute-start(bf16[768,384]{1,0:T(8,128)(2,1)S(1)} %dynamic-slice_bitcast_fusion), channel_id=1, source_target_pairs={{0,8},{2,10},{4,12},{6,14},{8,0},{10,2},{12,4},{14,6},{16,24},{18,... | collective-permute-start | bytes 1769480 | tf_op jit(solution)/shard_map/ppermute | solution.py:416
  43.5 13.7 %collective-permute-start.10 = (bf16[768,384]{1,0:T(8,128)(2,1)S(1)}, bf16[768,384]{1,0:T(8,128)(2,1)S(1)}, u32[]{:S(2)}, u32[]{:S(2)}) collective-permute-start(bf16[768,384]{1,0:T(8,128)(2,1)S(1)} %collective-permute-done.9.refs_7_), channel_id=1, source_target_pairs={{1,0},{0,1},{3,2},{2,3},{5,4},{4,5},{7,6},{6,7},{9,8},{8,9},{11,10... | collective-permute-start | bytes 1769480 | tf_op jit(solution)/shard_map/ppermute | solution.py:399
  44.5 12.7 %collective-permute-start.12 = (bf16[768,384]{1,0:T(8,128)(2,1)}, bf16[768,384]{1,0:T(8,128)(2,1)S(1)}, u32[]{:S(2)}, u32[]{:S(2)}) collective-permute-start(bf16[768,384]{1,0:T(8,128)(2,1)} %collective-permute-done.11.refs_9_), channel_id=1, source_target_pairs={{1,0},{0,1},{3,2},{2,3},{5,4},{4,5},{7,6},{6,7},{9,8},{8,9},{11,10... | collective-permute-start | bytes 1769480 | tf_op jit(solution)/shard_map/ppermute | solution.py:399
  50.8 6.4 %collective-permute-start.14 = (bf16[768,384]{1,0:T(8,128)(2,1)}, bf16[768,384]{1,0:T(8,128)(2,1)S(1)}, u32[]{:S(2)}, u32[]{:S(2)}) collective-permute-start(bf16[768,384]{1,0:T(8,128)(2,1)} %collective-permute-done.13.refs_11_), channel_id=1, source_target_pairs={{1,0},{0,1},{3,2},{2,3},{5,4},{4,5},{7,6},{6,7},{9,8},{8,9},{11,10... | collective-permute-start | bytes 1769480 | tf_op jit(solution)/shard_map/ppermute | solution.py:399
  57.2 8.6 %collective-permute-start.17 = (bf16[768,384]{1,0:T(8,128)(2,1)S(1)}, bf16[768,384]{1,0:T(8,128)(2,1)S(1)}, u32[]{:S(2)}, u32[]{:S(2)}) collective-permute-start(bf16[768,384]{1,0:T(8,128)(2,1)S(1)} %collective-permute-done.16.refs_1_.refs_2_.refs_8_), channel_id=1, source_target_pairs={{1,0},{0,1},{3,2},{2,3},{5,4},{4,5},{7,6},{6,7},{9,8},{8,9},{11,10... | collective-permute-start | bytes 1769480 | tf_op jit(solution)/shard_map/ppermute | solution.py:399
  64.0 19.0 %collective-permute-start.18 = (bf16[768,384]{1,0:T(8,128)(2,1)S(1)}, bf16[768,384]{1,0:T(8,128)(2,1)S(1)}, u32[]{:S(2)}, u32[]{:S(2)}) collective-permute-start(bf16[768,384]{1,0:T(8,128)(2,1)S(1)} %get-tuple-element.45.refs_6_), channel_id=1, source_target_pairs={{0,8},{2,10},{4,12},{6,14},{8,0},{10,2},{12,4},{14,6},{16,24},{18,... | collective-permute-start | bytes 1769480 | tf_op jit(solution)/shard_map/ppermute | solution.py:416
  66.7 16.3 %collective-permute-start.19 = (bf16[192,384]{1,0:T(8,128)(2,1)S(1)}, bf16[192,384]{1,0:T(8,128)(2,1)S(1)}, u32[]{:S(2)}, u32[]{:S(2)}) collective-permute-start(bf16[192,384]{1,0:T(8,128)(2,1)S(1)} %shard_map.54), channel_id=1, source_target_pairs={{16,0},{18,2},{20,4},{22,6},{24,8},{26,10},{28,12},{30,14},{17,1},... | collective-permute-start | bytes 442376 | tf_op jit(solution)/shard_map/ppermute | solution.py:416
  68.0 15.0 %collective-permute-start.15 = (bf16[768,384]{1,0:T(8,128)(2,1)S(1)}, bf16[768,384]{1,0:T(8,128)(2,1)S(1)}, u32[]{:S(2)}, u32[]{:S(2)}) collective-permute-start(bf16[768,384]{1,0:T(8,128)(2,1)S(1)} %get-tuple-element.45.refs_6_), channel_id=1, source_target_pairs={{1,0},{0,1},{3,2},{2,3},{5,4},{4,5},{7,6},{6,7},{9,8},{8,9},{11,10... | collective-permute-start | bytes 1769480 | tf_op jit(solution)/shard_map/ppermute | solution.py:399
  87.7 6.9 %collective-permute-start.34 = (bf16[192,384]{1,0:T(8,128)(2,1)S(1)}, bf16[192,384]{1,0:T(8,128)(2,1)S(1)}, u32[]{:S(2)}, u32[]{:S(2)}) collective-permute-start(bf16[192,384]{1,0:T(8,128)(2,1)S(1)} %collective-permute-done.19.refs_1_), channel_id=1, source_target_pairs={{0,6},{1,7},{2,4},{3,5},{4,2},{5,3},{6,0},{7,1},{8,14},{9,15},{10,... | collective-permute-start | bytes 442376 | tf_op jit(solution)/shard_map/ppermute | solution.py:410
  89.5 11.6 %collective-permute-start.21 = (bf16[192,384]{1,0:T(8,128)(2,1)S(1)}, bf16[192,384]{1,0:T(8,128)(2,1)S(1)}, u32[]{:S(2)}, u32[]{:S(2)}) collective-permute-start(bf16[192,384]{1,0:T(8,128)(2,1)S(1)} %get-tuple-element.52), channel_id=1, source_target_pairs={{16,0},{18,2},{20,4},{22,6},{24,8},{26,10},{28,12},{30,14},{17,1},... | collective-permute-start | bytes 442376 | tf_op jit(solution)/shard_map/ppermute | solution.py:416
  90.8 10.3 %collective-permute-start.32 = (bf16[192,384]{1,0:T(8,128)(2,1)S(1)}, bf16[192,384]{1,0:T(8,128)(2,1)S(1)}, u32[]{:S(2)}, u32[]{:S(2)}) collective-permute-start(bf16[192,384]{1,0:T(8,128)(2,1)S(1)} %collective-permute-done.19.refs_1_), channel_id=1, source_target_pairs={{0,4},{1,5},{2,6},{3,7},{4,0},{5,1},{6,2},{7,3},{8,12},{9,13},{10,... | collective-permute-start | bytes 442376 | tf_op jit(solution)/shard_map/ppermute | solution.py:410
  93.8 7.7 %collective-permute-start.30 = (bf16[192,384]{1,0:T(8,128)(2,1)S(1)}, bf16[192,384]{1,0:T(8,128)(2,1)S(1)}, u32[]{:S(2)}, u32[]{:S(2)}) collective-permute-start(bf16[192,384]{1,0:T(8,128)(2,1)S(1)} %collective-permute-done.19.refs_1_), channel_id=1, source_target_pairs={{0,2},{1,3},{2,0},{3,1},{4,6},{5,7},{6,4},{7,5},{8,10},{9,11},{10,... | collective-permute-start | bytes 442376 | tf_op jit(solution)/shard_map/ppermute | solution.py:410
  101.1 5.0 %collective-permute-start.33 = (bf16[192,384]{1,0:T(8,128)(2,1)S(1)}, bf16[192,384]{1,0:T(8,128)(2,1)S(1)}, u32[]{:S(2)}, u32[]{:S(2)}) collective-permute-start(bf16[192,384]{1,0:T(8,128)(2,1)S(1)} %collective-permute-done.32.refs_5_), channel_id=1, source_target_pairs={{1,0},{0,1},{3,2},{2,3},{5,4},{4,5},{7,6},{6,7},{9,8},{8,9},{11,10... | collective-permute-start | bytes 442376 | tf_op jit(solution)/shard_map/ppermute | solution.py:399
  101.6 4.5 %collective-permute-start.31 = (bf16[192,384]{1,0:T(8,128)(2,1)S(1)}, bf16[192,384]{1,0:T(8,128)(2,1)S(1)}, u32[]{:S(2)}, u32[]{:S(2)}) collective-permute-start(bf16[192,384]{1,0:T(8,128)(2,1)S(1)} %collective-permute-done.30.refs_3_), channel_id=1, source_target_pairs={{1,0},{0,1},{3,2},{2,3},{5,4},{4,5},{7,6},{6,7},{9,8},{8,9},{11,10... | collective-permute-start | bytes 442376 | tf_op jit(solution)/shard_map/ppermute | solution.py:399
  101.6 6.5 %collective-permute-start.23 = (bf16[192,384]{1,0:T(8,128)(2,1)S(1)}, bf16[192,384]{1,0:T(8,128)(2,1)S(1)}, u32[]{:S(2)}, u32[]{:S(2)}) collective-permute-start(bf16[192,384]{1,0:T(8,128)(2,1)S(1)} %collective-permute-done.21.refs_3_), channel_id=1, source_target_pairs={{0,2},{1,3},{2,0},{3,1},{4,6},{5,7},{6,4},{7,5},{8,10},{9,11},{10,... | collective-permute-start | bytes 442376 | tf_op jit(solution)/shard_map/ppermute | solution.py:410
  103.5 8.0 %collective-permute-start.25 = (bf16[192,384]{1,0:T(8,128)(2,1)S(1)}, bf16[192,384]{1,0:T(8,128)(2,1)S(1)}, u32[]{:S(2)}, u32[]{:S(2)}) collective-permute-start(bf16[192,384]{1,0:T(8,128)(2,1)S(1)} %collective-permute-done.21.refs_3_), channel_id=1, source_target_pairs={{0,4},{1,5},{2,6},{3,7},{4,0},{5,1},{6,2},{7,3},{8,12},{9,13},{10,... | collective-permute-start | bytes 442376 | tf_op jit(solution)/shard_map/ppermute | solution.py:410
  104.6 8.8 %collective-permute-start.27 = (bf16[192,384]{1,0:T(8,128)(2,1)S(1)}, bf16[192,384]{1,0:T(8,128)(2,1)S(1)}, u32[]{:S(2)}, u32[]{:S(2)}) collective-permute-start(bf16[192,384]{1,0:T(8,128)(2,1)S(1)} %collective-permute-done.21.refs_3_), channel_id=1, source_target_pairs={{0,6},{1,7},{2,4},{3,5},{4,2},{5,3},{6,0},{7,1},{8,14},{9,15},{10,... | collective-permute-start | bytes 442376 | tf_op jit(solution)/shard_map/ppermute | solution.py:410
  106.1 7.3 %collective-permute-start.29 = (bf16[192,384]{1,0:T(8,128)(2,1)S(1)}, bf16[192,384]{1,0:T(8,128)(2,1)S(1)}, u32[]{:S(2)}, u32[]{:S(2)}) collective-permute-start(bf16[192,384]{1,0:T(8,128)(2,1)S(1)} %collective-permute-done.19.refs_1_), channel_id=1, source_target_pairs={{1,0},{0,1},{3,2},{2,3},{5,4},{4,5},{7,6},{6,7},{9,8},{8,9},{11,10... | collective-permute-start | bytes 442376 | tf_op jit(solution)/shard_map/ppermute | solution.py:399
  106.1 9.0 %collective-permute-start.22 = (bf16[192,384]{1,0:T(8,128)(2,1)S(1)}, bf16[192,384]{1,0:T(8,128)(2,1)S(1)}, u32[]{:S(2)}, u32[]{:S(2)}) collective-permute-start(bf16[192,384]{1,0:T(8,128)(2,1)S(1)} %collective-permute-done.21.refs_3_), channel_id=1, source_target_pairs={{1,0},{0,1},{3,2},{2,3},{5,4},{4,5},{7,6},{6,7},{9,8},{8,9},{11,10... | collective-permute-start | bytes 442376 | tf_op jit(solution)/shard_map/ppermute | solution.py:399
  108.2 6.9 %collective-permute-start.24 = (bf16[192,384]{1,0:T(8,128)(2,1)S(1)}, bf16[192,384]{1,0:T(8,128)(2,1)S(1)}, u32[]{:S(2)}, u32[]{:S(2)}) collective-permute-start(bf16[192,384]{1,0:T(8,128)(2,1)S(1)} %collective-permute-done.23.refs_5_), channel_id=1, source_target_pairs={{1,0},{0,1},{3,2},{2,3},{5,4},{4,5},{7,6},{6,7},{9,8},{8,9},{11,10... | collective-permute-start | bytes 442376 | tf_op jit(solution)/shard_map/ppermute | solution.py:399
  111.5 3.6 %collective-permute-start.26 = (bf16[192,384]{1,0:T(8,128)(2,1)S(1)}, bf16[192,384]{1,0:T(8,128)(2,1)S(1)}, u32[]{:S(2)}, u32[]{:S(2)}) collective-permute-start(bf16[192,384]{1,0:T(8,128)(2,1)S(1)} %collective-permute-done.25.refs_7_), channel_id=1, source_target_pairs={{1,0},{0,1},{3,2},{2,3},{5,4},{4,5},{7,6},{6,7},{9,8},{8,9},{11,10... | collective-permute-start | bytes 442376 | tf_op jit(solution)/shard_map/ppermute | solution.py:399
  (6 other events, 33.7 us)

commit v2 on v1

--- a/solution.py
+++ b/solution.py
@@ -10,6 +10,7 @@
 BF = jnp.bfloat16
 F32 = jnp.float32
 GROUP = 4
+BLOCK = 128
 ANY = pl.BlockSpec(memory_space=pl.ANY)
 VMEM = pl.BlockSpec(memory_space=pltpu.VMEM)
 MIB = 1 << 20
@@ -76,6 +77,86 @@
     for slot in slots:
         for p in range(len(own)):
             pltpu.make_async_copy(own[p], dst.at[slot, p], sems.at[slot, p]).wait()
+
+
+def packs(n, w):
+    return n == 2 and w % BLOCK == 0
+
+
+def packed_shape(n, nb, w):
+    if not packs(n, w):
+        return nb, w
+    k = w // BLOCK
+    return (k * (k + 1) // 2 + (k * k + 1) // 2) * BLOCK, BLOCK
+
+
+def triangle(k):
+    return [(i, j) for i in range(k) for j in range(i + 1)]
+
+
+def halves(k):
+    every = [(a, b) for a in range(k) for b in range(k)]
+    half = (k * k + 1) // 2
+    return every[:half], every[k * k - half :]
+
+
+def pack(panel, out, q, n):
+    nb, w = panel.shape
+    if not packs(n, w):
+        out[...] = panel[...].astype(BF)
+        return
+    k = w // BLOCK
+    at = 0
+    for i, j in triangle(k):
+        rows = pl.ds(pl.multiple_of(q * w + i * BLOCK, BLOCK), BLOCK)
+        out[at : at + BLOCK, :] = panel[rows, j * BLOCK : (j + 1) * BLOCK].astype(BF)
+        at += BLOCK
+    for side, blocks in enumerate(halves(k)):
+
+        @pl.when(q == side)
+        def _():
+            to = at
+            for a, b in blocks:
+                i, j = (b, a) if side else (w // BLOCK + a, b)
+                value = panel[i * BLOCK : (i + 1) * BLOCK, j * BLOCK : (j + 1) * BLOCK]
+                out[to : to + BLOCK, :] = value.astype(BF)
+                to += BLOCK
+
+
+def unpack(src, dst, n):
+    nb = dst.shape[0]
+    w = nb // n
+    if not packs(n, w):
+        dst[...] = whole(src)
+        return
+    k = w // BLOCK
+
+    def both(block, i, j):
+        dst[i * BLOCK : (i + 1) * BLOCK, j * BLOCK : (j + 1) * BLOCK] = block
+        if i != j:
+            dst[j * BLOCK : (j + 1) * BLOCK, i * BLOCK : (i + 1) * BLOCK] = block.T
+
+    seen = set()
+    for p in range(n):
+        at = 0
+        for i, j in triangle(k):
+            both(src[p, at : at + BLOCK, :], p * k + i, p * k + j)
+            at += BLOCK
+        for a, b in halves(k)[p]:
+            if (a, b) not in seen:
+                i, j = (b, k + a) if p else (k + a, b)
+                both(src[p, at : at + BLOCK, :], i, j)
+            seen.add((a, b))
+            at += BLOCK
+
+
+def panel_of(matrix, q, n, use):
+    w = matrix.shape[1] // n
+    for p in range(n):
+
+        @pl.when(q == p)
+        def _():
+            use(matrix[:, p * w : (p + 1) * w])
 
 
 def split(refs, *counts):
@@ -129,7 +210,7 @@
         c_full = whole(c_all)
         base[...] += mm_t(c_full, mid_high) + mm_t(c_full, mid_low)
 
-    base_bf[...] = base[...].astype(BF)
+    pack(base, base_bf, q, n)
 
 
 def group_comp_kernel(n, *refs):
@@ -181,26 +262,37 @@
 
 
 def group_cov_kernel(n, *refs):
-    ins, *blocks, outs, scratch = split(refs, 5, n, n, n, n, 3, 3)
+    ins, *blocks, outs, scratch = split(refs, 5, n, n, n, n, 3, 4)
     base, c, c_t, c01, c01_t = ins
     mine, agg, agg_bf = outs
-    s, s23, sems = scratch
-    hi, lo, q = where_am_i()
-    group_start(blocks, s, sems, lo, q, (3, 2, 1, 0))
-    group_wait(blocks[0], s, sems, 3)
-    mid = mm(whole(s.at[3]), whole(c.at[2])).astype(BF)
-    group_wait(blocks[0], s, sems, 2)
-    s23[...] = (whole(s.at[2]).astype(F32) + mm(c_t[2], mid)).astype(BF)
-    group_wait(blocks[0], s, sems, 1, 0)
-    agg[...] = s[0, q].astype(F32)
+    sent, s, s23, sems = scratch
+    hi, lo, q = where_am_i()
+    group_start(blocks, sent, sems, lo, q, (3, 2, 1, 0))
+    group_wait(blocks[0], sent, sems, 3)
+    unpack(sent.at[3], s.at[3], n)
+    mid = mm(s[3], whole(c.at[2])).astype(BF)
+    group_wait(blocks[0], sent, sems, 2)
+    unpack(sent.at[2], s.at[2], n)
+    s23[...] = (s[2].astype(F32) + mm(c_t[2], mid)).astype(BF)
+    group_wait(blocks[0], sent, sems, 1, 0)
+    unpack(sent.at[1], s.at[1], n)
 
     @pl.when(lo == 0)
     def _():
         agg[...] = base[...]
 
-    agg[...] += sandwich(whole(s.at[1]), c[0, q], c_t[0])
+    @pl.when(lo != 0)
+    def _():
+        unpack(sent.at[0], s.at[0], n)
+
+        def use(columns):
+            agg[...] = columns.astype(F32)
+
+        panel_of(s.at[0], q, n, use)
+
+    agg[...] += sandwich(s[1], c[0, q], c_t[0])
     agg[...] += sandwich(s23[...], c01[q], c01_t[...])
-    agg_bf[...] = agg[...].astype(BF)
+    pack(agg, agg_bf, q, n)
 
     @pl.when(lo == 0)
     def _():
@@ -212,7 +304,7 @@
 
     @pl.when(lo == 2)
     def _():
-        mine[...] = base[...] + sandwich(whole(s.at[3]), c[2, q], c_t[2])
+        mine[...] = base[...] + sandwich(s[3], c[2, q], c_t[2])
 
     @pl.when(lo == 3)
     def _():
@@ -233,61 +325,46 @@
     return pl.ds(pl.multiple_of(place * rows, rows), rows)
 
 
-def times(pieces, right, lo, q, n):
-    nb = right.shape[0]
-    w = nb // n
-
-    def product(some):
-        return sum(mm(x[...], right[panel_rows(q, r, n, w), :]) for r, x in enumerate(some))
-
-    if len(pieces) == n:
-        return [(slice(None), product(pieces))]
-    return [
-        (quarter_rows(jnp.bitwise_xor(lo, k), nb), product(pieces[k * n : k * n + n]))
-        for k in range(GROUP)
-    ]
-
-
-def own_columns(pieces, lo, q, n, nb):
-    if len(pieces) == n:
-        return [(slice(None), pieces[0])]
-    return [(quarter_rows(jnp.bitwise_xor(lo, k), nb), pieces[k * n]) for k in range(GROUP)]
-
-
-def place_whole(pieces, dst, lo, q, n):
-    for r in range(n):
-        p = lax.rem(q + r, n)
-        if len(pieces) == n:
-            dst[p] = pieces[r][...]
-        else:
-            for k in range(GROUP):
-                rows = quarter_rows(jnp.bitwise_xor(lo, k), dst.shape[1])
-                dst[p, rows, :] = pieces[k * n + r][...]
-
-
-def share_comp_kernel(n, m, bit, *refs):
-    (agg,), parts, (share,), (got, pair) = split(refs, 1, m, 1, 2)
+def times(pieces, right, q):
+    n = len(pieces)
+    w = right.shape[0] // n
+    return sum(mm(x[...], right[panel_rows(q, r, n, w), :]) for r, x in enumerate(pieces))
+
+
+def place_whole(pieces, dst, q):
+    for r, piece in enumerate(pieces):
+        dst[lax.rem(q + r, len(pieces))] = piece[...]
+
+
+def join_kernel(*refs):
+    *quarters, out = refs
+    hi, lo, q = where_am_i()
+    for k, piece in enumerate(quarters):
+        out[quarter_rows(jnp.bitwise_xor(lo, k), out.shape[0]), :] = piece[...]
+
+
+def share_comp_kernel(n, bit, *refs):
+    (agg,), parts, (share,), (got, pair) = split(refs, 1, n, 1, 2)
     hi, lo, q = where_am_i()
     lower = is_lower(bit)
 
     @pl.when(lower)
     def _():
-        for rows, value in times(parts, agg.at[q], lo, q, n):
-            pair[rows, :] = value.astype(BF)
+        pair[...] = times(parts, agg.at[q], q).astype(BF)
 
     @pl.when(jnp.logical_not(lower))
     def _():
-        place_whole(parts, got, lo, q, n)
+        place_whole(parts, got, q)
         pair[...] = mm(whole(agg), got[q]).astype(BF)
 
     share[...] = pair[quarter_rows(lo, pair.shape[0]), :]
 
 
-def pair_comp_kernel(n, m, bit, *refs):
-    (agg,), parts, (new_agg, new_agg_t, share), (got,) = split(refs, 1, m, 3, 1)
+def pair_comp_kernel(n, bit, *refs):
+    (agg,), parts, (new_agg, new_agg_t, share), (got,) = split(refs, 1, n, 3, 1)
     hi, lo, q = where_am_i()
     lower = is_lower(bit)
-    place_whole(parts, got, lo, q, n)
+    place_whole(parts, got, q)
 
     @pl.when(lower)
     def _():
@@ -301,16 +378,15 @@
     share[...] = new_agg[q, quarter_rows(lo, new_agg.shape[1]), :]
 
 
-def mine_comp_kernel(n, m, bit, *refs):
-    (mine, mine_t), parts, (new_mine, new_mine_t) = split(refs, 2, m, 2)
+def mine_comp_kernel(n, bit, *refs):
+    (mine, mine_t), parts, (new_mine, new_mine_t) = split(refs, 2, n, 2)
     hi, lo, q = where_am_i()
     lower = is_lower(bit)
 
     @pl.when(lower)
     def _():
         for p in range(n):
-            for rows, value in times(parts, mine.at[p], lo, q, n):
-                new_mine[p, rows, :] = value.astype(BF)
+            new_mine[p] = times(parts, mine.at[p], q).astype(BF)
         new_mine_t[...] = whole(new_mine).T
 
     @pl.when(jnp.logical_not(lower))
@@ -319,74 +395,79 @@
         new_mine_t[...] = mine_t[...]
 
 
-def last_comp_kernel(n, m, bit, *refs):
-    (mine,), parts, (out,) = split(refs, 1, m, 1)
+def last_comp_kernel(n, bit, *refs):
+    (mine,), parts, (out,) = split(refs, 1, n, 1)
     hi, lo, q = where_am_i()
     lower = is_lower(bit)
 
     @pl.when(lower)
     def _():
-        for rows, value in times(parts, mine.at[q], lo, q, n):
-            out[0, rows, :] = value.astype(BF)
+        out[0] = times(parts, mine.at[q], q).astype(BF)
 
     @pl.when(jnp.logical_not(lower))
     def _():
         out[0] = mine[q]
 
 
-def level_cov_kernel(n, m, bit, to_last, *refs):
-    ins, here, c_parts, parts, outs, scratch = split(refs, 6, n, m, m, 2 if to_last else 4, 3)
-    cov, agg, mine, mine_t, agg_c, agg_t = ins
-    new_cov, share = outs[:2]
-    mid, total, got = scratch
+def pair_cov_kernel(n, bit, to_last, *refs):
+    ins, here, c_parts, parts, outs, scratch = split(refs, 3, n, n, n, 2 if to_last else 4, 5)
+    agg, agg_c, agg_t = ins
+    share, right = outs[:2]
+    sent, mid, total, got, packed = scratch
     hi, lo, q = where_am_i()
     lower = is_lower(bit)
-    nb, w = cov.shape
-    mine_rows = quarter_rows(lo, nb)
-
-    def middle(pieces, right):
-        for rows, value in times(pieces, right, lo, q, n):
-            mid[rows, :] = value.astype(BF)
+    nb, w = agg.shape
+    place_whole(parts, sent, q)
+    unpack(sent, right, n)
 
     @pl.when(lower)
     def _():
-        middle(parts, agg_c.at[q])
-        if to_last:
-            share[...] = (agg[mine_rows, :] + mm(agg_t[mine_rows, :], mid[...])).astype(BF)
-        else:
-            total[...] = agg[...] + mm(agg_t[...], mid[...])
-        middle(parts, mine.at[q])
-        new_cov[...] = cov[...] + mm(mine_t[...], mid[...])
+        total[...] = agg[...] + sandwich(right[...], agg_c[q], agg_t[...])
 
     @pl.when(jnp.logical_not(lower))
     def _():
-        place_whole(c_parts, got, lo, q, n)
-        middle(here, got.at[q])
-        for rows, value in own_columns(parts, lo, q, n, nb):
-            total[rows, :] = value[...].astype(F32)
+        def use(columns):
+            total[...] = columns.astype(F32)
+
+        panel_of(right, q, n, use)
+        place_whole(here, sent, q)
+        unpack(sent, right, n)
+        place_whole(c_parts, got, q)
+        mid[...] = mm(right[...], got[q]).astype(BF)
         for p in range(n):
             total[p * w : (p + 1) * w, :] += mm_t(got[p], mid[...])
-        new_cov[...] = cov[...]
-        if to_last:
-            share[...] = total[mine_rows, :].astype(BF)
-
+
+    pack(total, packed, q, n)
+    share[...] = packed[quarter_rows(lo, packed.shape[0]), :]
     if not to_last:
         new_agg, new_agg_bf = outs[2:]
         new_agg[...] = total[...]
-        new_agg_bf[...] = total[...].astype(BF)
-        share[...] = new_agg_bf[mine_rows, :]
-
-
-def last_cov_kernel(n, m, bit, *refs):
-    (cov, mine, mine_t), parts, (out,), (mid,) = split(refs, 3, m, 1, 1)
+        new_agg_bf[...] = packed[...]
+
+
+def mine_cov_kernel(n, bit, cov, mine, mine_t, right, out):
     hi, lo, q = where_am_i()
     lower = is_lower(bit)
 
     @pl.when(lower)
     def _():
-        for rows, value in times(parts, mine.at[q], lo, q, n):
-            mid[rows, :] = value.astype(BF)
-        out[0] = cov[...] + mm(mine_t[...], mid[...])
+        out[...] = cov[...] + sandwich(right[...], mine[q], mine_t[...])
+
+    @pl.when(jnp.logical_not(lower))
+    def _():
+        out[...] = cov[...]
+
+
+def last_cov_kernel(n, bit, *refs):
+    (cov, mine, mine_t), parts, (out,), (sent, right) = split(refs, 3, n, 1, 2)
+    hi, lo, q = where_am_i()
+    lower = is_lower(bit)
+
+    @pl.when(lower)
+    def _():
+        place_whole(parts, sent, q)
+        unpack(sent, right, n)
+        out[0] = cov[...] + sandwich(right[...], mine[q], mine_t[...])
 
     @pl.when(jnp.logical_not(lower))
     def _():
@@ -422,8 +503,11 @@
     return [x] + [swap(x, mask, mask) for mask in range(1, GROUP)]
 
 
-def quarters(x):
-    return [p for block in in_group(x) for p in over_panels(block)]
+def joined(x):
+    quarters = in_group(x)
+    rows, lanes = x.shape
+    whole_panel = jax.ShapeDtypeStruct((rows * GROUP, lanes), x.dtype)
+    return call(join_kernel, quarters, [VMEM] * GROUP, [whole_panel], [], 0)[0]
 
 
 def after(x, *others):
@@ -443,6 +527,11 @@
     turned_bf = jax.ShapeDtypeStruct((GROUP - 1, nb, nb), BF)
     share_bf = jax.ShapeDtypeStruct((nb // GROUP, w), BF)
     full_scratch = pltpu.VMEM((n, nb, w), BF)
+    rows, lanes = packed_shape(n, nb, w)
+    packed_bf = jax.ShapeDtypeStruct((rows, lanes), BF)
+    packed_share = jax.ShapeDtypeStruct((rows // GROUP, lanes), BF)
+    packed_scratch = pltpu.VMEM((n, rows, lanes), BF)
+    square_scratch = pltpu.VMEM((nb, nb), BF)
     one = 2 * nb * nb * w
     sems = pltpu.SemaphoreType.DMA
 
@@ -456,12 +545,12 @@
         functools.partial(base_kernel, n),
         [factor, sigma_after, *f_parts, *c_own],
         [VMEM] + [ANY] * (1 + 2 * n),
-        [panel_f32, panel_bf],
+        [panel_f32, packed_bf],
         [full_scratch, full_scratch, pltpu.VMEM((nb, n * w), F32), sems((n + 1,))],
         2 * one,
     )
-    c_diag = swap(c_first, 2, 1)
     s_first = swap(base_bf, 1, 2)
+    c_diag = swap(after(c_first, s_first), 2, 1)
     c_pieces = [p for v in (c_first, c_second, c_diag) for p in over_panels(v)]
     s_second = swap(base_bf, 2, 1)
     c_all, c01, c23, agg_c = call(
@@ -482,92 +571,108 @@
         [],
         n * one,
     )
-    s_diag = swap(s_first, 2, 1)
+    s_diag = after(swap(s_first, 2, 1), agg_panel)
     s_own = over_panels(base_bf)
     s_pieces = s_own + [p for v in (s_first, s_second, s_diag) for p in over_panels(v)]
     cov, agg, agg_bf = call(
         functools.partial(group_cov_kernel, n),
         [base, c_all, c_t, c01, c01_t, *s_pieces],
         [VMEM] * 5 + [ANY] * (GROUP * n),
-        [panel_f32, panel_f32, panel_bf],
-        [pltpu.VMEM((GROUP, n, nb, w), BF), pltpu.VMEM((nb, nb), BF), sems((GROUP, n))],
+        [panel_f32, panel_f32, packed_bf],
+        [
+            pltpu.VMEM((GROUP, n, rows, lanes), BF),
+            pltpu.VMEM((GROUP, nb, nb), BF),
+            square_scratch,
+            sems((GROUP, n)),
+        ],
         (2 * n + 6) * one,
     )
     out_cov = jax.ShapeDtypeStruct((1, nb, w), F32)
     out_comp = jax.ShapeDtypeStruct((1, nb, w), BF)
     panel_scratch = pltpu.VMEM((nb, w), BF)
     sum_scratch = pltpu.VMEM((nb, w), F32)
-    c_parts = over_panels(c_got)
-    s_send = agg_bf
+    c_parts = over_panels(after(c_got, agg_bf))
+    s_got = across(after(agg_bf, c_got), 0, levels == 1)
     for bit in range(levels):
         last = bit + 1 == levels
         to_last = bit + 2 == levels
-        m = len(c_parts)
-        s_got = s_far if bit else across(after(s_send, c_got), bit, last)
         if last:
             (prop,) = call(
-                functools.partial(last_comp_kernel, n, m, bit),
+                functools.partial(last_comp_kernel, n, bit),
                 [mine, *c_parts],
-                [VMEM] * (1 + m),
+                [VMEM] * (1 + n),
                 [out_comp],
                 [],
                 one,
             )
-            s_parts = quarters(s_got) if bit else over_panels(s_got)
+            s_parts = over_panels(after(s_got, prop))
             (cov,) = call(
-                functools.partial(last_cov_kernel, n, m, bit),
+                functools.partial(last_cov_kernel, n, bit),
                 [cov, mine, mine_t, *s_parts],
-                [VMEM] * (3 + m),
+                [VMEM] * (3 + n),
                 [out_cov],
-                [panel_scratch],
+                [packed_scratch, square_scratch],
                 2 * one,
             )
             break
         agg_in = after(agg_c, agg_bf)
         if to_last:
             (c_send,) = call(
-                functools.partial(share_comp_kernel, n, m, bit),
+                functools.partial(share_comp_kernel, n, bit),
                 [agg_in, *c_parts],
-                [VMEM] * (1 + m),
+                [VMEM] * (1 + n),
                 [share_bf],
                 [full_scratch, panel_scratch],
                 one,
             )
         else:
             new_agg_c, new_agg_t, c_send = call(
-                functools.partial(pair_comp_kernel, n, m, bit),
+                functools.partial(pair_comp_kernel, n, bit),
                 [agg_in, *c_parts],
-                [VMEM] * (1 + m),
+                [VMEM] * (1 + n),
                 [full_bf, square_bf, share_bf],
                 [full_scratch],
                 n * one,
             )
         c_far = across(c_send, bit + 1, to_last)
         new_mine, new_mine_t = call(
-            functools.partial(mine_comp_kernel, n, m, bit),
+            functools.partial(mine_comp_kernel, n, bit),
             [after(mine, c_send), mine_t, *c_parts],
-            [VMEM] * (2 + m),
+            [VMEM] * (2 + n),
             [full_bf, square_bf],
             [],
             n * one,
         )
-        s_got = after(s_got, c_far, new_mine)
-        s_parts = quarters(s_got) if bit else over_panels(s_got)
+        s_parts = over_panels(after(s_got, c_far, new_mine))
         outs = call(
-            functools.partial(level_cov_kernel, n, m, bit, to_last),
-            [cov, agg, mine, mine_t, agg_c, agg_t, *over_panels(agg_bf), *c_parts, *s_parts],
-            [VMEM] * (6 + n + 2 * m),
-            [panel_f32, share_bf] + ([] if to_last else [panel_f32, panel_bf]),
-            [panel_scratch, sum_scratch, full_scratch],
-            4 * one,
+            functools.partial(pair_cov_kernel, n, bit, to_last),
+            [agg, agg_c, agg_t, *over_panels(agg_bf), *c_parts, *s_parts],
+            [VMEM] * (3 + 3 * n),
+            [packed_share, square_bf] + ([] if to_last else [panel_f32, packed_bf]),
+            [
+                packed_scratch,
+                panel_scratch,
+                sum_scratch,
+                full_scratch,
+                pltpu.VMEM((rows, lanes), BF),
+            ],
+            2 * one,
         )
-        cov, s_send = outs[:2]
+        s_send, right = outs[:2]
+        (cov,) = call(
+            functools.partial(mine_cov_kernel, n, bit),
+            [cov, mine, mine_t, right],
+            [VMEM] * 4,
+            [panel_f32],
+            [],
+            2 * one,
+        )
         if not to_last:
             agg, agg_bf = outs[2:]
             agg_c, agg_t = new_agg_c, new_agg_t
         s_far = across(s_send, bit + 1, to_last)
-        c_blocks = in_group(after(c_far, s_send))
-        c_parts = [p for b in c_blocks for p in over_panels(after(b, s_far))]
+        c_parts = over_panels(after(joined(after(c_far, cov)), s_far))
+        s_got = joined(s_far)
         mine, mine_t = new_mine, new_mine_t
     return cov, prop
 

time: 118 us -> 110 us (0.932)
  waiting for transfers between devices: 61.5 us -> 52.5 us
  Pallas kernels: 24.6 us -> 26.3 us
    ppermute x4, waiting for transfers between devices: 24 us -> 15.3 us  [across(): lax.ppermute(x, 'tm', [(t, t ^ d) for t in range(steps) if t ^ d < steps...]
    ppermute x12, waiting for transfers between devices: 35.2 us -> 33.2 us  [swap(): return lax.ppermute(value, ('tm', 'panel'), pairs)]
    pallas_call x9 -> x12, Pallas kernels: 24.6 us -> 26.3 us  [call(): pl.pallas_call(kernel, in_specs=in_specs, out_specs=[VMEM] * len(outs), o...]
    ppermute x20 -> x14, waiting for transfers between devices: 2.32 us -> 3.97 us  [over_panels(): lax.ppermute(x, 'panel', [((i + r) % n, i) for i in range(n)])]
    ppermute x20 -> x14, starting transfers between devices: 2.48 us -> 1.83 us  [over_panels(): lax.ppermute(x, 'panel', [((i + r) % n, i) for i in range(n)])]
  transfers between devices with their start and end apart: 36 -> 30, of which waited for: 13 -> 15; matrix products, arithmetic and copies ran while one was open for 0% -> 0% of each run, Pallas kernels for 16% -> 17%
where the time goes in v2:
time: 110 us
  waiting for transfers between devices  52.5 us (48%)
  starting transfers between devices  28.6 us (26%)
  Pallas kernels  26.3 us (24%)
  other arithmetic  1.55 us (1%)
    ppermute x12, waiting for transfers between devices, swap(): return lax.ppermute(value, ('tm', 'panel'), pairs)  33.2 us
    pallas_call x12, Pallas kernels, call(): pl.pallas_call(kernel, in_specs=in_specs, out_specs=[VMEM] * len(outs), o...  26.3 us
    ppermute x12, starting transfers between devices, swap(): return lax.ppermute(value, ('tm', 'panel'), pairs)  21.4 us
    ppermute x4, waiting for transfers between devices, across(): lax.ppermute(x, 'tm', [(t, t ^ d) for t in range(steps) if t ^ d < steps...  15.3 us
    ppermute x4, starting transfers between devices, across(): lax.ppermute(x, 'tm', [(t, t ^ d) for t in range(steps) if t ^ d < steps...  5.36 us
    ppermute x14, waiting for transfers between devices, over_panels(): lax.ppermute(x, 'panel', [((i + r) % n, i) for i in range(n)])  3.97 us
  transfers between devices with their start and end apart: 30, of which 15 were waited for; matrix products, arithmetic and copies ran while one was open for 0% of the time, Pallas kernels for 17%

profile of v2, /device:TPU:0, one launch (start us, length us, event | category | flops | bytes accessed | tf_op | source)
XLA Modules:
  0.0 110.0 jit_solution(11610221152611271604)
XLA Ops:
  0.6 1.5 %convert_bitcast_fusion.refs_4_.refs_0_ = bf16[768,384]{1,0:T(8,128)(2,1)S(1)} fusion(f32[1,768,384]{2,1,0:T(8,128)} %param.4), kind=kLoop, calls=%fused_computation.1 | loop fusion | flops 294912 | bytes 1769472 | tf_op jit(solution)/shard_map/convert_element_type | solution.py:538
  2.9 2.9 %collective-permute-start.2 = (bf16[768,384]{1,0:T(8,128)(2,1)S(1)}, bf16[768,384]{1,0:T(8,128)(2,1)S(1)}, u32[]{:S(2)}, u32[]{:S(2)}) collective-permute-start(bf16[768,384]{1,0:T(8,128)(2,1)S(1)} %convert_bitcast_fusion.refs_4_.refs_0_), channel_id=1, source_target_pairs={{0,4},{1,3},{2,6},{3,1},{4,0},{5,7},{6,2},{7,5},{8,12},{9,11},{10,... | collective-permute-start | bytes 1769480 | tf_op jit(solution)/shard_map/ppermute | solution.py:491
  5.9 2.5 %shard_map.50 = (f32[768,384]{1,0:T(8,128)S(1)}, bf16[1408,128]{1,0:T(8,128)(2,1)}) custom-call(f32[768,384]{1,0:T(8,128)S(1)} %bitcast.6, f32[768,768]{1,0:T(8,128)S(1)} %copy-done.1, bf16[768,384]{1,0:T(8,128)(2,1)S(1)} %convert_element_type.10.refs_2_, bf16[768,384]{1,0:T(8,128)(2,1)S(1)} %collective-permute-done.refs_3_, ...), custom_call_target="tpu_custom_call" | custom-call | flops 905969664 | bytes 7438336 | tf_op jit(solution)/shard_map/pallas_call | solution.py:174
  8.4 2.4 %collective-permute-start.6 = (bf16[1408,128]{1,0:T(8,128)(2,1)}, bf16[1408,128]{1,0:T(8,128)(2,1)S(1)}, u32[]{:S(2)}, u32[]{:S(2)}) collective-permute-start(bf16[1408,128]{1,0:T(8,128)(2,1)} %get-tuple-element.33.refs_5_), channel_id=1, source_target_pairs={{0,4},{1,3},{2,6},{3,1},{4,0},{5,7},{6,2},{7,5},{8,12},{9,11},{10,... | collective-permute-start | bytes 1081352 | tf_op jit(solution)/shard_map/ppermute | solution.py:491
  10.7 1.5 %collective-permute-start.4 = (bf16[768,384]{1,0:T(8,128)(2,1)S(1)}, bf16[768,384]{1,0:T(8,128)(2,1)S(1)}, u32[]{:S(2)}, u32[]{:S(2)}) collective-permute-start(bf16[768,384]{1,0:T(8,128)(2,1)S(1)} %convert_bitcast_fusion.refs_4_.refs_0_), channel_id=1, source_target_pairs={{0,2},{1,5},{2,0},{3,7},{4,6},{5,1},{6,4},{7,3},{8,10},{9,13},{10,... | collective-permute-start | bytes 1769480 | tf_op jit(solution)/shard_map/ppermute | solution.py:491
  12.3 2.0 %collective-permute-done.2.refs_2_ = bf16[768,384]{1,0:T(8,128)(2,1)S(1)} collective-permute-done((bf16[768,384]{1,0:T(8,128)(2,1)S(1)}, bf16[768,384]{1,0:T(8,128)(2,1)S(1)}, u32[]{:S(2)}, u32[]{:S(2)}) %collective-permute-start.2) | collective-permute-done | bytes 589856 | tf_op jit(solution)/shard_map/ppermute | solution.py:491
  14.3 7.8 %collective-permute-done.6.refs_7_ = bf16[1408,128]{1,0:T(8,128)(2,1)S(1)} collective-permute-done((bf16[1408,128]{1,0:T(8,128)(2,1)}, bf16[1408,128]{1,0:T(8,128)(2,1)S(1)}, u32[]{:S(2)}, u32[]{:S(2)}) %collective-permute-start.6) | collective-permute-done | bytes 360480 | tf_op jit(solution)/shard_map/ppermute | solution.py:491
  22.1 3.5 %collective-permute-start.7 = (bf16[768,384]{1,0:T(8,128)(2,1)S(1)}, bf16[768,384]{1,0:T(8,128)(2,1)}, u32[]{:S(2)}, u32[]{:S(2)}) collective-permute-start(bf16[768,384]{1,0:T(8,128)(2,1)S(1)} %collective-permute-done.2.refs_2_), channel_id=1, source_target_pairs={{0,2},{1,5},{2,0},{3,7},{4,6},{5,1},{6,4},{7,3},{8,10},{9,13},{10,... | collective-permute-start | bytes 1769480 | tf_op jit(solution)/shard_map/ppermute | solution.py:491
  26.1 7.5 %collective-permute-done.7.refs_6_ = bf16[768,384]{1,0:T(8,128)(2,1)} collective-permute-done((bf16[768,384]{1,0:T(8,128)(2,1)S(1)}, bf16[768,384]{1,0:T(8,128)(2,1)}, u32[]{:S(2)}, u32[]{:S(2)}) %collective-permute-start.7) | collective-permute-done | bytes 589856 | tf_op jit(solution)/shard_map/ppermute | solution.py:491
  33.6 2.0 %collective-permute-start.11 = (bf16[1408,128]{1,0:T(8,128)(2,1)}, bf16[1408,128]{1,0:T(8,128)(2,1)}, u32[]{:S(2)}, u32[]{:S(2)}) collective-permute-start(bf16[1408,128]{1,0:T(8,128)(2,1)} %get-tuple-element.33.refs_5_), channel_id=1, source_target_pairs={{0,2},{1,5},{2,0},{3,7},{4,6},{5,1},{6,4},{7,3},{8,10},{9,13},{10,... | collective-permute-start | bytes 1081352 | tf_op jit(solution)/shard_map/ppermute | solution.py:491
  35.6 5.7 %collective-permute-done.11.refs_9_ = bf16[1408,128]{1,0:T(8,128)(2,1)} collective-permute-done((bf16[1408,128]{1,0:T(8,128)(2,1)}, bf16[1408,128]{1,0:T(8,128)(2,1)}, u32[]{:S(2)}, u32[]{:S(2)}) %collective-permute-start.11) | collective-permute-done | bytes 360480 | tf_op jit(solution)/shard_map/ppermute | solution.py:491
  41.3 2.0 %collective-permute-start.13 = (bf16[1408,128]{1,0:T(8,128)(2,1)}, bf16[1408,128]{1,0:T(8,128)(2,1)S(1)}, u32[]{:S(2)}, u32[]{:S(2)}) collective-permute-start(bf16[1408,128]{1,0:T(8,128)(2,1)} %copy-done.2), channel_id=1, source_target_pairs={{0,2},{1,5},{2,0},{3,7},{4,6},{5,1},{6,4},{7,3},{8,10},{9,13},{10,... | collective-permute-start | bytes 1081352 | tf_op jit(solution)/shard_map/ppermute | solution.py:491
  43.8 4.5 %shard_map.51 = (bf16[4,2,768,384]{3,2,1,0:T(8,128)(2,1)S(1)}, bf16[2,768,384]{2,1,0:T(8,128)(2,1)S(1)}, bf16[768,768]{1,0:T(8,128)(2,1)S(1)}, bf16[2,768,384]{2,1,0:T(8,128)(2,1)S(1)}) custom-call(bf16[768,384]{1,0:T(8,128)(2,1)S(1)} %convert_bitcast_fusion.refs_4_.refs_0_, bf16[768,384]{1,0:T(8,128)(2,1)S(1)} %collective-permute-done.1.refs_5_.refs_1_, ...), custom_call_target="tpu_custom_call" | custom-call | flops 2717908992 | bytes 12976128 | tf_op jit(solution)/shard_map/pallas_call | solution.py:174
  50.3 1.8 %shard_map.52 = (bf16[3,768,768]{2,1,0:T(8,128)(2,1)S(1)}, bf16[768,768]{1,0:T(8,128)(2,1)S(1)}, bf16[2,768,384]{2,1,0:T(8,128)(2,1)S(1)}, bf16[768,768]{1,0:T(8,128)(2,1)S(1)}, bf16[768,768]{1,0:T(8,128)(2,1)S(1)}) custom-call(bf16[4,2,768,384]{3,2,1,0:T(8,128)(2,1)S(1)} %get-tuple-element.35.c.refs_1_, ...), custom_call_target="tpu_custom_call" | custom-call | flops 905969664 | bytes 16515072 | tf_op jit(solution)/shard_map/pallas_call | solution.py:174
  52.1 7.2 %shard_map.53 = (f32[768,384]{1,0:T(8,128)S(1)}, f32[768,384]{1,0:T(8,128)S(1)}, bf16[1408,128]{1,0:T(8,128)(2,1)S(1)}) custom-call(f32[768,384]{1,0:T(8,128)S(1)} %get-tuple-element.32.refs_0_, bf16[4,2,768,384]{3,2,1,0:T(8,128)(2,1)S(1)} %get-tuple-element.35.c.refs_1_, bf16[3,768,768]{2,1,0:T(8,128)(2,1)S(1)} %get-tuple-element.39.refs_2_, ...), custom_call_target="tpu_custom_call" | custom-call | flops 4529848320 | bytes 17399808 | tf_op jit(solution)/shard_map/pallas_call | solution.py:174
  59.4 5.3 %collective-permute-done.16.refs_1_.refs_2_.refs_5_ = bf16[768,384]{1,0:T(8,128)(2,1)S(1)} collective-permute-done((bf16[768,384]{1,0:T(8,128)(2,1)S(1)}, bf16[768,384]{1,0:T(8,128)(2,1)S(1)}, u32[]{:S(2)}, u32[]{:S(2)}) %collective-permute-start.16) | collective-permute-done | bytes 589856 | tf_op jit(solution)/shard_map/ppermute | solution.py:497
  64.7 1.4 %collective-permute-start.18 = (bf16[1408,128]{1,0:T(8,128)(2,1)S(1)}, bf16[1408,128]{1,0:T(8,128)(2,1)S(1)}, u32[]{:S(2)}, u32[]{:S(2)}) collective-permute-start(bf16[1408,128]{1,0:T(8,128)(2,1)S(1)} %get-tuple-element.49.refs_3_), channel_id=1, source_target_pairs={{0,8},{2,10},{4,12},{6,14},{8,0},{10,2},{12,4},{14,6},{16,24},{18,... | collective-permute-start | bytes 1081352 | tf_op jit(solution)/shard_map/ppermute | solution.py:497
  69.1 1.8 %shard_map.55 = (bf16[2,768,384]{2,1,0:T(8,128)(2,1)S(1)}, bf16[768,768]{1,0:T(8,128)(2,1)S(1)}) custom-call(bf16[2,768,384]{2,1,0:T(8,128)(2,1)S(1)} %get-tuple-element.51.refs_0_.mine, bf16[768,768]{1,0:T(8,128)(2,1)S(1)} %get-tuple-element.44.refs_1_.mine_t, bf16[768,384]{1,0:T(8,128)(2,1)S(1)} %collective-permute-done.16.refs_1_.refs_2_.refs_5_, ...), custom_call_target="tpu_custom_call" | custom-call | flops 905969664 | bytes 5898240 | tf_op jit(solution)/shard_map/pallas_call | solution.py:174
  70.8 7.8 %collective-permute-done.18.refs_7_ = bf16[1408,128]{1,0:T(8,128)(2,1)S(1)} collective-permute-done((bf16[1408,128]{1,0:T(8,128)(2,1)S(1)}, bf16[1408,128]{1,0:T(8,128)(2,1)S(1)}, u32[]{:S(2)}, u32[]{:S(2)}) %collective-permute-start.18) | collective-permute-done | bytes 360480 | tf_op jit(solution)/shard_map/ppermute | solution.py:497
  78.7 1.7 %collective-permute-done.20.refs_8_ = bf16[1408,128]{1,0:T(8,128)(2,1)S(1)} collective-permute-done((bf16[1408,128]{1,0:T(8,128)(2,1)S(1)}, bf16[1408,128]{1,0:T(8,128)(2,1)S(1)}, u32[]{:S(2)}, u32[]{:S(2)}) %collective-permute-start.20) | collective-permute-done | bytes 360480 | tf_op jit(solution)/shard_map/ppermute | solution.py:480
  80.4 2.0 %shard_map.56 = (bf16[352,128]{1,0:T(8,128)(2,1)S(1)}, bf16[768,768]{1,0:T(8,128)(2,1)S(1)}) custom-call(f32[768,384]{1,0:T(8,128)S(1)} %get-tuple-element.45.refs_0_, bf16[2,768,384]{2,1,0:T(8,128)(2,1)S(1)} %get-tuple-element.50.agg.refs_0_.refs_1_, bf16[768,768]{1,0:T(8,128)(2,1)S(1)} %get-tuple-element.46.refs_2_, ...), custom_call_target="tpu_custom_call" | custom-call | flops 905969664 | bytes 7430144 | tf_op jit(solution)/shard_map/pallas_call | solution.py:174
  82.3 1.4 %shard_map.57.refs_0_ = f32[768,384]{1,0:T(8,128)S(1)} custom-call(f32[768,384]{1,0:T(8,128)S(1)} %get-tuple-element.42.cov, bf16[2,768,384]{2,1,0:T(8,128)(2,1)S(1)} %get-tuple-element.51.refs_0_.mine, bf16[768,768]{1,0:T(8,128)(2,1)S(1)} %get-tuple-element.44.refs_1_.mine_t, bf16[768,768]{1,0:T(8,128)(2,1)S(1)} %get-tuple-element.54.right), custom_call_target="tpu_custom_call" | custom-call | flops 905969664 | bytes 5898240 | tf_op jit(solution)/shard_map/pallas_call | solution.py:174
  83.7 2.9 %collective-permute-start.27 = (bf16[192,384]{1,0:T(8,128)(2,1)S(1)}, bf16[192,384]{1,0:T(8,128)(2,1)S(1)}, u32[]{:S(2)}, u32[]{:S(2)}) collective-permute-start(bf16[192,384]{1,0:T(8,128)(2,1)S(1)} %collective-permute-done.19.refs_0_), channel_id=1, source_target_pairs={{0,6},{1,7},{2,4},{3,5},{4,2},{5,3},{6,0},{7,1},{8,14},{9,15},{10,... | collective-permute-start | bytes 442376 | tf_op jit(solution)/shard_map/ppermute | solution.py:491
  88.6 2.6 %collective-permute-done.27.refs_3_ = bf16[192,384]{1,0:T(8,128)(2,1)S(1)} collective-permute-done((bf16[192,384]{1,0:T(8,128)(2,1)S(1)}, bf16[192,384]{1,0:T(8,128)(2,1)S(1)}, u32[]{:S(2)}, u32[]{:S(2)}) %collective-permute-start.27) | collective-permute-done | bytes 147488 | tf_op jit(solution)/shard_map/ppermute | solution.py:491
  91.2 2.7 %collective-permute-done.26.refs_2_ = bf16[192,384]{1,0:T(8,128)(2,1)S(1)} collective-permute-done((bf16[192,384]{1,0:T(8,128)(2,1)S(1)}, bf16[192,384]{1,0:T(8,128)(2,1)S(1)}, u32[]{:S(2)}, u32[]{:S(2)}) %collective-permute-start.26) | collective-permute-done | bytes 147488 | tf_op jit(solution)/shard_map/ppermute | solution.py:491
  94.0 2.2 %collective-permute-done.21.refs_0_ = bf16[352,128]{1,0:T(8,128)(2,1)S(1)} collective-permute-done((bf16[352,128]{1,0:T(8,128)(2,1)S(1)}, bf16[352,128]{1,0:T(8,128)(2,1)S(1)}, u32[]{:S(2)}, u32[]{:S(2)}) %collective-permute-start.21) | collective-permute-done | bytes 90144 | tf_op jit(solution)/shard_map/ppermute | solution.py:497
  96.2 2.6 %collective-permute-start.24 = (bf16[352,128]{1,0:T(8,128)(2,1)S(1)}, bf16[352,128]{1,0:T(8,128)(2,1)S(1)}, u32[]{:S(2)}, u32[]{:S(2)}) collective-permute-start(bf16[352,128]{1,0:T(8,128)(2,1)S(1)} %collective-permute-done.21.refs_0_), channel_id=1, source_target_pairs={{0,6},{1,7},{2,4},{3,5},{4,2},{5,3},{6,0},{7,1},{8,14},{9,15},{10,... | collective-permute-start | bytes 270344 | tf_op jit(solution)/shard_map/ppermute | solution.py:491
  99.7 2.5 %collective-permute-done.24.refs_3_ = bf16[352,128]{1,0:T(8,128)(2,1)S(1)} collective-permute-done((bf16[352,128]{1,0:T(8,128)(2,1)S(1)}, bf16[352,128]{1,0:T(8,128)(2,1)S(1)}, u32[]{:S(2)}, u32[]{:S(2)}) %collective-permute-start.24) | collective-permute-done | bytes 90144 | tf_op jit(solution)/shard_map/ppermute | solution.py:491
  102.2 1.9 %collective-permute-done.23.refs_2_ = bf16[352,128]{1,0:T(8,128)(2,1)S(1)} collective-permute-done((bf16[352,128]{1,0:T(8,128)(2,1)S(1)}, bf16[352,128]{1,0:T(8,128)(2,1)S(1)}, u32[]{:S(2)}, u32[]{:S(2)}) %collective-permute-start.23) | collective-permute-done | bytes 90144 | tf_op jit(solution)/shard_map/ppermute | solution.py:491
  104.1 1.7 %shard_map.60 = bf16[1,768,384]{2,1,0:T(8,128)(2,1)} custom-call(bf16[2,768,384]{2,1,0:T(8,128)(2,1)S(1)} %get-tuple-element.52.refs_0_.refs_1_, bf16[768,384]{1,0:T(8,128)(2,1)S(1)} %shard_map.59.refs_1_, bf16[768,384]{1,0:T(8,128)(2,1)S(1)} %collective-permute-done.28.refs_2_), custom_call_target="tpu_custom_call" | custom-call | flops 452984832 | bytes 2949120 | tf_op jit(solution)/shard_map/pallas_call | solution.py:174
  105.8 1.7 %collective-permute-done.29.refs_4_ = bf16[1408,128]{1,0:T(8,128)(2,1)S(1)} collective-permute-done((bf16[1408,128]{1,0:T(8,128)(2,1)S(1)}, bf16[1408,128]{1,0:T(8,128)(2,1)S(1)}, u32[]{:S(2)}, u32[]{:S(2)}) %collective-permute-start.29) | collective-permute-done | bytes 360480 | tf_op jit(solution)/shard_map/ppermute | solution.py:480
  107.5 2.5 %shard_map.61 = f32[1,768,384]{2,1,0:T(8,128)} custom-call(f32[768,384]{1,0:T(8,128)S(1)} %shard_map.57.refs_0_, bf16[2,768,384]{2,1,0:T(8,128)(2,1)S(1)} %get-tuple-element.52.refs_0_.refs_1_, bf16[768,768]{1,0:T(8,128)(2,1)S(1)} %get-tuple-element.55.refs_2_, bf16[1408,128]{1,0:T(8,128)(2,1)S(1)} %shard_map.58.refs_3_, ...), custom_call_target="tpu_custom_call" | custom-call | flops 905969664 | bytes 5439488 | tf_op jit(solution)/shard_map/pallas_call | solution.py:174
  (51 shorter events, 9.9 us)
Async XLA Ops:
  0.6 5.2 %copy-start.1 = (f32[768,768]{1,0:T(8,128)S(1)}, f32[768,768]{1,0:T(8,128)}, u32[]{:S(2)}) copy-start(f32[768,768]{1,0:T(8,128)} %refs_1_.1) | copy-start | bytes 7077892
  2.3 3.5 %collective-permute-start = (bf16[768,384]{1,0:T(8,128)(2,1)S(1)}, bf16[768,384]{1,0:T(8,128)(2,1)S(1)}, u32[]{:S(2)}, u32[]{:S(2)}) collective-permute-start(bf16[768,384]{1,0:T(8,128)(2,1)S(1)} %convert_element_type.10.refs_2_), channel_id=1, source_target_pairs={{1,0},{0,1},{3,2},{2,3},{5,4},{4,5},{7,6},{6,7},{9,8},{8,9},{11,10... | collective-permute-start | bytes 1769480 | tf_op jit(solution)/shard_map/ppermute | solution.py:480
  2.8 3.0 %collective-permute-start.1 = (bf16[768,384]{1,0:T(8,128)(2,1)S(1)}, bf16[768,384]{1,0:T(8,128)(2,1)S(1)}, u32[]{:S(2)}, u32[]{:S(2)}) collective-permute-start(bf16[768,384]{1,0:T(8,128)(2,1)S(1)} %convert_bitcast_fusion.refs_4_.refs_0_), channel_id=1, source_target_pairs={{1,0},{0,1},{3,2},{2,3},{5,4},{4,5},{7,6},{6,7},{9,8},{8,9},{11,10... | collective-permute-start | bytes 1769480 | tf_op jit(solution)/shard_map/ppermute | solution.py:480
  2.9 11.3 %collective-permute-start.2 = (bf16[768,384]{1,0:T(8,128)(2,1)S(1)}, bf16[768,384]{1,0:T(8,128)(2,1)S(1)}, u32[]{:S(2)}, u32[]{:S(2)}) collective-permute-start(bf16[768,384]{1,0:T(8,128)(2,1)S(1)} %convert_bitcast_fusion.refs_4_.refs_0_), channel_id=1, source_target_pairs={{0,4},{1,3},{2,6},{3,1},{4,0},{5,7},{6,2},{7,5},{8,12},{9,11},{10,... | collective-permute-start | bytes 1769480 | tf_op jit(solution)/shard_map/ppermute | solution.py:491
  8.4 13.7 %collective-permute-start.6 = (bf16[1408,128]{1,0:T(8,128)(2,1)}, bf16[1408,128]{1,0:T(8,128)(2,1)S(1)}, u32[]{:S(2)}, u32[]{:S(2)}) collective-permute-start(bf16[1408,128]{1,0:T(8,128)(2,1)} %get-tuple-element.33.refs_5_), channel_id=1, source_target_pairs={{0,4},{1,3},{2,6},{3,1},{4,0},{5,7},{6,2},{7,5},{8,12},{9,11},{10,... | collective-permute-start | bytes 1081352 | tf_op jit(solution)/shard_map/ppermute | solution.py:491
  10.7 14.8 %collective-permute-start.4 = (bf16[768,384]{1,0:T(8,128)(2,1)S(1)}, bf16[768,384]{1,0:T(8,128)(2,1)S(1)}, u32[]{:S(2)}, u32[]{:S(2)}) collective-permute-start(bf16[768,384]{1,0:T(8,128)(2,1)S(1)} %convert_bitcast_fusion.refs_4_.refs_0_), channel_id=1, source_target_pairs={{0,2},{1,5},{2,0},{3,7},{4,6},{5,1},{6,4},{7,3},{8,10},{9,13},{10,... | collective-permute-start | bytes 1769480 | tf_op jit(solution)/shard_map/ppermute | solution.py:491
  22.1 11.5 %copy-start.2 = (bf16[1408,128]{1,0:T(8,128)(2,1)}, bf16[1408,128]{1,0:T(8,128)(2,1)S(1)}, u32[]{:S(2)}) copy-start(bf16[1408,128]{1,0:T(8,128)(2,1)S(1)} %collective-permute-done.6.refs_7_) | copy-start | bytes 1081348
  22.1 11.4 %collective-permute-start.7 = (bf16[768,384]{1,0:T(8,128)(2,1)S(1)}, bf16[768,384]{1,0:T(8,128)(2,1)}, u32[]{:S(2)}, u32[]{:S(2)}) collective-permute-start(bf16[768,384]{1,0:T(8,128)(2,1)S(1)} %collective-permute-done.2.refs_2_), channel_id=1, source_target_pairs={{0,2},{1,5},{2,0},{3,7},{4,6},{5,1},{6,4},{7,3},{8,10},{9,13},{10,... | collective-permute-start | bytes 1769480 | tf_op jit(solution)/shard_map/ppermute | solution.py:491
  25.6 17.7 %collective-permute-start.5 = (bf16[768,384]{1,0:T(8,128)(2,1)S(1)}, bf16[768,384]{1,0:T(8,128)(2,1)}, u32[]{:S(2)}, u32[]{:S(2)}) collective-permute-start(bf16[768,384]{1,0:T(8,128)(2,1)S(1)} %collective-permute-done.4.refs_4_), channel_id=1, source_target_pairs={{1,0},{0,1},{3,2},{2,3},{5,4},{4,5},{7,6},{6,7},{9,8},{8,9},{11,10... | collective-permute-start | bytes 1769480 | tf_op jit(solution)/shard_map/ppermute | solution.py:480
  25.6 17.7 %collective-permute-start.3 = (bf16[768,384]{1,0:T(8,128)(2,1)S(1)}, bf16[768,384]{1,0:T(8,128)(2,1)}, u32[]{:S(2)}, u32[]{:S(2)}) collective-permute-start(bf16[768,384]{1,0:T(8,128)(2,1)S(1)} %collective-permute-done.2.refs_2_), channel_id=1, source_target_pairs={{1,0},{0,1},{3,2},{2,3},{5,4},{4,5},{7,6},{6,7},{9,8},{8,9},{11,10... | collective-permute-start | bytes 1769480 | tf_op jit(solution)/shard_map/ppermute | solution.py:480
  33.6 10.3 %collective-permute-start.8 = (bf16[768,384]{1,0:T(8,128)(2,1)}, bf16[768,384]{1,0:T(8,128)(2,1)}, u32[]{:S(2)}, u32[]{:S(2)}) collective-permute-start(bf16[768,384]{1,0:T(8,128)(2,1)} %collective-permute-done.7.refs_6_), channel_id=1, source_target_pairs={{1,0},{0,1},{3,2},{2,3},{5,4},{4,5},{7,6},{6,7},{9,8},{8,9},{11,10... | collective-permute-start | bytes 1769480 | tf_op jit(solution)/shard_map/ppermute | solution.py:480
  33.6 7.7 %collective-permute-start.11 = (bf16[1408,128]{1,0:T(8,128)(2,1)}, bf16[1408,128]{1,0:T(8,128)(2,1)}, u32[]{:S(2)}, u32[]{:S(2)}) collective-permute-start(bf16[1408,128]{1,0:T(8,128)(2,1)} %get-tuple-element.33.refs_5_), channel_id=1, source_target_pairs={{0,2},{1,5},{2,0},{3,7},{4,6},{5,1},{6,4},{7,3},{8,10},{9,13},{10,... | collective-permute-start | bytes 1081352 | tf_op jit(solution)/shard_map/ppermute | solution.py:491
  35.6 16.5 %collective-permute-start.9 = (bf16[1408,128]{1,0:T(8,128)(2,1)}, bf16[1408,128]{1,0:T(8,128)(2,1)S(1)}, u32[]{:S(2)}, u32[]{:S(2)}) collective-permute-start(bf16[1408,128]{1,0:T(8,128)(2,1)} %get-tuple-element.33.refs_5_), channel_id=1, source_target_pairs={{1,0},{0,1},{3,2},{2,3},{5,4},{4,5},{7,6},{6,7},{9,8},{8,9},{11,10... | collective-permute-start | bytes 1081352 | tf_op jit(solution)/shard_map/ppermute | solution.py:480
  41.3 7.6 %collective-permute-start.13 = (bf16[1408,128]{1,0:T(8,128)(2,1)}, bf16[1408,128]{1,0:T(8,128)(2,1)S(1)}, u32[]{:S(2)}, u32[]{:S(2)}) collective-permute-start(bf16[1408,128]{1,0:T(8,128)(2,1)} %copy-done.2), channel_id=1, source_target_pairs={{0,2},{1,5},{2,0},{3,7},{4,6},{5,1},{6,4},{7,3},{8,10},{9,13},{10,... | collective-permute-start | bytes 1081352 | tf_op jit(solution)/shard_map/ppermute | solution.py:491
  43.3 8.8 %collective-permute-start.10 = (bf16[1408,128]{1,0:T(8,128)(2,1)}, bf16[1408,128]{1,0:T(8,128)(2,1)S(1)}, u32[]{:S(2)}, u32[]{:S(2)}) collective-permute-start(bf16[1408,128]{1,0:T(8,128)(2,1)} %copy-done.2), channel_id=1, source_target_pairs={{1,0},{0,1},{3,2},{2,3},{5,4},{4,5},{7,6},{6,7},{9,8},{8,9},{11,10... | collective-permute-start | bytes 1081352 | tf_op jit(solution)/shard_map/ppermute | solution.py:480
  43.3 8.8 %collective-permute-start.12 = (bf16[1408,128]{1,0:T(8,128)(2,1)}, bf16[1408,128]{1,0:T(8,128)(2,1)S(1)}, u32[]{:S(2)}, u32[]{:S(2)}) collective-permute-start(bf16[1408,128]{1,0:T(8,128)(2,1)} %collective-permute-done.11.refs_9_), channel_id=1, source_target_pairs={{1,0},{0,1},{3,2},{2,3},{5,4},{4,5},{7,6},{6,7},{9,8},{8,9},{11,10... | collective-permute-start | bytes 1081352 | tf_op jit(solution)/shard_map/ppermute | solution.py:480
  48.9 3.2 %collective-permute-start.14 = (bf16[1408,128]{1,0:T(8,128)(2,1)S(1)}, bf16[1408,128]{1,0:T(8,128)(2,1)S(1)}, u32[]{:S(2)}, u32[]{:S(2)}) collective-permute-start(bf16[1408,128]{1,0:T(8,128)(2,1)S(1)} %collective-permute-done.13.refs_11_), channel_id=1, source_target_pairs={{1,0},{0,1},{3,2},{2,3},{5,4},{4,5},{7,6},{6,7},{9,8},{8,9},{11,10... | collective-permute-start | bytes 1081352 | tf_op jit(solution)/shard_map/ppermute | solution.py:480
  48.9 15.7 %collective-permute-start.16 = (bf16[768,384]{1,0:T(8,128)(2,1)S(1)}, bf16[768,384]{1,0:T(8,128)(2,1)S(1)}, u32[]{:S(2)}, u32[]{:S(2)}) collective-permute-start(bf16[768,384]{1,0:T(8,128)(2,1)S(1)} %dynamic-slice_bitcast_fusion), channel_id=1, source_target_pairs={{0,8},{2,10},{4,12},{6,14},{8,0},{10,2},{12,4},{14,6},{16,24},{18,... | collective-permute-start | bytes 1769480 | tf_op jit(solution)/shard_map/ppermute | solution.py:497
  64.7 2.0 %collective-permute-start.17 = (bf16[768,384]{1,0:T(8,128)(2,1)S(1)}, bf16[768,384]{1,0:T(8,128)(2,1)S(1)}, u32[]{:S(2)}, u32[]{:S(2)}) collective-permute-start(bf16[768,384]{1,0:T(8,128)(2,1)S(1)} %collective-permute-done.16.refs_1_.refs_2_.refs_5_), channel_id=1, source_target_pairs={{1,0},{0,1},{3,2},{2,3},{5,4},{4,5},{7,6},{6,7},{9,8},{8,9},{11,10... | collective-permute-start | bytes 1769480 | tf_op jit(solution)/shard_map/ppermute | solution.py:480
  64.7 14.0 %collective-permute-start.18 = (bf16[1408,128]{1,0:T(8,128)(2,1)S(1)}, bf16[1408,128]{1,0:T(8,128)(2,1)S(1)}, u32[]{:S(2)}, u32[]{:S(2)}) collective-permute-start(bf16[1408,128]{1,0:T(8,128)(2,1)S(1)} %get-tuple-element.49.refs_3_), channel_id=1, source_target_pairs={{0,8},{2,10},{4,12},{6,14},{8,0},{10,2},{12,4},{14,6},{16,24},{18,... | collective-permute-start | bytes 1081352 | tf_op jit(solution)/shard_map/ppermute | solution.py:497
  67.6 11.1 %collective-permute-start.19 = (bf16[192,384]{1,0:T(8,128)(2,1)S(1)}, bf16[192,384]{1,0:T(8,128)(2,1)S(1)}, u32[]{:S(2)}, u32[]{:S(2)}) collective-permute-start(bf16[192,384]{1,0:T(8,128)(2,1)S(1)} %shard_map.54), channel_id=1, source_target_pairs={{16,0},{18,2},{20,4},{22,6},{24,8},{26,10},{28,12},{30,14},{17,1},... | collective-permute-start | bytes 442376 | tf_op jit(solution)/shard_map/ppermute | solution.py:497
  68.9 9.8 %collective-permute-start.15 = (bf16[1408,128]{1,0:T(8,128)(2,1)S(1)}, bf16[1408,128]{1,0:T(8,128)(2,1)S(1)}, u32[]{:S(2)}, u32[]{:S(2)}) collective-permute-start(bf16[1408,128]{1,0:T(8,128)(2,1)S(1)} %get-tuple-element.49.refs_3_), channel_id=1, source_target_pairs={{1,0},{0,1},{3,2},{2,3},{5,4},{4,5},{7,6},{6,7},{9,8},{8,9},{11,10... | collective-permute-start | bytes 1081352 | tf_op jit(solution)/shard_map/ppermute | solution.py:480
  78.7 1.7 %collective-permute-start.20 = (bf16[1408,128]{1,0:T(8,128)(2,1)S(1)}, bf16[1408,128]{1,0:T(8,128)(2,1)S(1)}, u32[]{:S(2)}, u32[]{:S(2)}) collective-permute-start(bf16[1408,128]{1,0:T(8,128)(2,1)S(1)} %collective-permute-done.18.refs_7_), channel_id=1, source_target_pairs={{1,0},{0,1},{3,2},{2,3},{5,4},{4,5},{7,6},{6,7},{9,8},{8,9},{11,10... | collective-permute-start | bytes 1081352 | tf_op jit(solution)/shard_map/ppermute | solution.py:480
  83.7 7.5 %collective-permute-start.27 = (bf16[192,384]{1,0:T(8,128)(2,1)S(1)}, bf16[192,384]{1,0:T(8,128)(2,1)S(1)}, u32[]{:S(2)}, u32[]{:S(2)}) collective-permute-start(bf16[192,384]{1,0:T(8,128)(2,1)S(1)} %collective-permute-done.19.refs_0_), channel_id=1, source_target_pairs={{0,6},{1,7},{2,4},{3,5},{4,2},{5,3},{6,0},{7,1},{8,14},{9,15},{10,... | collective-permute-start | bytes 442376 | tf_op jit(solution)/shard_map/ppermute | solution.py:491
  86.6 7.3 %collective-permute-start.26 = (bf16[192,384]{1,0:T(8,128)(2,1)S(1)}, bf16[192,384]{1,0:T(8,128)(2,1)S(1)}, u32[]{:S(2)}, u32[]{:S(2)}) collective-permute-start(bf16[192,384]{1,0:T(8,128)(2,1)S(1)} %collective-permute-done.19.refs_0_), channel_id=1, source_target_pairs={{0,4},{1,5},{2,6},{3,7},{4,0},{5,1},{6,2},{7,3},{8,12},{9,13},{10,... | collective-permute-start | bytes 442376 | tf_op jit(solution)/shard_map/ppermute | solution.py:491
  87.3 6.6 %collective-permute-start.25 = (bf16[192,384]{1,0:T(8,128)(2,1)S(1)}, bf16[192,384]{1,0:T(8,128)(2,1)S(1)}, u32[]{:S(2)}, u32[]{:S(2)}) collective-permute-start(bf16[192,384]{1,0:T(8,128)(2,1)S(1)} %collective-permute-done.19.refs_0_), channel_id=1, source_target_pairs={{0,2},{1,3},{2,0},{3,1},{4,6},{5,7},{6,4},{7,5},{8,10},{9,11},{10,... | collective-permute-start | bytes 442376 | tf_op jit(solution)/shard_map/ppermute | solution.py:491
  87.3 8.9 %collective-permute-start.21 = (bf16[352,128]{1,0:T(8,128)(2,1)S(1)}, bf16[352,128]{1,0:T(8,128)(2,1)S(1)}, u32[]{:S(2)}, u32[]{:S(2)}) collective-permute-start(bf16[352,128]{1,0:T(8,128)(2,1)S(1)} %get-tuple-element.56), channel_id=1, source_target_pairs={{16,0},{18,2},{20,4},{22,6},{24,8},{26,10},{28,12},{30,14},{17,1},... | collective-permute-start | bytes 270344 | tf_op jit(solution)/shard_map/ppermute | solution.py:497
  96.2 7.9 %collective-permute-start.28 = (bf16[768,384]{1,0:T(8,128)(2,1)S(1)}, bf16[768,384]{1,0:T(8,128)(2,1)S(1)}, u32[]{:S(2)}, u32[]{:S(2)}) collective-permute-start(bf16[768,384]{1,0:T(8,128)(2,1)S(1)} %shard_map.59.refs_1_), channel_id=1, source_target_pairs={{1,0},{0,1},{3,2},{2,3},{5,4},{4,5},{7,6},{6,7},{9,8},{8,9},{11,10... | collective-permute-start | bytes 1769480 | tf_op jit(solution)/shard_map/ppermute | solution.py:480
  96.2 6.0 %collective-permute-start.24 = (bf16[352,128]{1,0:T(8,128)(2,1)S(1)}, bf16[352,128]{1,0:T(8,128)(2,1)S(1)}, u32[]{:S(2)}, u32[]{:S(2)}) collective-permute-start(bf16[352,128]{1,0:T(8,128)(2,1)S(1)} %collective-permute-done.21.refs_0_), channel_id=1, source_target_pairs={{0,6},{1,7},{2,4},{3,5},{4,2},{5,3},{6,0},{7,1},{8,14},{9,15},{10,... | collective-permute-start | bytes 270344 | tf_op jit(solution)/shard_map/ppermute | solution.py:491
  98.7 5.3 %collective-permute-start.23 = (bf16[352,128]{1,0:T(8,128)(2,1)S(1)}, bf16[352,128]{1,0:T(8,128)(2,1)S(1)}, u32[]{:S(2)}, u32[]{:S(2)}) collective-permute-start(bf16[352,128]{1,0:T(8,128)(2,1)S(1)} %collective-permute-done.21.refs_0_), channel_id=1, source_target_pairs={{0,4},{1,5},{2,6},{3,7},{4,0},{5,1},{6,2},{7,3},{8,12},{9,13},{10,... | collective-permute-start | bytes 270344 | tf_op jit(solution)/shard_map/ppermute | solution.py:491
  99.3 4.7 %collective-permute-start.22 = (bf16[352,128]{1,0:T(8,128)(2,1)S(1)}, bf16[352,128]{1,0:T(8,128)(2,1)S(1)}, u32[]{:S(2)}, u32[]{:S(2)}) collective-permute-start(bf16[352,128]{1,0:T(8,128)(2,1)S(1)} %collective-permute-done.21.refs_0_), channel_id=1, source_target_pairs={{0,2},{1,3},{2,0},{3,1},{4,6},{5,7},{6,4},{7,5},{8,10},{9,11},{10,... | collective-permute-start | bytes 270344 | tf_op jit(solution)/shard_map/ppermute | solution.py:491
  105.8 1.7 %collective-permute-start.29 = (bf16[1408,128]{1,0:T(8,128)(2,1)S(1)}, bf16[1408,128]{1,0:T(8,128)(2,1)S(1)}, u32[]{:S(2)}, u32[]{:S(2)}) collective-permute-start(bf16[1408,128]{1,0:T(8,128)(2,1)S(1)} %shard_map.58.refs_3_), channel_id=1, source_target_pairs={{1,0},{0,1},{3,2},{2,3},{5,4},{4,5},{7,6},{6,7},{9,8},{8,9},{11,10... | collective-permute-start | bytes 1081352 | tf_op jit(solution)/shard_map/ppermute | solution.py:480
  (2 other events, 3.4 us)

commit v3 on v2

--- a/solution.py
+++ b/solution.py
@@ -262,10 +262,10 @@
 
 
 def group_cov_kernel(n, *refs):
-    ins, *blocks, outs, scratch = split(refs, 5, n, n, n, n, 3, 4)
+    ins, *blocks, outs, scratch = split(refs, 5, n, n, n, n, 4, 3)
     base, c, c_t, c01, c01_t = ins
-    mine, agg, agg_bf = outs
-    sent, s, s23, sems = scratch
+    agg, agg_bf, s3, s23 = outs
+    sent, s, sems = scratch
     hi, lo, q = where_am_i()
     group_start(blocks, sent, sems, lo, q, (3, 2, 1, 0))
     group_wait(blocks[0], sent, sems, 3)
@@ -293,6 +293,11 @@
     agg[...] += sandwich(s[1], c[0, q], c_t[0])
     agg[...] += sandwich(s23[...], c01[q], c01_t[...])
     pack(agg, agg_bf, q, n)
+    s3[...] = s[3]
+
+
+def group_mine_kernel(base, agg, s3, s23, c, c_t, mine):
+    hi, lo, q = where_am_i()
 
     @pl.when(lo == 0)
     def _():
@@ -304,7 +309,7 @@
 
     @pl.when(lo == 2)
     def _():
-        mine[...] = base[...] + sandwich(s[3], c[2, q], c_t[2])
+        mine[...] = base[...] + sandwich(s3[...], c[2, q], c_t[2])
 
     @pl.when(lo == 3)
     def _():
@@ -503,8 +508,8 @@
     return [x] + [swap(x, mask, mask) for mask in range(1, GROUP)]
 
 
-def joined(x):
-    quarters = in_group(x)
+def joined(x, *earlier):
+    quarters = lax.optimization_barrier((*in_group(x), *earlier))[:GROUP]
     rows, lanes = x.shape
     whole_panel = jax.ShapeDtypeStruct((rows * GROUP, lanes), x.dtype)
     return call(join_kernel, quarters, [VMEM] * GROUP, [whole_panel], [], 0)[0]
@@ -551,8 +556,9 @@
     )
     s_first = swap(base_bf, 1, 2)
     c_diag = swap(after(c_first, s_first), 2, 1)
+    s_second = swap(base_bf, 2, 1)
+    c_diag = after(c_diag, s_second)
     c_pieces = [p for v in (c_first, c_second, c_diag) for p in over_panels(v)]
-    s_second = swap(base_bf, 2, 1)
     c_all, c01, c23, agg_c = call(
         functools.partial(group_comp_kernel, n),
         c_own + c_pieces,
@@ -574,25 +580,32 @@
     s_diag = after(swap(s_first, 2, 1), agg_panel)
     s_own = over_panels(base_bf)
     s_pieces = s_own + [p for v in (s_first, s_second, s_diag) for p in over_panels(v)]
-    cov, agg, agg_bf = call(
+    agg, agg_bf, s3, s23 = call(
         functools.partial(group_cov_kernel, n),
         [base, c_all, c_t, c01, c01_t, *s_pieces],
         [VMEM] * 5 + [ANY] * (GROUP * n),
-        [panel_f32, panel_f32, packed_bf],
+        [panel_f32, packed_bf, square_bf, square_bf],
         [
             pltpu.VMEM((GROUP, n, rows, lanes), BF),
             pltpu.VMEM((GROUP, nb, nb), BF),
-            square_scratch,
             sems((GROUP, n)),
         ],
-        (2 * n + 6) * one,
+        (2 * n + 4) * one,
+    )
+    (cov,) = call(
+        group_mine_kernel,
+        [base, agg, s3, s23, c_all, c_t],
+        [VMEM] * 6,
+        [panel_f32],
+        [],
+        2 * one,
     )
     out_cov = jax.ShapeDtypeStruct((1, nb, w), F32)
     out_comp = jax.ShapeDtypeStruct((1, nb, w), BF)
     panel_scratch = pltpu.VMEM((nb, w), BF)
     sum_scratch = pltpu.VMEM((nb, w), F32)
     c_parts = over_panels(after(c_got, agg_bf))
-    s_got = across(after(agg_bf, c_got), 0, levels == 1)
+    s_got = across(agg_bf, 0, levels == 1)
     for bit in range(levels):
         last = bit + 1 == levels
         to_last = bit + 2 == levels
@@ -659,19 +672,19 @@
             2 * one,
         )
         s_send, right = outs[:2]
+        s_far = across(s_send, bit + 1, to_last)
         (cov,) = call(
             functools.partial(mine_cov_kernel, n, bit),
-            [cov, mine, mine_t, right],
+            [after(cov, s_far), mine, mine_t, right],
             [VMEM] * 4,
             [panel_f32],
             [],
-            2 * one,
+            20 * one,
         )
         if not to_last:
             agg, agg_bf = outs[2:]
             agg_c, agg_t = new_agg_c, new_agg_t
-        s_far = across(s_send, bit + 1, to_last)
-        c_parts = over_panels(after(joined(after(c_far, cov)), s_far))
+        c_parts = over_panels(joined(after(c_far, s_send), cov))
         s_got = joined(s_far)
         mine, mine_t = new_mine, new_mine_t
     return cov, prop

time: 110 us -> 107 us (0.973)
  waiting for transfers between devices: 52.5 us -> 49.3 us
    ppermute x4, waiting for transfers between devices: 15.3 us -> 13.4 us  [across(): lax.ppermute(x, 'tm', [(t, t ^ d) for t in range(steps) if t ^ d < steps...]
    ppermute x12, waiting for transfers between devices: 33.2 us -> 31.5 us  [swap(): return lax.ppermute(value, ('tm', 'panel'), pairs)]
    pallas_call x12 -> x13, Pallas kernels: 26.3 us -> 26 us  [call(): pl.pallas_call(kernel, in_specs=in_specs, out_specs=[VMEM] * len(outs), o...]
  transfers between devices with their start and end apart: 30 -> 30, of which waited for: 15 -> 16; matrix products, arithmetic and copies ran while one was open for 0% -> 0% of each run, Pallas kernels for 17% -> 19%
where the time goes in v3:
time: 107 us; the launch traced here: 106 us
  waiting for transfers between devices  49.3 us (46%)
  starting transfers between devices  28.3 us (26%)
  Pallas kernels  26 us (24%)
  other arithmetic  1.55 us (1%)
    ppermute x12, waiting for transfers between devices, swap(): return lax.ppermute(value, ('tm', 'panel'), pairs)  31.5 us
    pallas_call x13, Pallas kernels, call(): pl.pallas_call(kernel, in_specs=in_specs, out_specs=[VMEM] * len(outs), o...  26 us
    ppermute x12, starting transfers between devices, swap(): return lax.ppermute(value, ('tm', 'panel'), pairs)  20.6 us
    ppermute x4, waiting for transfers between devices, across(): lax.ppermute(x, 'tm', [(t, t ^ d) for t in range(steps) if t ^ d < steps...  13.4 us
    ppermute x4, starting transfers between devices, across(): lax.ppermute(x, 'tm', [(t, t ^ d) for t in range(steps) if t ^ d < steps...  5.73 us
    ppermute x14, waiting for transfers between devices, over_panels(): lax.ppermute(x, 'panel', [((i + r) % n, i) for i in range(n)])  4.36 us
  transfers between devices with their start and end apart: 30, of which 16 were waited for; matrix products, arithmetic and copies ran while one was open for 0% of the time, Pallas kernels for 19%

profile of v3, /device:TPU:0, one launch (start us, length us, event | category | flops | bytes accessed | tf_op | source)
XLA Modules:
  0.0 106.2 jit_solution(33418086650314505)
XLA Ops:
  0.6 1.5 %convert_bitcast_fusion.refs_4_.refs_0_ = bf16[768,384]{1,0:T(8,128)(2,1)S(1)} fusion(f32[1,768,384]{2,1,0:T(8,128)} %param.4), kind=kLoop, calls=%fused_computation.1 | loop fusion | flops 294912 | bytes 1769472 | tf_op jit(solution)/shard_map/convert_element_type | solution.py:543
  2.9 2.9 %collective-permute-start.2 = (bf16[768,384]{1,0:T(8,128)(2,1)S(1)}, bf16[768,384]{1,0:T(8,128)(2,1)}, u32[]{:S(2)}, u32[]{:S(2)}) collective-permute-start(bf16[768,384]{1,0:T(8,128)(2,1)S(1)} %convert_bitcast_fusion.refs_4_.refs_0_), channel_id=1, source_target_pairs={{0,4},{1,3},{2,6},{3,1},{4,0},{5,7},{6,2},{7,5},{8,12},{9,11},{10,... | collective-permute-start | bytes 1769480 | tf_op jit(solution)/shard_map/ppermute | solution.py:496
  5.9 1.7 %shard_map.50 = (f32[768,384]{1,0:T(8,128)S(1)}, bf16[1408,128]{1,0:T(8,128)(2,1)S(1)}) custom-call(f32[768,384]{1,0:T(8,128)S(1)} %bitcast.6, f32[768,768]{1,0:T(8,128)S(1)} %copy-done.1, bf16[768,384]{1,0:T(8,128)(2,1)S(1)} %convert_element_type.10.refs_2_, bf16[768,384]{1,0:T(8,128)(2,1)S(1)} %collective-permute-done.refs_3_, ...), custom_call_target="tpu_custom_call" | custom-call | flops 905969664 | bytes 7438336 | tf_op jit(solution)/shard_map/pallas_call | solution.py:174
  7.6 2.4 %collective-permute-start.6 = (bf16[1408,128]{1,0:T(8,128)(2,1)S(1)}, bf16[1408,128]{1,0:T(8,128)(2,1)S(1)}, u32[]{:S(2)}, u32[]{:S(2)}) collective-permute-start(bf16[1408,128]{1,0:T(8,128)(2,1)S(1)} %get-tuple-element.42.refs_5_), channel_id=1, source_target_pairs={{0,4},{1,3},{2,6},{3,1},{4,0},{5,7},{6,2},{7,5},{8,12},{9,11},{10,... | collective-permute-start | bytes 1081352 | tf_op jit(solution)/shard_map/ppermute | solution.py:496
  10.0 1.5 %collective-permute-start.4 = (bf16[768,384]{1,0:T(8,128)(2,1)S(1)}, bf16[768,384]{1,0:T(8,128)(2,1)}, u32[]{:S(2)}, u32[]{:S(2)}) collective-permute-start(bf16[768,384]{1,0:T(8,128)(2,1)S(1)} %convert_bitcast_fusion.refs_4_.refs_0_), channel_id=1, source_target_pairs={{0,2},{1,5},{2,0},{3,7},{4,6},{5,1},{6,4},{7,3},{8,10},{9,13},{10,... | collective-permute-start | bytes 1769480 | tf_op jit(solution)/shard_map/ppermute | solution.py:496
  11.5 3.5 %collective-permute-done.2.refs_2_ = bf16[768,384]{1,0:T(8,128)(2,1)} collective-permute-done((bf16[768,384]{1,0:T(8,128)(2,1)S(1)}, bf16[768,384]{1,0:T(8,128)(2,1)}, u32[]{:S(2)}, u32[]{:S(2)}) %collective-permute-start.2) | collective-permute-done | bytes 589856 | tf_op jit(solution)/shard_map/ppermute | solution.py:496
  15.1 7.7 %collective-permute-done.6.refs_7_ = bf16[1408,128]{1,0:T(8,128)(2,1)S(1)} collective-permute-done((bf16[1408,128]{1,0:T(8,128)(2,1)S(1)}, bf16[1408,128]{1,0:T(8,128)(2,1)S(1)}, u32[]{:S(2)}, u32[]{:S(2)}) %collective-permute-start.6) | collective-permute-done | bytes 360480 | tf_op jit(solution)/shard_map/ppermute | solution.py:496
  22.7 3.2 %collective-permute-start.7 = (bf16[768,384]{1,0:T(8,128)(2,1)}, bf16[768,384]{1,0:T(8,128)(2,1)}, u32[]{:S(2)}, u32[]{:S(2)}) collective-permute-start(bf16[768,384]{1,0:T(8,128)(2,1)} %collective-permute-done.2.refs_2_), channel_id=1, source_target_pairs={{0,2},{1,5},{2,0},{3,7},{4,6},{5,1},{6,4},{7,3},{8,10},{9,13},{10,... | collective-permute-start | bytes 1769480 | tf_op jit(solution)/shard_map/ppermute | solution.py:496
  26.5 11.4 %collective-permute-done.8.refs_9_ = bf16[1408,128]{1,0:T(8,128)(2,1)S(1)} collective-permute-done((bf16[1408,128]{1,0:T(8,128)(2,1)S(1)}, bf16[1408,128]{1,0:T(8,128)(2,1)S(1)}, u32[]{:S(2)}, u32[]{:S(2)}) %collective-permute-start.8) | collective-permute-done | bytes 360480 | tf_op jit(solution)/shard_map/ppermute | solution.py:496
  38.4 2.0 %collective-permute-start.13 = (bf16[1408,128]{1,0:T(8,128)(2,1)S(1)}, bf16[1408,128]{1,0:T(8,128)(2,1)S(1)}, u32[]{:S(2)}, u32[]{:S(2)}) collective-permute-start(bf16[1408,128]{1,0:T(8,128)(2,1)S(1)} %collective-permute-done.6.refs_7_), channel_id=1, source_target_pairs={{0,2},{1,5},{2,0},{3,7},{4,6},{5,1},{6,4},{7,3},{8,10},{9,13},{10,... | collective-permute-start | bytes 1081352 | tf_op jit(solution)/shard_map/ppermute | solution.py:496
  41.0 4.5 %shard_map.51 = (bf16[4,2,768,384]{3,2,1,0:T(8,128)(2,1)S(1)}, bf16[2,768,384]{2,1,0:T(8,128)(2,1)S(1)}, bf16[768,768]{1,0:T(8,128)(2,1)S(1)}, bf16[2,768,384]{2,1,0:T(8,128)(2,1)S(1)}) custom-call(bf16[768,384]{1,0:T(8,128)(2,1)S(1)} %convert_bitcast_fusion.refs_4_.refs_0_, bf16[768,384]{1,0:T(8,128)(2,1)S(1)} %collective-permute-done.1.refs_5_.refs_1_, ...), custom_call_target="tpu_custom_call" | custom-call | flops 2717908992 | bytes 12976128 | tf_op jit(solution)/shard_map/pallas_call | solution.py:174
  45.8 1.6 %collective-permute-start.16 = (bf16[768,384]{1,0:T(8,128)(2,1)S(1)}, bf16[768,384]{1,0:T(8,128)(2,1)S(1)}, u32[]{:S(2)}, u32[]{:S(2)}) collective-permute-start(bf16[768,384]{1,0:T(8,128)(2,1)S(1)} %dynamic-slice_bitcast_fusion), channel_id=1, source_target_pairs={{0,8},{2,10},{4,12},{6,14},{8,0},{10,2},{12,4},{14,6},{16,24},{18,... | collective-permute-start | bytes 1769480 | tf_op jit(solution)/shard_map/ppermute | solution.py:502
  47.4 1.8 %shard_map.52 = (bf16[3,768,768]{2,1,0:T(8,128)(2,1)S(1)}, bf16[768,768]{1,0:T(8,128)(2,1)S(1)}, bf16[2,768,384]{2,1,0:T(8,128)(2,1)S(1)}, bf16[768,768]{1,0:T(8,128)(2,1)S(1)}, bf16[768,768]{1,0:T(8,128)(2,1)S(1)}) custom-call(bf16[4,2,768,384]{3,2,1,0:T(8,128)(2,1)S(1)} %get-tuple-element.45.c.refs_1_, ...), custom_call_target="tpu_custom_call" | custom-call | flops 905969664 | bytes 16515072 | tf_op jit(solution)/shard_map/pallas_call | solution.py:174
  49.2 7.5 %shard_map.53 = (f32[768,384]{1,0:T(8,128)S(1)}, bf16[1408,128]{1,0:T(8,128)(2,1)S(1)}, bf16[768,768]{1,0:T(8,128)(2,1)S(1)}, bf16[768,768]{1,0:T(8,128)(2,1)S(1)}) custom-call(f32[768,384]{1,0:T(8,128)S(1)} %get-tuple-element.41.refs_0_.base, bf16[4,2,768,384]{3,2,1,0:T(8,128)(2,1)S(1)} %get-tuple-element.45.c.refs_1_, ...), custom_call_target="tpu_custom_call" | custom-call | flops 3623878656 | bytes 18579456 | tf_op jit(solution)/shard_map/pallas_call | solution.py:174
  56.7 4.8 %collective-permute-done.16.refs_1_.refs_2_.refs_5_ = bf16[768,384]{1,0:T(8,128)(2,1)S(1)} collective-permute-done((bf16[768,384]{1,0:T(8,128)(2,1)S(1)}, bf16[768,384]{1,0:T(8,128)(2,1)S(1)}, u32[]{:S(2)}, u32[]{:S(2)}) %collective-permute-start.16) | collective-permute-done | bytes 589856 | tf_op jit(solution)/shard_map/ppermute | solution.py:502
  61.5 1.6 %collective-permute-start.18 = (bf16[1408,128]{1,0:T(8,128)(2,1)S(1)}, bf16[1408,128]{1,0:T(8,128)(2,1)S(1)}, u32[]{:S(2)}, u32[]{:S(2)}) collective-permute-start(bf16[1408,128]{1,0:T(8,128)(2,1)S(1)} %get-tuple-element.56.refs_3_), channel_id=1, source_target_pairs={{0,8},{2,10},{4,12},{6,14},{8,0},{10,2},{12,4},{14,6},{16,24},{18,... | collective-permute-start | bytes 1081352 | tf_op jit(solution)/shard_map/ppermute | solution.py:502
  65.9 1.8 %shard_map.56 = (bf16[2,768,384]{2,1,0:T(8,128)(2,1)S(1)}, bf16[768,768]{1,0:T(8,128)(2,1)S(1)}) custom-call(bf16[2,768,384]{2,1,0:T(8,128)(2,1)S(1)} %get-tuple-element.60.refs_0_.mine, bf16[768,768]{1,0:T(8,128)(2,1)S(1)} %get-tuple-element.61.refs_1_.mine_t, bf16[768,384]{1,0:T(8,128)(2,1)S(1)} %collective-permute-done.16.refs_1_.refs_2_.refs_5_, ...), custom_call_target="tpu_custom_call" | custom-call | flops 905969664 | bytes 5898240 | tf_op jit(solution)/shard_map/pallas_call | solution.py:174
  67.7 7.8 %collective-permute-done.18.refs_7_ = bf16[1408,128]{1,0:T(8,128)(2,1)S(1)} collective-permute-done((bf16[1408,128]{1,0:T(8,128)(2,1)S(1)}, bf16[1408,128]{1,0:T(8,128)(2,1)S(1)}, u32[]{:S(2)}, u32[]{:S(2)}) %collective-permute-start.18) | collective-permute-done | bytes 360480 | tf_op jit(solution)/shard_map/ppermute | solution.py:502
  75.5 1.7 %collective-permute-done.20.refs_8_ = bf16[1408,128]{1,0:T(8,128)(2,1)S(1)} collective-permute-done((bf16[1408,128]{1,0:T(8,128)(2,1)S(1)}, bf16[1408,128]{1,0:T(8,128)(2,1)S(1)}, u32[]{:S(2)}, u32[]{:S(2)}) %collective-permute-start.20) | collective-permute-done | bytes 360480 | tf_op jit(solution)/shard_map/ppermute | solution.py:485
  77.2 1.7 %shard_map.57 = (bf16[352,128]{1,0:T(8,128)(2,1)S(1)}, bf16[768,768]{1,0:T(8,128)(2,1)S(1)}) custom-call(f32[768,384]{1,0:T(8,128)S(1)} %get-tuple-element.52.agg.refs_0_, bf16[2,768,384]{2,1,0:T(8,128)(2,1)S(1)} %get-tuple-element.58.agg.refs_0_.refs_1_, bf16[768,768]{1,0:T(8,128)(2,1)S(1)} %get-tuple-element.55.refs_2_, ...), custom_call_target="tpu_custom_call" | custom-call | flops 905969664 | bytes 7430144 | tf_op jit(solution)/shard_map/pallas_call | solution.py:174
  78.9 1.3 %collective-permute-start.21 = (bf16[352,128]{1,0:T(8,128)(2,1)S(1)}, bf16[352,128]{1,0:T(8,128)(2,1)S(1)}, u32[]{:S(2)}, u32[]{:S(2)}) collective-permute-start(bf16[352,128]{1,0:T(8,128)(2,1)S(1)} %get-tuple-element.64), channel_id=1, source_target_pairs={{16,0},{18,2},{20,4},{22,6},{24,8},{26,10},{28,12},{30,14},{17,1},... | collective-permute-start | bytes 270344 | tf_op jit(solution)/shard_map/ppermute | solution.py:502
  80.6 3.3 %collective-permute-start.27 = (bf16[192,384]{1,0:T(8,128)(2,1)S(1)}, bf16[192,384]{1,0:T(8,128)(2,1)S(1)}, u32[]{:S(2)}, u32[]{:S(2)}) collective-permute-start(bf16[192,384]{1,0:T(8,128)(2,1)S(1)} %collective-permute-done.19.refs_0_), channel_id=1, source_target_pairs={{0,6},{1,7},{2,4},{3,5},{4,2},{5,3},{6,0},{7,1},{8,14},{9,15},{10,... | collective-permute-start | bytes 442376 | tf_op jit(solution)/shard_map/ppermute | solution.py:496
  83.9 1.7 %collective-permute-start.26 = (bf16[192,384]{1,0:T(8,128)(2,1)S(1)}, bf16[192,384]{1,0:T(8,128)(2,1)S(1)}, u32[]{:S(2)}, u32[]{:S(2)}) collective-permute-start(bf16[192,384]{1,0:T(8,128)(2,1)S(1)} %collective-permute-done.19.refs_0_), channel_id=1, source_target_pairs={{0,4},{1,5},{2,6},{3,7},{4,0},{5,1},{6,2},{7,3},{8,12},{9,13},{10,... | collective-permute-start | bytes 442376 | tf_op jit(solution)/shard_map/ppermute | solution.py:496
  86.4 1.4 %shard_map.58.refs_0_ = f32[768,384]{1,0:T(8,128)S(1)} custom-call(f32[768,384]{1,0:T(8,128)S(1)} %shard_map.54.cov, bf16[2,768,384]{2,1,0:T(8,128)(2,1)S(1)} %get-tuple-element.60.refs_0_.mine, bf16[768,768]{1,0:T(8,128)(2,1)S(1)} %get-tuple-element.61.refs_1_.mine_t, bf16[768,768]{1,0:T(8,128)(2,1)S(1)} %get-tuple-element.66.right), custom_call_target="tpu_custom_call" | custom-call | flops 9059696640 | bytes 5898240 | tf_op jit(solution)/shard_map/pallas_call | solution.py:174
  88.5 2.7 %collective-permute-done.26.refs_2_ = bf16[192,384]{1,0:T(8,128)(2,1)S(1)} collective-permute-done((bf16[192,384]{1,0:T(8,128)(2,1)S(1)}, bf16[192,384]{1,0:T(8,128)(2,1)S(1)}, u32[]{:S(2)}, u32[]{:S(2)}) %collective-permute-start.26) | collective-permute-done | bytes 147488 | tf_op jit(solution)/shard_map/ppermute | solution.py:496
  92.4 2.0 %collective-permute-start.24 = (bf16[352,128]{1,0:T(8,128)(2,1)S(1)}, bf16[352,128]{1,0:T(8,128)(2,1)S(1)}, u32[]{:S(2)}, u32[]{:S(2)}) collective-permute-start(bf16[352,128]{1,0:T(8,128)(2,1)S(1)} %collective-permute-done.21.refs_0_), channel_id=1, source_target_pairs={{0,6},{1,7},{2,4},{3,5},{4,2},{5,3},{6,0},{7,1},{8,14},{9,15},{10,... | collective-permute-start | bytes 270344 | tf_op jit(solution)/shard_map/ppermute | solution.py:496
  94.3 1.3 %collective-permute-start.23 = (bf16[352,128]{1,0:T(8,128)(2,1)S(1)}, bf16[352,128]{1,0:T(8,128)(2,1)S(1)}, u32[]{:S(2)}, u32[]{:S(2)}) collective-permute-start(bf16[352,128]{1,0:T(8,128)(2,1)S(1)} %collective-permute-done.21.refs_0_), channel_id=1, source_target_pairs={{0,4},{1,5},{2,6},{3,7},{4,0},{5,1},{6,2},{7,3},{8,12},{9,13},{10,... | collective-permute-start | bytes 270344 | tf_op jit(solution)/shard_map/ppermute | solution.py:496
  95.9 2.5 %collective-permute-done.24.refs_3_ = bf16[352,128]{1,0:T(8,128)(2,1)S(1)} collective-permute-done((bf16[352,128]{1,0:T(8,128)(2,1)S(1)}, bf16[352,128]{1,0:T(8,128)(2,1)S(1)}, u32[]{:S(2)}, u32[]{:S(2)}) %collective-permute-start.24) | collective-permute-done | bytes 90144 | tf_op jit(solution)/shard_map/ppermute | solution.py:496
  98.4 1.8 %collective-permute-done.23.refs_2_ = bf16[352,128]{1,0:T(8,128)(2,1)S(1)} collective-permute-done((bf16[352,128]{1,0:T(8,128)(2,1)S(1)}, bf16[352,128]{1,0:T(8,128)(2,1)S(1)}, u32[]{:S(2)}, u32[]{:S(2)}) %collective-permute-start.23) | collective-permute-done | bytes 90144 | tf_op jit(solution)/shard_map/ppermute | solution.py:496
  100.3 1.7 %shard_map.61 = bf16[1,768,384]{2,1,0:T(8,128)(2,1)} custom-call(bf16[2,768,384]{2,1,0:T(8,128)(2,1)S(1)} %get-tuple-element.62.refs_0_.refs_1_, bf16[768,384]{1,0:T(8,128)(2,1)S(1)} %shard_map.60.refs_1_, bf16[768,384]{1,0:T(8,128)(2,1)S(1)} %collective-permute-done.28.refs_2_), custom_call_target="tpu_custom_call" | custom-call | flops 452984832 | bytes 2949120 | tf_op jit(solution)/shard_map/pallas_call | solution.py:174
  102.1 1.6 %collective-permute-done.29.refs_4_ = bf16[1408,128]{1,0:T(8,128)(2,1)S(1)} collective-permute-done((bf16[1408,128]{1,0:T(8,128)(2,1)S(1)}, bf16[1408,128]{1,0:T(8,128)(2,1)S(1)}, u32[]{:S(2)}, u32[]{:S(2)}) %collective-permute-start.29) | collective-permute-done | bytes 360480 | tf_op jit(solution)/shard_map/ppermute | solution.py:485
  103.7 2.5 %shard_map.62 = f32[1,768,384]{2,1,0:T(8,128)} custom-call(f32[768,384]{1,0:T(8,128)S(1)} %shard_map.58.refs_0_, bf16[2,768,384]{2,1,0:T(8,128)(2,1)S(1)} %get-tuple-element.62.refs_0_.refs_1_, bf16[768,768]{1,0:T(8,128)(2,1)S(1)} %get-tuple-element.67.refs_2_, bf16[1408,128]{1,0:T(8,128)(2,1)S(1)} %shard_map.59.refs_3_, ...), custom_call_target="tpu_custom_call" | custom-call | flops 905969664 | bytes 5439488 | tf_op jit(solution)/shard_map/pallas_call | solution.py:174
  (48 shorter events, 9.0 us)
Async XLA Ops:
  0.6 1.6 %copy-start = (f32[1,768,384]{2,1,0:T(8,128)S(1)}, f32[1,768,384]{2,1,0:T(8,128)}, u32[]{:S(2)}) copy-start(f32[1,768,384]{2,1,0:T(8,128)} %param.3) | copy-start | bytes 3538948
  0.6 5.2 %copy-start.1 = (f32[768,768]{1,0:T(8,128)S(1)}, f32[768,768]{1,0:T(8,128)}, u32[]{:S(2)}) copy-start(f32[768,768]{1,0:T(8,128)} %refs_1_.1) | copy-start | bytes 7077892
  2.3 3.5 %collective-permute-start = (bf16[768,384]{1,0:T(8,128)(2,1)S(1)}, bf16[768,384]{1,0:T(8,128)(2,1)S(1)}, u32[]{:S(2)}, u32[]{:S(2)}) collective-permute-start(bf16[768,384]{1,0:T(8,128)(2,1)S(1)} %convert_element_type.10.refs_2_), channel_id=1, source_target_pairs={{1,0},{0,1},{3,2},{2,3},{5,4},{4,5},{7,6},{6,7},{9,8},{8,9},{11,10... | collective-permute-start | bytes 1769480 | tf_op jit(solution)/shard_map/ppermute | solution.py:485
  2.8 3.0 %collective-permute-start.1 = (bf16[768,384]{1,0:T(8,128)(2,1)S(1)}, bf16[768,384]{1,0:T(8,128)(2,1)S(1)}, u32[]{:S(2)}, u32[]{:S(2)}) collective-permute-start(bf16[768,384]{1,0:T(8,128)(2,1)S(1)} %convert_bitcast_fusion.refs_4_.refs_0_), channel_id=1, source_target_pairs={{1,0},{0,1},{3,2},{2,3},{5,4},{4,5},{7,6},{6,7},{9,8},{8,9},{11,10... | collective-permute-start | bytes 1769480 | tf_op jit(solution)/shard_map/ppermute | solution.py:485
  2.9 12.1 %collective-permute-start.2 = (bf16[768,384]{1,0:T(8,128)(2,1)S(1)}, bf16[768,384]{1,0:T(8,128)(2,1)}, u32[]{:S(2)}, u32[]{:S(2)}) collective-permute-start(bf16[768,384]{1,0:T(8,128)(2,1)S(1)} %convert_bitcast_fusion.refs_4_.refs_0_), channel_id=1, source_target_pairs={{0,4},{1,3},{2,6},{3,1},{4,0},{5,7},{6,2},{7,5},{8,12},{9,11},{10,... | collective-permute-start | bytes 1769480 | tf_op jit(solution)/shard_map/ppermute | solution.py:496
  7.6 15.1 %collective-permute-start.6 = (bf16[1408,128]{1,0:T(8,128)(2,1)S(1)}, bf16[1408,128]{1,0:T(8,128)(2,1)S(1)}, u32[]{:S(2)}, u32[]{:S(2)}) collective-permute-start(bf16[1408,128]{1,0:T(8,128)(2,1)S(1)} %get-tuple-element.42.refs_5_), channel_id=1, source_target_pairs={{0,4},{1,3},{2,6},{3,1},{4,0},{5,7},{6,2},{7,5},{8,12},{9,11},{10,... | collective-permute-start | bytes 1081352 | tf_op jit(solution)/shard_map/ppermute | solution.py:496
  10.0 15.9 %collective-permute-start.4 = (bf16[768,384]{1,0:T(8,128)(2,1)S(1)}, bf16[768,384]{1,0:T(8,128)(2,1)}, u32[]{:S(2)}, u32[]{:S(2)}) collective-permute-start(bf16[768,384]{1,0:T(8,128)(2,1)S(1)} %convert_bitcast_fusion.refs_4_.refs_0_), channel_id=1, source_target_pairs={{0,2},{1,5},{2,0},{3,7},{4,6},{5,1},{6,4},{7,3},{8,10},{9,13},{10,... | collective-permute-start | bytes 1769480 | tf_op jit(solution)/shard_map/ppermute | solution.py:496
  22.7 15.1 %collective-permute-start.7 = (bf16[768,384]{1,0:T(8,128)(2,1)}, bf16[768,384]{1,0:T(8,128)(2,1)}, u32[]{:S(2)}, u32[]{:S(2)}) collective-permute-start(bf16[768,384]{1,0:T(8,128)(2,1)} %collective-permute-done.2.refs_2_), channel_id=1, source_target_pairs={{0,2},{1,5},{2,0},{3,7},{4,6},{5,1},{6,4},{7,3},{8,10},{9,13},{10,... | collective-permute-start | bytes 1769480 | tf_op jit(solution)/shard_map/ppermute | solution.py:496
  25.9 11.9 %collective-permute-start.8 = (bf16[1408,128]{1,0:T(8,128)(2,1)S(1)}, bf16[1408,128]{1,0:T(8,128)(2,1)S(1)}, u32[]{:S(2)}, u32[]{:S(2)}) collective-permute-start(bf16[1408,128]{1,0:T(8,128)(2,1)S(1)} %get-tuple-element.42.refs_5_), channel_id=1, source_target_pairs={{0,2},{1,5},{2,0},{3,7},{4,6},{5,1},{6,4},{7,3},{8,10},{9,13},{10,... | collective-permute-start | bytes 1081352 | tf_op jit(solution)/shard_map/ppermute | solution.py:496
  25.9 14.4 %collective-permute-start.3 = (bf16[768,384]{1,0:T(8,128)(2,1)}, bf16[768,384]{1,0:T(8,128)(2,1)}, u32[]{:S(2)}, u32[]{:S(2)}) collective-permute-start(bf16[768,384]{1,0:T(8,128)(2,1)} %collective-permute-done.2.refs_2_), channel_id=1, source_target_pairs={{1,0},{0,1},{3,2},{2,3},{5,4},{4,5},{7,6},{6,7},{9,8},{8,9},{11,10... | collective-permute-start | bytes 1769480 | tf_op jit(solution)/shard_map/ppermute | solution.py:485
  25.9 12.4 %collective-permute-start.5 = (bf16[768,384]{1,0:T(8,128)(2,1)}, bf16[768,384]{1,0:T(8,128)(2,1)}, u32[]{:S(2)}, u32[]{:S(2)}) collective-permute-start(bf16[768,384]{1,0:T(8,128)(2,1)} %collective-permute-done.4.refs_4_), channel_id=1, source_target_pairs={{1,0},{0,1},{3,2},{2,3},{5,4},{4,5},{7,6},{6,7},{9,8},{8,9},{11,10... | collective-permute-start | bytes 1769480 | tf_op jit(solution)/shard_map/ppermute | solution.py:485
  37.8 3.2 %collective-permute-start.9 = (bf16[768,384]{1,0:T(8,128)(2,1)}, bf16[768,384]{1,0:T(8,128)(2,1)}, u32[]{:S(2)}, u32[]{:S(2)}) collective-permute-start(bf16[768,384]{1,0:T(8,128)(2,1)} %collective-permute-done.7.refs_6_), channel_id=1, source_target_pairs={{1,0},{0,1},{3,2},{2,3},{5,4},{4,5},{7,6},{6,7},{9,8},{8,9},{11,10... | collective-permute-start | bytes 1769480 | tf_op jit(solution)/shard_map/ppermute | solution.py:485
  37.8 11.3 %collective-permute-start.10 = (bf16[1408,128]{1,0:T(8,128)(2,1)S(1)}, bf16[1408,128]{1,0:T(8,128)(2,1)S(1)}, u32[]{:S(2)}, u32[]{:S(2)}) collective-permute-start(bf16[1408,128]{1,0:T(8,128)(2,1)S(1)} %get-tuple-element.42.refs_5_), channel_id=1, source_target_pairs={{1,0},{0,1},{3,2},{2,3},{5,4},{4,5},{7,6},{6,7},{9,8},{8,9},{11,10... | collective-permute-start | bytes 1081352 | tf_op jit(solution)/shard_map/ppermute | solution.py:485
  38.4 10.8 %collective-permute-start.12 = (bf16[1408,128]{1,0:T(8,128)(2,1)S(1)}, bf16[1408,128]{1,0:T(8,128)(2,1)S(1)}, u32[]{:S(2)}, u32[]{:S(2)}) collective-permute-start(bf16[1408,128]{1,0:T(8,128)(2,1)S(1)} %collective-permute-done.8.refs_9_), channel_id=1, source_target_pairs={{1,0},{0,1},{3,2},{2,3},{5,4},{4,5},{7,6},{6,7},{9,8},{8,9},{11,10... | collective-permute-start | bytes 1081352 | tf_op jit(solution)/shard_map/ppermute | solution.py:485
  38.4 7.4 %collective-permute-start.13 = (bf16[1408,128]{1,0:T(8,128)(2,1)S(1)}, bf16[1408,128]{1,0:T(8,128)(2,1)S(1)}, u32[]{:S(2)}, u32[]{:S(2)}) collective-permute-start(bf16[1408,128]{1,0:T(8,128)(2,1)S(1)} %collective-permute-done.6.refs_7_), channel_id=1, source_target_pairs={{0,2},{1,5},{2,0},{3,7},{4,6},{5,1},{6,4},{7,3},{8,10},{9,13},{10,... | collective-permute-start | bytes 1081352 | tf_op jit(solution)/shard_map/ppermute | solution.py:496
  40.4 8.8 %collective-permute-start.11 = (bf16[1408,128]{1,0:T(8,128)(2,1)S(1)}, bf16[1408,128]{1,0:T(8,128)(2,1)S(1)}, u32[]{:S(2)}, u32[]{:S(2)}) collective-permute-start(bf16[1408,128]{1,0:T(8,128)(2,1)S(1)} %collective-permute-done.6.refs_7_), channel_id=1, source_target_pairs={{1,0},{0,1},{3,2},{2,3},{5,4},{4,5},{7,6},{6,7},{9,8},{8,9},{11,10... | collective-permute-start | bytes 1081352 | tf_op jit(solution)/shard_map/ppermute | solution.py:485
  45.8 3.4 %collective-permute-start.14 = (bf16[1408,128]{1,0:T(8,128)(2,1)S(1)}, bf16[1408,128]{1,0:T(8,128)(2,1)S(1)}, u32[]{:S(2)}, u32[]{:S(2)}) collective-permute-start(bf16[1408,128]{1,0:T(8,128)(2,1)S(1)} %collective-permute-done.13.refs_11_), channel_id=1, source_target_pairs={{1,0},{0,1},{3,2},{2,3},{5,4},{4,5},{7,6},{6,7},{9,8},{8,9},{11,10... | collective-permute-start | bytes 1081352 | tf_op jit(solution)/shard_map/ppermute | solution.py:485
  45.8 15.7 %collective-permute-start.16 = (bf16[768,384]{1,0:T(8,128)(2,1)S(1)}, bf16[768,384]{1,0:T(8,128)(2,1)S(1)}, u32[]{:S(2)}, u32[]{:S(2)}) collective-permute-start(bf16[768,384]{1,0:T(8,128)(2,1)S(1)} %dynamic-slice_bitcast_fusion), channel_id=1, source_target_pairs={{0,8},{2,10},{4,12},{6,14},{8,0},{10,2},{12,4},{14,6},{16,24},{18,... | collective-permute-start | bytes 1769480 | tf_op jit(solution)/shard_map/ppermute | solution.py:502
  61.5 2.0 %collective-permute-start.17 = (bf16[768,384]{1,0:T(8,128)(2,1)S(1)}, bf16[768,384]{1,0:T(8,128)(2,1)S(1)}, u32[]{:S(2)}, u32[]{:S(2)}) collective-permute-start(bf16[768,384]{1,0:T(8,128)(2,1)S(1)} %collective-permute-done.16.refs_1_.refs_2_.refs_5_), channel_id=1, source_target_pairs={{1,0},{0,1},{3,2},{2,3},{5,4},{4,5},{7,6},{6,7},{9,8},{8,9},{11,10... | collective-permute-start | bytes 1769480 | tf_op jit(solution)/shard_map/ppermute | solution.py:485
  61.5 14.0 %collective-permute-start.18 = (bf16[1408,128]{1,0:T(8,128)(2,1)S(1)}, bf16[1408,128]{1,0:T(8,128)(2,1)S(1)}, u32[]{:S(2)}, u32[]{:S(2)}) collective-permute-start(bf16[1408,128]{1,0:T(8,128)(2,1)S(1)} %get-tuple-element.56.refs_3_), channel_id=1, source_target_pairs={{0,8},{2,10},{4,12},{6,14},{8,0},{10,2},{12,4},{14,6},{16,24},{18,... | collective-permute-start | bytes 1081352 | tf_op jit(solution)/shard_map/ppermute | solution.py:502
  64.4 11.1 %collective-permute-start.19 = (bf16[192,384]{1,0:T(8,128)(2,1)S(1)}, bf16[192,384]{1,0:T(8,128)(2,1)S(1)}, u32[]{:S(2)}, u32[]{:S(2)}) collective-permute-start(bf16[192,384]{1,0:T(8,128)(2,1)S(1)} %shard_map.55), channel_id=1, source_target_pairs={{16,0},{18,2},{20,4},{22,6},{24,8},{26,10},{28,12},{30,14},{17,1},... | collective-permute-start | bytes 442376 | tf_op jit(solution)/shard_map/ppermute | solution.py:502
  65.7 9.8 %collective-permute-start.15 = (bf16[1408,128]{1,0:T(8,128)(2,1)S(1)}, bf16[1408,128]{1,0:T(8,128)(2,1)S(1)}, u32[]{:S(2)}, u32[]{:S(2)}) collective-permute-start(bf16[1408,128]{1,0:T(8,128)(2,1)S(1)} %get-tuple-element.56.refs_3_), channel_id=1, source_target_pairs={{1,0},{0,1},{3,2},{2,3},{5,4},{4,5},{7,6},{6,7},{9,8},{8,9},{11,10... | collective-permute-start | bytes 1081352 | tf_op jit(solution)/shard_map/ppermute | solution.py:485
  75.5 1.7 %collective-permute-start.20 = (bf16[1408,128]{1,0:T(8,128)(2,1)S(1)}, bf16[1408,128]{1,0:T(8,128)(2,1)S(1)}, u32[]{:S(2)}, u32[]{:S(2)}) collective-permute-start(bf16[1408,128]{1,0:T(8,128)(2,1)S(1)} %collective-permute-done.18.refs_7_), channel_id=1, source_target_pairs={{1,0},{0,1},{3,2},{2,3},{5,4},{4,5},{7,6},{6,7},{9,8},{8,9},{11,10... | collective-permute-start | bytes 1081352 | tf_op jit(solution)/shard_map/ppermute | solution.py:485
  78.9 7.5 %collective-permute-start.21 = (bf16[352,128]{1,0:T(8,128)(2,1)S(1)}, bf16[352,128]{1,0:T(8,128)(2,1)S(1)}, u32[]{:S(2)}, u32[]{:S(2)}) collective-permute-start(bf16[352,128]{1,0:T(8,128)(2,1)S(1)} %get-tuple-element.64), channel_id=1, source_target_pairs={{16,0},{18,2},{20,4},{22,6},{24,8},{26,10},{28,12},{30,14},{17,1},... | collective-permute-start | bytes 270344 | tf_op jit(solution)/shard_map/ppermute | solution.py:502
  80.6 7.9 %collective-permute-start.27 = (bf16[192,384]{1,0:T(8,128)(2,1)S(1)}, bf16[192,384]{1,0:T(8,128)(2,1)S(1)}, u32[]{:S(2)}, u32[]{:S(2)}) collective-permute-start(bf16[192,384]{1,0:T(8,128)(2,1)S(1)} %collective-permute-done.19.refs_0_), channel_id=1, source_target_pairs={{0,6},{1,7},{2,4},{3,5},{4,2},{5,3},{6,0},{7,1},{8,14},{9,15},{10,... | collective-permute-start | bytes 442376 | tf_op jit(solution)/shard_map/ppermute | solution.py:496
  83.9 7.3 %collective-permute-start.26 = (bf16[192,384]{1,0:T(8,128)(2,1)S(1)}, bf16[192,384]{1,0:T(8,128)(2,1)S(1)}, u32[]{:S(2)}, u32[]{:S(2)}) collective-permute-start(bf16[192,384]{1,0:T(8,128)(2,1)S(1)} %collective-permute-done.19.refs_0_), channel_id=1, source_target_pairs={{0,4},{1,5},{2,6},{3,7},{4,0},{5,1},{6,2},{7,3},{8,12},{9,13},{10,... | collective-permute-start | bytes 442376 | tf_op jit(solution)/shard_map/ppermute | solution.py:496
  85.6 6.6 %collective-permute-start.25 = (bf16[192,384]{1,0:T(8,128)(2,1)S(1)}, bf16[192,384]{1,0:T(8,128)(2,1)S(1)}, u32[]{:S(2)}, u32[]{:S(2)}) collective-permute-start(bf16[192,384]{1,0:T(8,128)(2,1)S(1)} %collective-permute-done.19.refs_0_), channel_id=1, source_target_pairs={{0,2},{1,3},{2,0},{3,1},{4,6},{5,7},{6,4},{7,5},{8,10},{9,11},{10,... | collective-permute-start | bytes 442376 | tf_op jit(solution)/shard_map/ppermute | solution.py:496
  92.3 8.0 %collective-permute-start.28 = (bf16[768,384]{1,0:T(8,128)(2,1)S(1)}, bf16[768,384]{1,0:T(8,128)(2,1)S(1)}, u32[]{:S(2)}, u32[]{:S(2)}) collective-permute-start(bf16[768,384]{1,0:T(8,128)(2,1)S(1)} %shard_map.60.refs_1_), channel_id=1, source_target_pairs={{1,0},{0,1},{3,2},{2,3},{5,4},{4,5},{7,6},{6,7},{9,8},{8,9},{11,10... | collective-permute-start | bytes 1769480 | tf_op jit(solution)/shard_map/ppermute | solution.py:485
  92.4 6.0 %collective-permute-start.24 = (bf16[352,128]{1,0:T(8,128)(2,1)S(1)}, bf16[352,128]{1,0:T(8,128)(2,1)S(1)}, u32[]{:S(2)}, u32[]{:S(2)}) collective-permute-start(bf16[352,128]{1,0:T(8,128)(2,1)S(1)} %collective-permute-done.21.refs_0_), channel_id=1, source_target_pairs={{0,6},{1,7},{2,4},{3,5},{4,2},{5,3},{6,0},{7,1},{8,14},{9,15},{10,... | collective-permute-start | bytes 270344 | tf_op jit(solution)/shard_map/ppermute | solution.py:496
  94.3 5.9 %collective-permute-start.23 = (bf16[352,128]{1,0:T(8,128)(2,1)S(1)}, bf16[352,128]{1,0:T(8,128)(2,1)S(1)}, u32[]{:S(2)}, u32[]{:S(2)}) collective-permute-start(bf16[352,128]{1,0:T(8,128)(2,1)S(1)} %collective-permute-done.21.refs_0_), channel_id=1, source_target_pairs={{0,4},{1,5},{2,6},{3,7},{4,0},{5,1},{6,2},{7,3},{8,12},{9,13},{10,... | collective-permute-start | bytes 270344 | tf_op jit(solution)/shard_map/ppermute | solution.py:496
  95.6 4.6 %collective-permute-start.22 = (bf16[352,128]{1,0:T(8,128)(2,1)S(1)}, bf16[352,128]{1,0:T(8,128)(2,1)S(1)}, u32[]{:S(2)}, u32[]{:S(2)}) collective-permute-start(bf16[352,128]{1,0:T(8,128)(2,1)S(1)} %collective-permute-done.21.refs_0_), channel_id=1, source_target_pairs={{0,2},{1,3},{2,0},{3,1},{4,6},{5,7},{6,4},{7,5},{8,10},{9,11},{10,... | collective-permute-start | bytes 270344 | tf_op jit(solution)/shard_map/ppermute | solution.py:496
  102.0 1.7 %collective-permute-start.29 = (bf16[1408,128]{1,0:T(8,128)(2,1)S(1)}, bf16[1408,128]{1,0:T(8,128)(2,1)S(1)}, u32[]{:S(2)}, u32[]{:S(2)}) collective-permute-start(bf16[1408,128]{1,0:T(8,128)(2,1)S(1)} %shard_map.59.refs_3_), channel_id=1, source_target_pairs={{1,0},{0,1},{3,2},{2,3},{5,4},{4,5},{7,6},{6,7},{9,8},{8,9},{11,10... | collective-permute-start | bytes 1081352 | tf_op jit(solution)/shard_map/ppermute | solution.py:485
